TPU v7x, 32 devices: a whole 2x2x4 slice. The times are simulated.
32 devices in a mesh: cb: 4 (over x, core), frame: 8 (over z, y).
Axes of the slice: x: 2, y: 2, z: 4, core: 2. Of those that a mesh axis runs over, the one named last changes fastest.
Arguments:
- inputs: bfloat16 [2048, 16, 1024], P('frame', 'cb'), may hold values from -64 to 64
- norm_gain: float32 [1024], replicated, may hold values from 0.1 to 1.9
- w_qkv: bfloat16 [16, 1024, 3072], P('cb', 'frame'), may hold values from -4 to 4
- w_out: bfloat16 [16, 1024, 1024], P('cb', 'frame'), may hold values from -0.1875 to 0.1875
- grad_out: bfloat16 [2048, 16, 1024], P('frame', 'cb'), may hold values from -6 to 6
Outputs:
- outputs: bfloat16 [2048, 16, 1024], P('frame', 'cb')
- grad_in: bfloat16 [2048, 16, 1024], P('frame', 'cb')
All inputs are finite; a program needn't handle non-finite values.
Results may differ from a plain program's by a relative error of at most 0.0053.
Values may be sent and summed in bfloat16 or wider, within the bound.
No kernel may reach another device: no remote copies, remote signals or barrier semaphores. Data moves between devices by JAX's collectives and lax.ppermute only.
A program may use at most 128 MiB of HBM per device.

v0:
```python
import jax
import jax.numpy as jnp
from jax import lax
from jax.sharding import PartitionSpec as P

HEADS = 16


epsilon = 1e-05


def to_heads(values, head_count):
    frames, depth, columns = values.shape
    return values.reshape(frames, depth, head_count, columns // head_count)


def attention_probs(queries, key_rows, head_count):
    depth = queries.shape[1]
    factor = (queries.shape[2] // head_count) ** (-0.5)
    scores = (
        jnp.einsum(
            "fihe,fjhe->fhij",
            to_heads(queries, head_count),
            to_heads(key_rows, head_count),
            preferred_element_type=jnp.float32,
        )
        * factor
    )
    causal = lax.broadcasted_iota(jnp.int32, (depth, depth), 0) >= lax.broadcasted_iota(
        jnp.int32, (depth, depth), 1
    )
    scores = jnp.where(causal, scores, -jnp.inf)
    weights = jnp.exp(scores - jnp.max(scores, axis=-1, keepdims=True))
    return weights / jnp.sum(weights, axis=-1, keepdims=True)


def attend_all(queries, key_rows, values, head_count):
    probs_low = attention_probs(queries, key_rows, head_count).astype(jnp.bfloat16)
    mixed = jnp.einsum(
        "fhij,fjhe->fihe",
        probs_low,
        to_heads(values, head_count),
        preferred_element_type=jnp.float32,
    )
    return mixed.reshape(values.shape).astype(jnp.bfloat16)


def attention_grads(queries, key_rows, values, grad_context, head_count):
    shape_full = queries.shape
    factor = (queries.shape[2] // head_count) ** (-0.5)
    probs = attention_probs(queries, key_rows, head_count)
    probs_low = probs.astype(jnp.bfloat16)
    grad_heads = to_heads(grad_context, head_count)
    grad_values = jnp.einsum(
        "fhij,fihe->fjhe", probs_low, grad_heads, preferred_element_type=jnp.float32
    )
    grad_probs = jnp.einsum(
        "fihe,fjhe->fhij",
        grad_heads,
        to_heads(values, head_count),
        preferred_element_type=jnp.float32,
    )
    inner = jnp.sum(probs * grad_probs, axis=-1, keepdims=True)
    grad_scores = (probs * (grad_probs - inner) * factor).astype(jnp.bfloat16)
    grad_queries = jnp.einsum(
        "fhij,fjhe->fihe",
        grad_scores,
        to_heads(key_rows, head_count),
        preferred_element_type=jnp.float32,
    )
    grad_keys = jnp.einsum(
        "fhij,fihe->fjhe",
        grad_scores,
        to_heads(queries, head_count),
        preferred_element_type=jnp.float32,
    )
    return (
        grad_queries.reshape(shape_full).astype(jnp.bfloat16),
        grad_keys.reshape(shape_full).astype(jnp.bfloat16),
        grad_values.reshape(shape_full).astype(jnp.bfloat16),
    )


def body(inputs, norm_gain, w_qkv, w_out, grad_out):
    frames, local_cb, columns = inputs.shape
    wide_in = inputs.astype(jnp.float32)
    inverse_rms = lax.rsqrt(jnp.mean(wide_in * wide_in, axis=-1, keepdims=True) + epsilon)
    normed = (wide_in * inverse_rms * norm_gain).astype(jnp.bfloat16)
    full_qkv, full_out = (
        lax.all_gather(w_qkv, "frame", axis=1, tiled=True),
        lax.all_gather(w_out, "frame", axis=1, tiled=True),
    )
    projected = jnp.einsum(
        "fcd,cde->fce", normed, full_qkv, preferred_element_type=jnp.float32
    ).astype(jnp.bfloat16)
    queries = projected[:, :, :columns]
    key_rows = projected[:, :, columns : 2 * columns]
    values = projected[:, :, 2 * columns :]
    grad_context = jnp.einsum(
        "fce,cde->fcd", grad_out, full_out, preferred_element_type=jnp.float32
    ).astype(jnp.bfloat16)
    pair_shape = (frames, local_cb, HEADS // 2, 2 * (columns // HEADS))
    part_q = lax.all_to_all(
        queries.reshape(pair_shape), "cb", split_axis=0, concat_axis=1, tiled=True
    )
    part_k = lax.all_to_all(
        key_rows.reshape(pair_shape), "cb", split_axis=0, concat_axis=1, tiled=True
    )
    part_v = lax.all_to_all(
        values.reshape(pair_shape), "cb", split_axis=0, concat_axis=1, tiled=True
    )
    flat_shape = (part_q.shape[0], part_q.shape[1], part_q.shape[2] * part_q.shape[3])
    mixed = attend_all(
        part_q.reshape(flat_shape),
        part_k.reshape(flat_shape),
        part_v.reshape(flat_shape),
        2 * part_q.shape[2],
    )
    returned = lax.all_to_all(
        mixed.reshape(part_q.shape), "cb", split_axis=1, concat_axis=0, tiled=True
    )
    returned, own_q, own_k, own_v = (returned, part_q, part_k, part_v)
    context = returned.reshape(frames, local_cb, columns)
    owner_shape = (own_q.shape[0], own_q.shape[1], columns)
    own_q = own_q.reshape(owner_shape)
    own_k = own_k.reshape(owner_shape)
    own_v = own_v.reshape(owner_shape)
    own_grad = lax.all_to_all(grad_context, "cb", split_axis=0, concat_axis=1, tiled=True)
    grad_q, grad_k, grad_v = attention_grads(own_q, own_k, own_v, own_grad, HEADS)
    back_q, back_k, back_v = (
        lax.all_to_all(grad_q, "cb", split_axis=1, concat_axis=0, tiled=True),
        lax.all_to_all(grad_k, "cb", split_axis=1, concat_axis=0, tiled=True),
        lax.all_to_all(grad_v, "cb", split_axis=1, concat_axis=0, tiled=True),
    )
    outputs = (
        wide_in + jnp.einsum("fcd,cde->fce", context, full_out, preferred_element_type=jnp.float32)
    ).astype(jnp.bfloat16)
    grad_qkv = jnp.concatenate([back_q, back_k, back_v], axis=-1)
    scaled = (
        jnp.einsum("fce,cde->fcd", grad_qkv, full_qkv, preferred_element_type=jnp.float32)
        * norm_gain
    )
    inner = jnp.mean(scaled * wide_in, axis=-1, keepdims=True)
    grad_in = grad_out.astype(jnp.float32) + inverse_rms * (
        scaled - wide_in * inverse_rms * inverse_rms * inner
    )
    return (outputs, grad_in.astype(jnp.bfloat16))


def solution(mesh):
    return jax.shard_map(
        body,
        mesh=mesh,
        in_specs=(
            P("frame", "cb", None),
            P(),
            P("cb", "frame", None),
            P("cb", "frame", None),
            P("frame", "cb", None),
        ),
        out_specs=(P("frame", "cb", None), P("frame", "cb", None)),
        check_vma=False,
    )
```

profile of v0, /device:TPU:0, one launch (start us, length us, event | category | flops | bytes accessed | tf_op | source)
XLA Modules:
  0.0 866.0 jit_solution(13620348402024444469)
XLA Ops:
  9.9 482.8 %all-gather.3.cloned.1.call-done = bf16[4,1024,3072]{2,1,0:T(8,128)(2,1)} async-done(((bf16[4,128,3072]{2,1,0:T(8,128)(2,1)}), bf16[4,1024,3072]{2,1,0:T(8,128)(2,1)}) %all-gather.3.cloned.1.call-update) | async-done | bytes 25165840 | tf_op jit(solution)/shard_map/all_gather | solution.py:90
  492.7 15.9 %convert_bitcast_fusion = bf16[256,4,3072]{2,0,1:T(8,128)(2,1)S(1)} fusion(bf16[4,1024,3072]{2,1,0:T(8,128)(2,1)} %all-gather.3.cloned.1.call-done, f32[1024]{0:T(1024)S(1)} %copy-done.5, f32[256,4]{0,1:T(4,128)S(1)} %add_rsqrt_fusion, bf16[256,4,1024]{2,1,0:T(4,128)(2,1)S(1)} %copy-done.1), kind=kOutput, calls=%fused_computation.18 | convolution fusion | flops 6449790976 | bytes 33562624 | tf_op jit(solution)/shard_map/fcd,cde->fce/dot_general | solution.py:93
  521.4 21.7 %all-to-all-done.2 = bf16[256,4,8,128]{3,2,1,0:T(8,128)(2,1)S(1)} async-done(((bf16[256,4,8,128]{3,2,1,0:T(8,128)(2,1)}), bf16[256,4,8,128]{3,2,1,0:T(8,128)(2,1)S(1)}, u32[]{:S(2)}, u32[]{:S(2)}) %all-to-all-start.2) | async-done | bytes 2097184 | tf_op jit(solution)/shard_map/all_to_all | solution.py:106
  551.6 21.7 %all-to-all-done.1 = bf16[256,4,8,128]{3,2,1,0:T(8,128)(2,1)} async-done(((bf16[256,4,8,128]{3,2,1,0:T(8,128)(2,1)}), bf16[256,4,8,128]{3,2,1,0:T(8,128)(2,1)}, u32[]{:S(2)}, u32[]{:S(2)}) %all-to-all-start.1) | async-done | bytes 2097184 | tf_op jit(solution)/shard_map/all_to_all | solution.py:103
  573.3 4.7 all-to-all-start
  578.1 41.8 %all-gather.5.cloned.1.call-done = bf16[4,1024,1024]{2,1,0:T(8,128)(2,1)} async-done(((bf16[4,128,1024]{2,1,0:T(8,128)(2,1)}), bf16[4,1024,1024]{2,1,0:T(8,128)(2,1)}) %all-gather.5.cloned.1.call-update) | async-done | bytes 8388624 | tf_op jit(solution)/shard_map/all_gather | solution.py:91
  619.8 6.4 convert_bitcast_fusion.5
  640.4 9.0 %fusion.35 = f32[64,16,16,16]{2,3,1,0:T(8,128)} fusion(bf16[64,16,16,64]{3,2,1,0:T(8,128)(2,1)} %reshape_reshape.16, bf16[64,16,16,64]{3,2,1,0:T(8,128)(2,1)} %reshape_reshape.7), kind=kOutput, calls=%fused_computation.47 | convolution fusion | flops 33554432 | bytes 5242880 | tf_op jit(solution)/shard_map/fihe,fjhe->fhij/dot_general | solution.py:21
  649.4 5.0 all-to-all-start.4
  654.4 12.5 %fusion.67 = (f32[64,16,16]{2,1,0:T(8,128)S(1)}, f32[64,16,16,16]{2,3,1,0:T(8,128)}) fusion(f32[64,16,16,16]{2,3,1,0:T(8,128)} %fusion.35, pred[16,16]{0,1:T(8,128)(4,1)S(1)} %iota_compare_fusion), kind=kOutput, calls=%fused_computation.70 | output fusion | flops 1572879 | bytes 2162944 | tf_op jit(solution)/shard_map/sub | solution.py:33
  672.4 5.8 convert_bitcast_fusion.4
  681.2 6.2 reshape.55
  698.4 7.8 convert_bitcast_fusion.1
  709.2 6.5 reshape.58
  721.6 10.0 %fusion.28 = f32[64,16,16,16]{2,3,1,0:T(8,128)} fusion(bf16[64,16,16,64]{3,2,0,1:T(8,128)(2,1)} %reshape.54, bf16[64,16,16,64]{3,2,1,0:T(8,128)(2,1)} %reshape_reshape.6), kind=kOutput, calls=%fused_computation.40 | convolution fusion | flops 33554432 | bytes 5242880 | tf_op jit(solution)/shard_map/fihe,fjhe->fhij/dot_general | solution.py:57
  731.6 16.3 %convert_bitcast_fusion.2 = bf16[64,16,16,64]{3,1,2,0:T(8,128)(2,1)} fusion(bf16[64,16,16,64]{3,2,1,0:T(8,128)(2,1)} %reshape_reshape.7, f32[64,16,16,16]{2,3,1,0:T(8,128)} %fusion.28, f32[64,16,16,16]{2,3,1,0:T(8,128)} %get-tuple-element.14, f32[64,16,16]{2,1,0:T(8,128)S(1)} %get-tuple-element.13), kind=kOutput, calls=%fused_computation.31 | convolution fusion | flops 36454416 | bytes 6356992 | tf_op jit(solution)/shard_map/fhij,fihe->fjhe/dot_general | solution.py:71
  747.9 5.2 copy.118
  753.2 6.5 reshape.57
  764.1 17.7 %convert_bitcast_fusion.3 = bf16[64,16,16,64]{3,1,2,0:T(8,128)(2,1)} fusion(bf16[64,16,16,64]{3,2,1,0:T(8,128)(2,1)} %reshape_reshape.16, f32[64,16,16,16]{2,3,1,0:T(8,128)} %fusion.28, f32[64,16,16,16]{2,3,1,0:T(8,128)} %get-tuple-element.14, f32[64,16,16]{2,1,0:T(8,128)S(1)} %get-tuple-element.13), kind=kOutput, calls=%fused_computation.32 | convolution fusion | flops 36454416 | bytes 6356992 | tf_op jit(solution)/shard_map/fhij,fjhe->fihe/dot_general | solution.py:65
  781.8 5.3 copy.117
  787.2 6.5 reshape.56
  793.6 4.7 all-to-all-start.5
  805.6 7.9 fusion.21
  827.2 24.8 %fusion.22 = (f32[256,4]{0,1:T(4,128)S(1)}, f32[4,256,1024]{2,1,0:T(8,128)}) fusion(f32[1024]{0:T(1024)S(1)} %copy-done.5, bf16[256,4,1024]{2,1,0:T(4,128)(2,1)S(1)} %copy-done.2, bf16[4,1024,3072]{2,1,0:T(8,128)(2,1)} %all-gather.3.cloned.1.call-done, bf16[256,4,1024]{2,0,1:T(8,128)(2,1)} %bitcast.106, bf16[256,4,1024]{2,0,1:T(8,128)(2,1)} %bitcast.107, ...), kind=kOutput, calls=%fused_computation.29 | convolution fusion | flops 6465518592 | bytes 37756928 | tf_op jit(solution)/shard_map/fce,cde->fcd/dot_general | solution.py:140
  (58 shorter events, 98.7 us)
Async XLA Ops:
  7.2 1.6 copy-start.1
  7.2 485.6 %copy-start.5 = (f32[1024]{0:T(1024)S(1)}, f32[1024]{0:T(1024)}, u32[]{:S(2)}) copy-start(f32[1024]{0:T(1024)} %param.6) | copy-start | bytes 12292
  7.2 485.5 %all-gather.3.cloned.1.call-start = ((), (), s32[]{:S(2)}) async-start(), calls=%async_computation.8 | async-start | bytes 28311552 | tf_op jit(solution)/shard_map/all_gather | solution.py:90
  7.9 611.9 %all-gather.5.cloned.1.call-start = ((), (), s32[]{:S(2)}) async-start(), calls=%async_computation.9 | async-start | bytes 9437184 | tf_op jit(solution)/shard_map/all_gather | solution.py:91
  9.9 498.7 %copy-start.3 = (f32[256,4]{0,1:T(4,128)}, f32[256,4]{0,1:T(4,128)S(1)}, u32[]{:S(2)}) copy-start(f32[256,4]{0,1:T(4,128)S(1)} %add_rsqrt_fusion) | copy-start | bytes 12292
  513.8 29.3 %all-to-all-start.2 = ((bf16[256,4,8,128]{3,2,1,0:T(8,128)(2,1)}), bf16[256,4,8,128]{3,2,1,0:T(8,128)(2,1)S(1)}, u32[]{:S(2)}, u32[]{:S(2)}) async-start(bf16[256,4,8,128]{3,2,1,0:T(8,128)(2,1)} %copy.81), calls=%async_computation.2 | async-start | bytes 4194304 | tf_op jit(solution)/shard_map/all_to_all | solution.py:106
  543.1 6.8 copy-start
  543.1 30.2 %all-to-all-start.1 = ((bf16[256,4,8,128]{3,2,1,0:T(8,128)(2,1)}), bf16[256,4,8,128]{3,2,1,0:T(8,128)(2,1)}, u32[]{:S(2)}, u32[]{:S(2)}) async-start(bf16[256,4,8,128]{3,2,1,0:T(8,128)(2,1)} %copy.79), calls=%async_computation.1 | async-start | bytes 4194304 | tf_op jit(solution)/shard_map/all_to_all | solution.py:103
  573.3 76.1 %all-to-all-start = ((bf16[256,4,8,128]{3,2,1,0:T(8,128)(2,1)}), bf16[256,4,8,128]{3,2,1,0:T(8,128)(2,1)}, u32[]{:S(2)}, u32[]{:S(2)}) async-start(bf16[256,4,8,128]{3,2,1,0:T(8,128)(2,1)} %copy.77), calls=%async_computation | async-start | bytes 4194304 | tf_op jit(solution)/shard_map/all_to_all | solution.py:109
  649.4 38.0 %all-to-all-start.4 = ((bf16[256,4,1024]{2,1,0:T(4,128)(2,1)}), bf16[256,4,1024]{2,1,0:T(4,128)(2,1)}, u32[]{:S(2)}, u32[]{:S(2)}) async-start(bf16[256,4,1024]{2,1,0:T(4,128)(2,1)} %copy.93), calls=%async_computation.4 | async-start | bytes 4194304 | tf_op jit(solution)/shard_map/all_to_all | solution.py:128
  687.4 30.4 %all-to-all-start.3 = ((bf16[64,16,8,128]{3,2,0,1:T(8,128)(2,1)}), bf16[64,16,8,128]{3,2,0,1:T(8,128)(2,1)}, u32[]{:S(2)}, u32[]{:S(2)}) async-start(bf16[64,16,8,128]{3,2,0,1:T(8,128)(2,1)} %reshape.55), calls=%async_computation.3 | async-start | bytes 4194304 | tf_op jit(solution)/shard_map/all_to_all | solution.py:119
  717.8 41.9 %all-to-all-start.7 = ((bf16[64,16,1024]{2,0,1:T(8,128)(2,1)}), bf16[64,16,1024]{2,0,1:T(8,128)(2,1)S(1)}, u32[]{:S(2)}, u32[]{:S(2)}) async-start(bf16[64,16,1024]{2,0,1:T(8,128)(2,1)} %reshape.58), calls=%async_computation.7 | async-start | bytes 4194304 | tf_op jit(solution)/shard_map/all_to_all | solution.py:133
  759.7 34.0 %all-to-all-start.6 = ((bf16[64,16,1024]{2,0,1:T(8,128)(2,1)}), bf16[64,16,1024]{2,0,1:T(8,128)(2,1)}, u32[]{:S(2)}, u32[]{:S(2)}) async-start(bf16[64,16,1024]{2,0,1:T(8,128)(2,1)} %reshape.57), calls=%async_computation.6 | async-start | bytes 4194304 | tf_op jit(solution)/shard_map/all_to_all | solution.py:132
  793.6 30.5 %all-to-all-start.5 = ((bf16[64,16,1024]{2,0,1:T(8,128)(2,1)}), bf16[64,16,1024]{2,0,1:T(8,128)(2,1)}, u32[]{:S(2)}, u32[]{:S(2)}) async-start(bf16[64,16,1024]{2,0,1:T(8,128)(2,1)} %reshape.56), calls=%async_computation.5 | async-start | bytes 4194304 | tf_op jit(solution)/shard_map/all_to_all | solution.py:131
  818.1 9.2 %copy-start.2 = (bf16[256,4,1024]{2,1,0:T(4,128)(2,1)S(1)}, bf16[256,4,1024]{2,1,0:T(4,128)(2,1)}, u32[]{:S(2)}) copy-start(bf16[256,4,1024]{2,1,0:T(4,128)(2,1)} %param.5) | copy-start | bytes 6291460
  827.2 24.8 %copy-start.4 = (f32[256,4]{0,1:T(4,128)S(1)}, f32[256,4]{0,1:T(4,128)}, u32[]{:S(2)}) copy-start(f32[256,4]{0,1:T(4,128)} %copy-done.3) | copy-start | bytes 12292
Sparse Core Ops, SparseCore 0:
  9.6 483.1 all-gather.2
  494.9 124.8 all-gather.4
where the time goes:
time: 874 us; the launch traced here: 866 us
  waiting for transfers between devices  574 us (66%)
  matrix products  121 us (14%)
  local copies, waits for them, and re-layouts  103 us (12%)
  starting transfers between devices  35.4 us (4%)
  other arithmetic  17.5 us (2%)
  between operations  14.7 us (2%)
    all_gather x1, waiting for transfers between devices, body(): lax.all_gather(w_qkv, 'frame', axis=1, tiled=True)  483 us
    all_gather x1, waiting for transfers between devices, body(): lax.all_gather(w_out, 'frame', axis=1, tiled=True)  41.8 us
    dot_general x1, matrix products, body(): jnp.einsum('fce,cde->fcd', grad_qkv, full_qkv, preferred_element_type=jnp...  24.8 us
    all_to_all x1, waiting for transfers between devices, body(): lax.all_to_all(key_rows.reshape(pair_shape), 'cb', split_axis=0, concat_a...  21.7 us
    all_to_all x1, waiting for transfers between devices, body(): lax.all_to_all(queries.reshape(pair_shape), 'cb', split_axis=0, concat_ax...  21.7 us
    dot_general x1, matrix products, attention_grads(): jnp.einsum('fhij,fjhe->fihe', grad_scores, to_heads(key_rows, head_count)...  17.7 us
  transfers between devices with their start and end apart: 10, of which 6 were waited for; matrix products, arithmetic and copies ran while one was open for 24% of the time, Pallas kernels for 0%

commit v1 on v0

v1 whole, which is shorter than its diff:
```python
import functools

import jax
import jax.numpy as jnp
from jax import lax
from jax.experimental import pallas as pl
from jax.experimental.pallas import tpu as pltpu
from jax.sharding import PartitionSpec as P

HEADS = 16
GROUPS = 4
EPSILON = 1e-05
F32 = jnp.float32
BF16 = jnp.bfloat16
FRAME_BLOCK = 16
HALF = 8


def params(mib):
    return pltpu.CompilerParams(
        dimension_semantics=("arbitrary",), vmem_limit_bytes=mib * 1024 * 1024
    )


def cost(flops, byte_count):
    return pl.CostEstimate(flops=flops, bytes_accessed=byte_count, transcendentals=0)


def fill(source_ref, slot_refs, whole_ref):
    depth = slot_refs[0].shape[1]
    for slot, ref in enumerate(slot_refs):
        start = pl.multiple_of(source_ref[slot] * depth, depth)
        whole_ref[pl.ds(start, depth), :] = ref[0]


def project_kernel(back, source_ref, rows_ref, *refs):
    slot_refs, out_ref, whole_ref = refs[:-2], refs[-2], refs[-1]
    fill(source_ref, slot_refs, whole_ref)
    contract = ((1,), (1,)) if back else ((1,), (0,))
    result = lax.dot_general(
        rows_ref[0], whole_ref[...], (contract, ((), ())), preferred_element_type=F32
    )
    out_ref[...] = result.astype(BF16).reshape(out_ref.shape)


def project(source, rows, slots, parts, back):
    codebooks, frames, columns = rows.shape
    depth, width = slots[0].shape[1:]
    wide = depth * len(slots)
    out_columns = wide if back else width
    share = frames // parts
    return pl.pallas_call(
        functools.partial(project_kernel, back),
        grid=(codebooks,),
        in_specs=[
            pl.BlockSpec(memory_space=pltpu.SMEM),
            pl.BlockSpec((1, frames, columns), lambda c: (c, 0, 0)),
        ]
        + [pl.BlockSpec((1, depth, width), lambda c: (c, 0, 0)) for _ in slots],
        out_specs=pl.BlockSpec((parts, 1, share, out_columns), lambda c: (0, c, 0, 0)),
        out_shape=jax.ShapeDtypeStruct((parts, codebooks, share, out_columns), BF16),
        scratch_shapes=[pltpu.VMEM((wide, width), BF16)],
        compiler_params=params(32),
        cost_estimate=cost(
            2 * codebooks * frames * wide * width, 2 * codebooks * wide * (width + 1024)
        ),
        name="project_back" if back else "project",
    )(source, rows, *slots)


def attend_kernel(heads, qkv_ref, grad_ref, out_ref):
    codebooks, _, width = grad_ref.shape
    head_width = width // heads
    rows = codebooks * HALF
    factor = head_width ** (-0.5)
    row = lax.broadcasted_iota(jnp.int32, (rows, rows), 0)
    column = lax.broadcasted_iota(jnp.int32, (rows, rows), 1)
    allowed = jnp.logical_and(row % HALF == column % HALF, row >= column)[None]
    lane_head = lax.broadcasted_iota(jnp.int32, (rows, width), 1) // head_width

    def wide(ref, first):
        values = ref[:, :, first : first + width].astype(F32)
        return values.reshape(codebooks, FRAME_BLOCK // HALF, HALF, width)

    def stacked(values):
        pieces = [jnp.where(lane_head == h, values, 0.0).astype(BF16) for h in range(heads)]
        return jnp.concatenate(pieces, axis=0)

    def beside(values):
        return jnp.concatenate([values[h * rows : (h + 1) * rows] for h in range(heads)], axis=1)

    def dot(left, right, left_dim, right_dim):
        return lax.dot_general(
            left, right, (((left_dim,), (right_dim,)), ((), ())), preferred_element_type=F32
        )

    parts = [wide(qkv_ref, 0), wide(qkv_ref, width), wide(qkv_ref, 2 * width), wide(grad_ref, 0)]
    results = [[], [], [], []]
    for half in range(FRAME_BLOCK // HALF):
        q, k, v, g = [part[:, half].reshape(rows, width) for part in parts]
        q_heads, k_heads, v_heads, g_heads = stacked(q), stacked(k), stacked(v), stacked(g)
        scores = dot(q_heads, k.astype(BF16), 1, 1).reshape(heads, rows, rows) * factor
        scores = jnp.where(allowed, scores, -jnp.inf)
        weights = jnp.exp(scores - jnp.max(scores, axis=-1, keepdims=True))
        probs = weights / jnp.sum(weights, axis=-1, keepdims=True)
        grad_probs = dot(g_heads, v.astype(BF16), 1, 1).reshape(heads, rows, rows)
        inner = jnp.sum(probs * grad_probs, axis=-1, keepdims=True)
        grad_scores = (probs * (grad_probs - inner) * factor).astype(BF16)
        probs_low = probs.astype(BF16).reshape(heads * rows, rows)
        grad_scores = grad_scores.reshape(heads * rows, rows)
        results[0].append(dot(beside(probs_low), v_heads, 1, 0))
        results[1].append(dot(beside(grad_scores), k_heads, 1, 0))
        results[2].append(dot(grad_scores, q_heads, 0, 0))
        results[3].append(dot(probs_low, g_heads, 0, 0))
    for index, halves in enumerate(results):
        halves = [value.reshape(codebooks, 1, HALF, width) for value in halves]
        whole = jnp.concatenate(halves, axis=1).reshape(codebooks, FRAME_BLOCK, width)
        out_ref[:, :, index * width : (index + 1) * width] = whole.astype(BF16)


def attend(group, heads, qkv, grad_context):
    codebooks, frames, columns = qkv.shape
    width = columns // 3
    rows = codebooks * HALF
    return pl.pallas_call(
        functools.partial(attend_kernel, heads),
        grid=(frames // FRAME_BLOCK,),
        in_specs=[
            pl.BlockSpec((codebooks, FRAME_BLOCK, columns), lambda f: (0, f, 0)),
            pl.BlockSpec((codebooks, FRAME_BLOCK, width), lambda f: (0, f, group)),
        ],
        out_specs=pl.BlockSpec((codebooks, FRAME_BLOCK, 4 * width), lambda f: (0, f, 0)),
        out_shape=jax.ShapeDtypeStruct((codebooks, frames, 4 * width), BF16),
        compiler_params=params(32),
        cost_estimate=cost(
            12 * heads * rows * rows * width * (frames // HALF),
            2 * codebooks * frames * width * 8,
        ),
        name="attend",
    )(qkv, grad_context)


def backward_kernel(first, last, source_ref, back_ref, *refs):
    refs = list(refs)
    whole_ref = refs.pop()
    out_ref = refs.pop()
    total_ref = None if first else refs.pop(0)
    if last:
        rows_ref, grad_ref, gain_ref = refs.pop(0), refs.pop(0), refs.pop(0)
    fill(source_ref, refs, whole_ref)
    frames = out_ref.shape[1]
    width = whole_ref.shape[1] // 3
    grad = back_ref[...].reshape(frames, 4 * width)[:, width:]
    total = lax.dot_general(
        grad, whole_ref[...], (((1,), (1,)), ((), ())), preferred_element_type=F32
    )
    if not first:
        total = total + total_ref[0]
    if last:
        rows = rows_ref[0].astype(F32)
        inverse_rms = lax.rsqrt(jnp.mean(rows * rows, axis=-1, keepdims=True) + EPSILON)
        scaled = total * gain_ref[...]
        inner = jnp.mean(scaled * rows, axis=-1, keepdims=True)
        total = grad_ref[0].astype(F32) + inverse_rms * (
            scaled - rows * (inverse_rms * inverse_rms * inner)
        )
    out_ref[0] = total.astype(out_ref.dtype)


def backward(source, returned, slots, total, epilogue):
    parts, codebooks, share, columns = returned.shape
    frames = parts * share
    depth, width = slots[0].shape[1:]
    wide = depth * len(slots)
    row_spec = pl.BlockSpec((1, frames, wide), lambda c: (c, 0, 0))
    operands = [source, returned]
    specs = [
        pl.BlockSpec(memory_space=pltpu.SMEM),
        pl.BlockSpec((parts, 1, share, columns), lambda c: (0, c, 0, 0)),
    ]
    if total is not None:
        operands.append(total)
        specs.append(row_spec)
    if epilogue is not None:
        rows, grad_out, gain = epilogue
        operands += [rows, grad_out, gain.reshape(1, wide)]
        specs += [row_spec, row_spec, pl.BlockSpec((1, wide), lambda c: (0, 0))]
    operands += slots
    specs += [pl.BlockSpec((1, depth, width), lambda c: (c, 0, 0)) for _ in slots]
    return pl.pallas_call(
        functools.partial(backward_kernel, total is None, epilogue is not None),
        grid=(codebooks,),
        in_specs=specs,
        out_specs=row_spec,
        out_shape=jax.ShapeDtypeStruct(
            (codebooks, frames, wide), F32 if epilogue is None else BF16
        ),
        scratch_shapes=[pltpu.VMEM((wide, width), BF16)],
        compiler_params=params(40),
        cost_estimate=cost(
            2 * codebooks * frames * wide * width, 2 * codebooks * wide * (width + 5 * frames)
        ),
        name="backward",
    )(*operands)


def output_kernel(groups, source_ref, rows_ref, *refs):
    refs = list(refs)
    whole_ref = refs.pop()
    out_ref = refs.pop()
    fill(source_ref, refs[groups:], whole_ref)
    frames = out_ref.shape[1]
    pieces = [ref[...].reshape(frames, ref.shape[3]) for ref in refs[:groups]]
    result = jnp.dot(
        jnp.concatenate(pieces, axis=1), whole_ref[...], preferred_element_type=F32
    )
    out_ref[0] = (rows_ref[0].astype(F32) + result).astype(BF16)


def output(source, rows, returned, slots):
    codebooks, frames, columns = rows.shape
    parts, _, share, group_columns = returned[0].shape
    depth, width = slots[0].shape[1:]
    row_spec = pl.BlockSpec((1, frames, columns), lambda c: (c, 0, 0))
    return pl.pallas_call(
        functools.partial(output_kernel, len(returned)),
        grid=(codebooks,),
        in_specs=[pl.BlockSpec(memory_space=pltpu.SMEM), row_spec]
        + [
            pl.BlockSpec((parts, 1, share, group_columns // 4), lambda c: (0, c, 0, 0))
            for _ in returned
        ]
        + [pl.BlockSpec((1, depth, width), lambda c: (c, 0, 0)) for _ in slots],
        out_specs=row_spec,
        out_shape=jax.ShapeDtypeStruct(rows.shape, BF16),
        scratch_shapes=[pltpu.VMEM((columns, width), BF16)],
        compiler_params=params(32),
        cost_estimate=cost(
            2 * codebooks * frames * columns * width, 2 * codebooks * columns * (width + 3 * frames)
        ),
        name="output",
    )(source, rows, *returned, *slots)


def tie(values, *after):
    return lax.optimization_barrier((values,) + after)[0]


def body(lines, columns_wide, inputs, norm_gain, w_qkv, w_out, grad_out):
    frames, codebooks, columns = inputs.shape
    parts = lax.axis_size("cb")
    place = lax.axis_index("frame")
    line_place, column_place = place // columns_wide, place % columns_wide
    count = lines * columns_wide

    right = [(i, i + columns_wide) for i in range(count - columns_wide)]
    left = [(j, i) for i, j in right]

    def turn(step):
        return [
            (i, i // columns_wide * columns_wide + (i + step) % columns_wide) for i in range(count)
        ]

    def along_line(own):
        to_right, to_left = [own], [own]
        for _ in range(lines - 1):
            to_right.append(lax.ppermute(to_right[-1], "frame", right))
            to_left.append(lax.ppermute(to_left[-1], "frame", left))
        return [own] + [
            jnp.where(line_place >= k, to_right[k], to_left[lines - k]) for k in range(1, lines)
        ]

    def across(own):
        return [own] + [lax.ppermute(own, "frame", turn(step)) for step in range(1, columns_wide)]

    order = [
        (line_place - k) % lines * columns_wide + (column_place - m) % columns_wide
        for k in range(lines)
        for m in range(columns_wide)
    ]
    source = jnp.stack(order).astype(jnp.int32)

    width = columns // GROUPS
    shards = [w_out] + [
        jnp.concatenate(
            [
                w_qkv[:, :, kind * columns + g * width : kind * columns + (g + 1) * width]
                for kind in range(3)
            ],
            axis=-1,
        )
        for g in range(GROUPS)
    ]
    lined, slots = [], []
    for index, own in enumerate(shards):
        if index >= 2:
            own = tie(own, *lined[index - 2])
        if index < len(shards) - 1:
            line = along_line(own)
            lined.append(line)
            slots.append([piece for shard in line for piece in across(shard)])
        else:
            crossed = [along_line(piece) for piece in across(own)]
            slots.append([crossed[m][k] for k in range(lines) for m in range(columns_wide)])

    wide_in = inputs.astype(F32)
    inverse_rms = lax.rsqrt(jnp.mean(wide_in * wide_in, axis=-1, keepdims=True) + EPSILON)
    normed = (wide_in * inverse_rms * norm_gain).astype(BF16).transpose(1, 0, 2)
    rows = inputs.transpose(1, 0, 2)
    grad_rows = grad_out.transpose(1, 0, 2)

    def exchange(values):
        return lax.all_to_all(values, "cb", split_axis=0, concat_axis=0, tiled=True)

    def joined(values):
        return values.reshape((values.shape[0] * values.shape[1],) + values.shape[2:])

    grad_context = joined(exchange(project(source, grad_rows, slots[0], parts, True)))
    returned, total = [], None
    for g in range(GROUPS):
        weight = slots[1 + g]
        qkv = joined(exchange(project(source, normed, weight, parts, False)))
        mixed = attend(g, HEADS // GROUPS, qkv, grad_context)
        back = exchange(mixed.reshape((parts, codebooks) + mixed.shape[1:]))
        returned.append(back)
        epilogue = (rows, grad_rows, norm_gain) if g == GROUPS - 1 else None
        total = backward(source, back, weight, total, epilogue)
    outputs = output(source, rows, returned, slots[0])
    return outputs.transpose(1, 0, 2), total.transpose(1, 0, 2)


def solution(mesh):
    count = mesh.shape["frame"]
    columns_wide = 2 if count % 2 == 0 else 1
    return jax.shard_map(
        functools.partial(body, count // columns_wide, columns_wide),
        mesh=mesh,
        in_specs=(
            P("frame", "cb", None),
            P(),
            P("cb", "frame", None),
            P("cb", "frame", None),
            P("frame", "cb", None),
        ),
        out_specs=(P("frame", "cb", None), P("frame", "cb", None)),
        check_vma=False,
    )
```

time: 874 us -> 643 us (0.74)
  waiting for transfers between devices: 574 us -> 298 us
  starting transfers between devices: 35.4 us -> 177 us
  matrix products: 121 us -> 0 us
  Pallas kernels: 0 us -> 76 us
  local copies, waits for them, and re-layouts: 103 us -> 56.6 us
  between operations: 14.7 us -> 1.87 us
  other arithmetic: 17.5 us -> 29 us
    all_gather x2 -> x0, waiting for transfers between devices: 525 us -> none  [the longest x1 483 us: body(): lax.all_gather(w_qkv, 'frame', axis=1, tiled=True)]
    ppermute x0 -> x53, waiting for transfers between devices: none -> 268 us  [the longest x17 132 us: across(): lax.ppermute(own, 'frame', turn(step))]
    ppermute x0 -> x53, starting transfers between devices: none -> 138 us  [the longest x18 91.9 us: along_line(): to_right.append(lax.ppermute(to_right[-1], 'frame', right))]
    dot_general x10 -> x0, matrix products: 121 us -> none  [the longest x1 24.8 us: body(): jnp.einsum('fce,cde->fcd', grad_qkv, full_qkv, preferred_element_type=jnp...]
    pallas_call x0 -> x14, Pallas kernels: none -> 76 us  [the longest x4 26.3 us: attend(): pl.pallas_call(functools.partial(attend_kernel, heads), grid=(frames // F...]
    convert_element_type x9 -> x0, local copies, waits for them, and re-layouts: 45.4 us -> none  [the longest x2 11.8 us: attention_grads(): grad_queries.reshape(shape_full).astype(jnp.bfloat16)]
    unnamed x17 -> x156, local copies, waits for them, and re-layouts: 11.2 us -> 53.2 us
    select_n x0 -> x18, other arithmetic: none -> 20.9 us  [along_line(): jnp.where(line_place >= k, to_right[k], to_left[lines - k])]
  transfers between devices with their start and end apart: 10 -> 62, of which waited for: 6 -> 28; matrix products, arithmetic and copies ran while one was open for 24% -> 6% of each run, Pallas kernels for 0% -> 10%
where the time goes in v1:
time: 643 us; the launch traced here: 639 us
  waiting for transfers between devices  298 us (46%)
  starting transfers between devices  177 us (28%)
  Pallas kernels  76 us (12%)
  local copies, waits for them, and re-layouts  56.6 us (9%)
  other arithmetic  29 us (5%)
    ppermute x17, waiting for transfers between devices, across(): lax.ppermute(own, 'frame', turn(step))  132 us
    ppermute x18, starting transfers between devices, along_line(): to_right.append(lax.ppermute(to_right[-1], 'frame', right))  91.9 us
    ppermute x18, waiting for transfers between devices, along_line(): to_left.append(lax.ppermute(to_left[-1], 'frame', left))  72.3 us
    ppermute x18, waiting for transfers between devices, along_line(): to_right.append(lax.ppermute(to_right[-1], 'frame', right))  64.3 us
    unnamed x156, local copies, waits for them, and re-layouts  53.2 us
    all_to_all x9, starting transfers between devices, exchange(): return lax.all_to_all(values, 'cb', split_axis=0, concat_axis=0, tiled=True)  39.3 us
    all_to_all x9, waiting for transfers between devices, exchange(): return lax.all_to_all(values, 'cb', split_axis=0, concat_axis=0, tiled=True)  29.9 us
    pallas_call x4, Pallas kernels, attend(): pl.pallas_call(functools.partial(attend_kernel, heads), grid=(frames // F...  26.3 us
  transfers between devices with their start and end apart: 62, of which 28 were waited for; matrix products, arithmetic and copies ran while one was open for 6% of the time, Pallas kernels for 10%

profile of v1, /device:TPU:0, one launch (start us, length us, event | category | flops | bytes accessed | tf_op | source)
XLA Modules:
  0.0 638.8 jit_solution(2796373598894100080)
XLA Ops:
  17.1 11.7 %collective-permute-done.1 = bf16[4,128,768]{2,1,0:T(8,128)(2,1)S(1)} collective-permute-done((bf16[4,128,768]{2,1,0:T(8,128)(2,1)S(1)}, bf16[4,128,768]{2,1,0:T(8,128)(2,1)S(1)}, u32[]{:S(2)}, u32[]{:S(2)}) %collective-permute-start.1) | collective-permute-done | bytes 786464 | tf_op jit(solution)/shard_map/ppermute | solution.py:267
  35.4 11.2 %collective-permute-done.2 = bf16[4,128,768]{2,1,0:T(8,128)(2,1)S(1)} collective-permute-done((bf16[4,128,768]{2,1,0:T(8,128)(2,1)S(1)}, bf16[4,128,768]{2,1,0:T(8,128)(2,1)S(1)}, u32[]{:S(2)}, u32[]{:S(2)}) %collective-permute-start.2) | collective-permute-done | bytes 786464 | tf_op jit(solution)/shard_map/ppermute | solution.py:268
  58.8 9.3 %collective-permute-done.6 = bf16[4,128,768]{2,1,0:T(8,128)(2,1)} collective-permute-done((bf16[4,128,768]{2,1,0:T(8,128)(2,1)S(1)}, bf16[4,128,768]{2,1,0:T(8,128)(2,1)}, u32[]{:S(2)}, u32[]{:S(2)}) %collective-permute-start.6) | collective-permute-done | bytes 786464 | tf_op jit(solution)/shard_map/ppermute | solution.py:267
  74.7 10.5 %collective-permute-done.3 = bf16[4,128,768]{2,1,0:T(8,128)(2,1)} collective-permute-done((bf16[4,128,768]{2,1,0:T(8,128)(2,1)S(1)}, bf16[4,128,768]{2,1,0:T(8,128)(2,1)}, u32[]{:S(2)}, u32[]{:S(2)}) %collective-permute-start.3) | collective-permute-done | bytes 786464 | tf_op jit(solution)/shard_map/ppermute | solution.py:268
  92.7 13.7 %collective-permute-done.8 = bf16[4,128,768]{2,1,0:T(8,128)(2,1)} collective-permute-done((bf16[4,128,768]{2,1,0:T(8,128)(2,1)}, bf16[4,128,768]{2,1,0:T(8,128)(2,1)}, u32[]{:S(2)}, u32[]{:S(2)}) %collective-permute-start.8) | collective-permute-done | bytes 786464 | tf_op jit(solution)/shard_map/ppermute | solution.py:267
  117.4 11.2 %collective-permute-done.14 = bf16[4,128,1024]{2,1,0:T(8,128)(2,1)} collective-permute-done((bf16[4,128,1024]{2,1,0:T(8,128)(2,1)}, bf16[4,128,1024]{2,1,0:T(8,128)(2,1)}, u32[]{:S(2)}, u32[]{:S(2)}) %collective-permute-start.14) | collective-permute-done | bytes 1048608 | tf_op jit(solution)/shard_map/ppermute | solution.py:268
  140.9 8.8 %collective-permute-done.9.refs_7_ = bf16[4,128,768]{2,1,0:T(8,128)(2,1)S(1)} collective-permute-done((bf16[4,128,768]{2,1,0:T(8,128)(2,1)S(1)}, bf16[4,128,768]{2,1,0:T(8,128)(2,1)S(1)}, u32[]{:S(2)}, u32[]{:S(2)}) %collective-permute-start.9) | collective-permute-done | bytes 786464 | tf_op jit(solution)/shard_map/ppermute | solution.py:274
  151.3 15.2 %collective-permute-done.5.refs_3_ = bf16[4,128,768]{2,1,0:T(8,128)(2,1)S(1)} collective-permute-done((bf16[4,128,768]{2,1,0:T(8,128)(2,1)S(1)}, bf16[4,128,768]{2,1,0:T(8,128)(2,1)S(1)}, u32[]{:S(2)}, u32[]{:S(2)}) %collective-permute-start.5) | collective-permute-done | bytes 786464 | tf_op jit(solution)/shard_map/ppermute | solution.py:274
  190.9 15.4 %collective-permute-done.33 = bf16[4,128,768]{2,1,0:T(8,128)(2,1)} collective-permute-done((bf16[4,128,768]{2,1,0:T(8,128)(2,1)}, bf16[4,128,768]{2,1,0:T(8,128)(2,1)}, u32[]{:S(2)}, u32[]{:S(2)}) %collective-permute-start.33) | collective-permute-done | bytes 786464 | tf_op jit(solution)/shard_map/ppermute | solution.py:268
  217.8 16.2 %collective-permute-done.19.refs_7_.refs_11_ = bf16[4,128,1024]{2,1,0:T(8,128)(2,1)} collective-permute-done((bf16[4,128,1024]{2,1,0:T(8,128)(2,1)}, bf16[4,128,1024]{2,1,0:T(8,128)(2,1)}, u32[]{:S(2)}, u32[]{:S(2)}) %collective-permute-start.19) | collective-permute-done | bytes 1048608 | tf_op jit(solution)/shard_map/ppermute | solution.py:274
  261.3 7.3 %collective-permute-done.37.refs_5_.refs_6_ = bf16[4,128,768]{2,1,0:T(8,128)(2,1)S(1)} collective-permute-done((bf16[4,128,768]{2,1,0:T(8,128)(2,1)S(1)}, bf16[4,128,768]{2,1,0:T(8,128)(2,1)S(1)}, u32[]{:S(2)}, u32[]{:S(2)}) %collective-permute-start.37) | collective-permute-done | bytes 786464 | tf_op jit(solution)/shard_map/ppermute | solution.py:274
  268.6 16.9 %collective-permute-done.39.refs_7_.refs_8_ = bf16[4,128,768]{2,1,0:T(8,128)(2,1)S(1)} collective-permute-done((bf16[4,128,768]{2,1,0:T(8,128)(2,1)S(1)}, bf16[4,128,768]{2,1,0:T(8,128)(2,1)S(1)}, u32[]{:S(2)}, u32[]{:S(2)}) %collective-permute-start.39) | collective-permute-done | bytes 786464 | tf_op jit(solution)/shard_map/ppermute | solution.py:274
  285.4 16.4 %collective-permute-done.35.refs_3_.refs_4_ = bf16[4,128,768]{2,1,0:T(8,128)(2,1)S(1)} collective-permute-done((bf16[4,128,768]{2,1,0:T(8,128)(2,1)S(1)}, bf16[4,128,768]{2,1,0:T(8,128)(2,1)S(1)}, u32[]{:S(2)}, u32[]{:S(2)}) %collective-permute-start.35) | collective-permute-done | bytes 786464 | tf_op jit(solution)/shard_map/ppermute | solution.py:274
  322.1 15.3 %collective-permute-done.23 = bf16[4,128,768]{2,1,0:T(8,128)(2,1)} collective-permute-done((bf16[4,128,768]{2,1,0:T(8,128)(2,1)}, bf16[4,128,768]{2,1,0:T(8,128)(2,1)}, u32[]{:S(2)}, u32[]{:S(2)}) %collective-permute-start.23) | collective-permute-done | bytes 786464 | tf_op jit(solution)/shard_map/ppermute | solution.py:268
  368.6 9.1 %collective-permute-done.27.refs_5_.refs_6_ = bf16[4,128,768]{2,1,0:T(8,128)(2,1)S(1)} collective-permute-done((bf16[4,128,768]{2,1,0:T(8,128)(2,1)S(1)}, bf16[4,128,768]{2,1,0:T(8,128)(2,1)S(1)}, u32[]{:S(2)}, u32[]{:S(2)}) %collective-permute-start.27) | collective-permute-done | bytes 786464 | tf_op jit(solution)/shard_map/ppermute | solution.py:274
  379.0 15.7 %collective-permute-done.40.refs_1_.refs_5_ = bf16[4,128,768]{2,1,0:T(8,128)(2,1)} collective-permute-done((bf16[4,128,768]{2,1,0:T(8,128)(2,1)}, bf16[4,128,768]{2,1,0:T(8,128)(2,1)}, u32[]{:S(2)}, u32[]{:S(2)}) %collective-permute-start.40) | collective-permute-done | bytes 786464 | tf_op jit(solution)/shard_map/ppermute | solution.py:274
  399.9 11.5 %collective-permute-done.29.refs_7_.refs_8_ = bf16[4,128,768]{2,1,0:T(8,128)(2,1)S(1)} collective-permute-done((bf16[4,128,768]{2,1,0:T(8,128)(2,1)S(1)}, bf16[4,128,768]{2,1,0:T(8,128)(2,1)S(1)}, u32[]{:S(2)}, u32[]{:S(2)}) %collective-permute-start.29) | collective-permute-done | bytes 786464 | tf_op jit(solution)/shard_map/ppermute | solution.py:274
  412.7 14.7 %collective-permute-done.25.refs_3_.refs_4_ = bf16[4,128,768]{2,1,0:T(8,128)(2,1)S(1)} collective-permute-done((bf16[4,128,768]{2,1,0:T(8,128)(2,1)S(1)}, bf16[4,128,768]{2,1,0:T(8,128)(2,1)S(1)}, u32[]{:S(2)}, u32[]{:S(2)}) %collective-permute-start.25) | collective-permute-done | bytes 786464 | tf_op jit(solution)/shard_map/ppermute | solution.py:274
  454.0 9.2 %collective-permute-done.49 = bf16[4,128,768]{2,1,0:T(8,128)(2,1)} collective-permute-done((bf16[4,128,768]{2,1,0:T(8,128)(2,1)}, bf16[4,128,768]{2,1,0:T(8,128)(2,1)}, u32[]{:S(2)}, u32[]{:S(2)}) %collective-permute-start.49) | collective-permute-done | bytes 786464 | tf_op jit(solution)/shard_map/ppermute | solution.py:267
  503.5 9.8 %collective-permute-done.52 = bf16[4,128,768]{2,1,0:T(8,128)(2,1)S(1)} collective-permute-done((bf16[4,128,768]{2,1,0:T(8,128)(2,1)}, bf16[4,128,768]{2,1,0:T(8,128)(2,1)S(1)}, u32[]{:S(2)}, u32[]{:S(2)}) %collective-permute-start.52) | collective-permute-done | bytes 786464 | tf_op jit(solution)/shard_map/ppermute | solution.py:267
  529.1 6.6 %attend.5 = bf16[16,64,1024]{2,1,0:T(8,128)(2,1)S(1)} custom-call(bf16[16,64,768]{2,1,0:T(8,128)(2,1)} %bitcast.14.qkv_ref, bf16[16,64,1024]{2,1,0:T(8,128)(2,1)} %bitcast.12.grad_ref), custom_call_target="tpu_custom_call" | custom-call | flops 1610612736 | bytes 4194304 | tf_op jit(solution)/shard_map/attend/pallas_call | solution.py:125
  537.1 12.2 %all-to-all-done.7 = bf16[4,4,64,768]{3,2,1,0:T(8,128)(2,1)} async-done(((bf16[4,4,64,768]{3,2,1,0:T(8,128)(2,1)}), bf16[4,4,64,768]{3,2,1,0:T(8,128)(2,1)}, u32[]{:S(2)}, u32[]{:S(2)}) %all-to-all-start.7) | async-done | bytes 1572896 | tf_op jit(solution)/shard_map/all_to_all | solution.py:313
  552.9 6.6 %attend.7 = bf16[16,64,1024]{2,1,0:T(8,128)(2,1)S(1)} custom-call(bf16[16,64,768]{2,1,0:T(8,128)(2,1)} %bitcast.18.qkv_ref, bf16[16,64,1024]{2,1,0:T(8,128)(2,1)} %bitcast.12.grad_ref), custom_call_target="tpu_custom_call" | custom-call | flops 1610612736 | bytes 4194304 | tf_op jit(solution)/shard_map/attend/pallas_call | solution.py:125
  560.9 17.7 %all-to-all-done.4.refs_1_.back_ref = bf16[4,4,64,1024]{3,2,1,0:T(8,128)(2,1)S(1)} async-done(((bf16[4,4,64,1024]{3,2,1,0:T(8,128)(2,1)}), bf16[4,4,64,1024]{3,2,1,0:T(8,128)(2,1)S(1)}, u32[]{:S(2)}, u32[]{:S(2)}) %all-to-all-start.4) | async-done | bytes 2097184 | tf_op jit(solution)/shard_map/all_to_all | solution.py:313
  (297 shorter events, 344.7 us)
Async XLA Ops:
  34.1 52.4 %collective-permute-start.13 = (bf16[4,128,1024]{2,1,0:T(8,128)(2,1)S(1)}, bf16[4,128,1024]{2,1,0:T(8,128)(2,1)}, u32[]{:S(2)}, u32[]{:S(2)}) collective-permute-start(bf16[4,128,1024]{2,1,0:T(8,128)(2,1)S(1)} %collective-permute-done.12), channel_id=1, source_target_pairs={{2,0},{3,1},{4,2},{5,3},{6,4},{7,5},{10,8},{11,9},{12,10},{13,11},... | collective-permute-start | bytes 3145736 | tf_op jit(solution)/shard_map/ppermute | solution.py:268
  56.8 58.9 %collective-permute-start.10 = (bf16[4,128,1024]{2,1,0:T(8,128)(2,1)}, bf16[4,128,1024]{2,1,0:T(8,128)(2,1)}, u32[]{:S(2)}, u32[]{:S(2)}) collective-permute-start(bf16[4,128,1024]{2,1,0:T(8,128)(2,1)} %refs_4_.1), channel_id=1, source_target_pairs={{0,1},{1,0},{2,3},{3,2},{4,5},{5,4},{6,7},{7,6},{8,9},{9,8},{10,11... | collective-permute-start | bytes 3145736 | tf_op jit(solution)/shard_map/ppermute | solution.py:274
  86.5 42.1 %collective-permute-start.14 = (bf16[4,128,1024]{2,1,0:T(8,128)(2,1)}, bf16[4,128,1024]{2,1,0:T(8,128)(2,1)}, u32[]{:S(2)}, u32[]{:S(2)}) collective-permute-start(bf16[4,128,1024]{2,1,0:T(8,128)(2,1)} %collective-permute-done.13), channel_id=1, source_target_pairs={{2,0},{3,1},{4,2},{5,3},{6,4},{7,5},{10,8},{11,9},{12,10},{13,11},... | collective-permute-start | bytes 3145736 | tf_op jit(solution)/shard_map/ppermute | solution.py:268
  115.7 50.8 %collective-permute-start.5 = (bf16[4,128,768]{2,1,0:T(8,128)(2,1)S(1)}, bf16[4,128,768]{2,1,0:T(8,128)(2,1)S(1)}, u32[]{:S(2)}, u32[]{:S(2)}) collective-permute-start(bf16[4,128,768]{2,1,0:T(8,128)(2,1)S(1)} %broadcast_select_fusion.17.refs_2_), channel_id=1, source_target_pairs={{0,1},{1,0},{2,3},{3,2},{4,5},{5,4},{6,7},{7,6},{8,9},{9,8},{10,11... | collective-permute-start | bytes 2359304 | tf_op jit(solution)/shard_map/ppermute | solution.py:274
  134.7 49.4 %collective-permute-start.32 = (bf16[4,128,768]{2,1,0:T(8,128)(2,1)}, bf16[4,128,768]{2,1,0:T(8,128)(2,1)}, u32[]{:S(2)}, u32[]{:S(2)}) collective-permute-start(bf16[4,128,768]{2,1,0:T(8,128)(2,1)} %pad_maximum_fusion.2.refs_0_.refs_1_), channel_id=1, source_target_pairs={{2,0},{3,1},{4,2},{5,3},{6,4},{7,5},{10,8},{11,9},{12,10},{13,11},... | collective-permute-start | bytes 2359304 | tf_op jit(solution)/shard_map/ppermute | solution.py:268
  139.5 72.3 %collective-permute-start.17 = (bf16[4,128,1024]{2,1,0:T(8,128)(2,1)S(1)}, bf16[4,128,1024]{2,1,0:T(8,128)(2,1)}, u32[]{:S(2)}, u32[]{:S(2)}) collective-permute-start(bf16[4,128,1024]{2,1,0:T(8,128)(2,1)S(1)} %broadcast_select_fusion.1.refs_4_.refs_8_), channel_id=1, source_target_pairs={{0,1},{1,0},{2,3},{3,2},{4,5},{5,4},{6,7},{7,6},{8,9},{9,8},{10,11... | collective-permute-start | bytes 3145736 | tf_op jit(solution)/shard_map/ppermute | solution.py:274
  149.7 62.7 %collective-permute-start.15 = (bf16[4,128,1024]{2,1,0:T(8,128)(2,1)}, bf16[4,128,1024]{2,1,0:T(8,128)(2,1)}, u32[]{:S(2)}, u32[]{:S(2)}) collective-permute-start(bf16[4,128,1024]{2,1,0:T(8,128)(2,1)} %broadcast_select_fusion.2.refs_2_.refs_6_), channel_id=1, source_target_pairs={{0,1},{1,0},{2,3},{3,2},{4,5},{5,4},{6,7},{7,6},{8,9},{9,8},{10,11... | collective-permute-start | bytes 3145736 | tf_op jit(solution)/shard_map/ppermute | solution.py:274
  166.5 67.5 %collective-permute-start.19 = (bf16[4,128,1024]{2,1,0:T(8,128)(2,1)}, bf16[4,128,1024]{2,1,0:T(8,128)(2,1)}, u32[]{:S(2)}, u32[]{:S(2)}) collective-permute-start(bf16[4,128,1024]{2,1,0:T(8,128)(2,1)} %broadcast_select_fusion.refs_6_.refs_10_), channel_id=1, source_target_pairs={{0,1},{1,0},{2,3},{3,2},{4,5},{5,4},{6,7},{7,6},{8,9},{9,8},{10,11... | collective-permute-start | bytes 3145736 | tf_op jit(solution)/shard_map/ppermute | solution.py:274
  179.8 62.7 %all-to-all-start = ((bf16[4,4,64,768]{3,2,1,0:T(8,128)(2,1)}), bf16[4,4,64,768]{3,2,1,0:T(8,128)(2,1)}, u32[]{:S(2)}, u32[]{:S(2)}) async-start(bf16[4,4,64,768]{3,2,1,0:T(8,128)(2,1)} %copy-done.41), calls=%async_computation | async-start | bytes 3145728 | tf_op jit(solution)/shard_map/all_to_all | solution.py:313
  185.4 64.5 %collective-permute-start.38 = (bf16[4,128,768]{2,1,0:T(8,128)(2,1)}, bf16[4,128,768]{2,1,0:T(8,128)(2,1)}, u32[]{:S(2)}, u32[]{:S(2)}) collective-permute-start(bf16[4,128,768]{2,1,0:T(8,128)(2,1)} %collective-permute-done.36), channel_id=1, source_target_pairs={{0,2},{1,3},{2,4},{3,5},{4,6},{5,7},{8,10},{9,11},{10,12},{11,13},... | collective-permute-start | bytes 2359304 | tf_op jit(solution)/shard_map/ppermute | solution.py:267
  206.2 45.4 %collective-permute-start.34 = (bf16[4,128,768]{2,1,0:T(8,128)(2,1)}, bf16[4,128,768]{2,1,0:T(8,128)(2,1)}, u32[]{:S(2)}, u32[]{:S(2)}) collective-permute-start(bf16[4,128,768]{2,1,0:T(8,128)(2,1)} %collective-permute-done.33), channel_id=1, source_target_pairs={{2,0},{3,1},{4,2},{5,3},{6,4},{7,5},{10,8},{11,9},{12,10},{13,11},... | collective-permute-start | bytes 2359304 | tf_op jit(solution)/shard_map/ppermute | solution.py:268
  211.8 42.8 %collective-permute-start.30 = (bf16[4,128,768]{2,1,0:T(8,128)(2,1)}, bf16[4,128,768]{2,1,0:T(8,128)(2,1)}, u32[]{:S(2)}, u32[]{:S(2)}) collective-permute-start(bf16[4,128,768]{2,1,0:T(8,128)(2,1)} %pad_maximum_fusion.2.refs_0_.refs_1_), channel_id=1, source_target_pairs={{0,1},{1,0},{2,3},{3,2},{4,5},{5,4},{6,7},{7,6},{8,9},{9,8},{10,11... | collective-permute-start | bytes 2359304 | tf_op jit(solution)/shard_map/ppermute | solution.py:274
  212.4 43.5 %collective-permute-start.21 = (bf16[4,128,768]{2,1,0:T(8,128)(2,1)}, bf16[4,128,768]{2,1,0:T(8,128)(2,1)}, u32[]{:S(2)}, u32[]{:S(2)}) collective-permute-start(bf16[4,128,768]{2,1,0:T(8,128)(2,1)} %pad_maximum_fusion.1.refs_0_.refs_1_), channel_id=1, source_target_pairs={{0,2},{1,3},{2,4},{3,5},{4,6},{5,7},{8,10},{9,11},{10,12},{11,13},... | collective-permute-start | bytes 2359304 | tf_op jit(solution)/shard_map/ppermute | solution.py:267
  242.4 68.5 %all-to-all-start.1 = ((bf16[4,4,64,1024]{3,2,1,0:T(8,128)(2,1)}), bf16[4,4,64,1024]{3,2,1,0:T(8,128)(2,1)}, u32[]{:S(2)}, u32[]{:S(2)}) async-start(bf16[4,4,64,1024]{3,2,1,0:T(8,128)(2,1)} %copy-done.6), calls=%async_computation.1 | async-start | bytes 4194304 | tf_op jit(solution)/shard_map/all_to_all | solution.py:313
  252.8 49.0 %collective-permute-start.35 = (bf16[4,128,768]{2,1,0:T(8,128)(2,1)S(1)}, bf16[4,128,768]{2,1,0:T(8,128)(2,1)S(1)}, u32[]{:S(2)}, u32[]{:S(2)}) collective-permute-start(bf16[4,128,768]{2,1,0:T(8,128)(2,1)S(1)} %broadcast_select_fusion.15.refs_2_.refs_3_), channel_id=1, source_target_pairs={{0,1},{1,0},{2,3},{3,2},{4,5},{5,4},{6,7},{7,6},{8,9},{9,8},{10,11... | collective-permute-start | bytes 2359304 | tf_op jit(solution)/shard_map/ppermute | solution.py:274
  254.5 60.8 %collective-permute-start.22 = (bf16[4,128,768]{2,1,0:T(8,128)(2,1)}, bf16[4,128,768]{2,1,0:T(8,128)(2,1)}, u32[]{:S(2)}, u32[]{:S(2)}) collective-permute-start(bf16[4,128,768]{2,1,0:T(8,128)(2,1)} %pad_maximum_fusion.1.refs_0_.refs_1_), channel_id=1, source_target_pairs={{2,0},{3,1},{4,2},{5,3},{6,4},{7,5},{10,8},{11,9},{12,10},{13,11},... | collective-permute-start | bytes 2359304 | tf_op jit(solution)/shard_map/ppermute | solution.py:268
  255.8 60.8 %collective-permute-start.26 = (bf16[4,128,768]{2,1,0:T(8,128)(2,1)}, bf16[4,128,768]{2,1,0:T(8,128)(2,1)}, u32[]{:S(2)}, u32[]{:S(2)}) collective-permute-start(bf16[4,128,768]{2,1,0:T(8,128)(2,1)} %collective-permute-done.21), channel_id=1, source_target_pairs={{0,2},{1,3},{2,4},{3,5},{4,6},{5,7},{8,10},{9,11},{10,12},{11,13},... | collective-permute-start | bytes 2359304 | tf_op jit(solution)/shard_map/ppermute | solution.py:267
  350.3 86.2 %all-to-all-start.2 = ((bf16[4,4,64,1024]{3,2,1,0:T(8,128)(2,1)}), bf16[4,4,64,1024]{3,2,1,0:T(8,128)(2,1)}, u32[]{:S(2)}, u32[]{:S(2)}) async-start(bf16[4,4,64,1024]{3,2,1,0:T(8,128)(2,1)} %bitcast.34), calls=%async_computation.2 | async-start | bytes 4194304 | tf_op jit(solution)/shard_map/all_to_all | solution.py:313
  361.7 49.7 %collective-permute-start.29 = (bf16[4,128,768]{2,1,0:T(8,128)(2,1)S(1)}, bf16[4,128,768]{2,1,0:T(8,128)(2,1)S(1)}, u32[]{:S(2)}, u32[]{:S(2)}) collective-permute-start(bf16[4,128,768]{2,1,0:T(8,128)(2,1)S(1)} %broadcast_select_fusion.6.refs_6_.refs_7_), channel_id=1, source_target_pairs={{0,1},{1,0},{2,3},{3,2},{4,5},{5,4},{6,7},{7,6},{8,9},{9,8},{10,11... | collective-permute-start | bytes 2359304 | tf_op jit(solution)/shard_map/ppermute | solution.py:274
  362.0 65.4 %collective-permute-start.25 = (bf16[4,128,768]{2,1,0:T(8,128)(2,1)S(1)}, bf16[4,128,768]{2,1,0:T(8,128)(2,1)S(1)}, u32[]{:S(2)}, u32[]{:S(2)}) collective-permute-start(bf16[4,128,768]{2,1,0:T(8,128)(2,1)S(1)} %broadcast_select_fusion.16.refs_2_.refs_3_), channel_id=1, source_target_pairs={{0,1},{1,0},{2,3},{3,2},{4,5},{5,4},{6,7},{7,6},{8,9},{9,8},{10,11... | collective-permute-start | bytes 2359304 | tf_op jit(solution)/shard_map/ppermute | solution.py:274
  363.7 77.1 %collective-permute-start.41 = (bf16[4,128,768]{2,1,0:T(8,128)(2,1)}, bf16[4,128,768]{2,1,0:T(8,128)(2,1)}, u32[]{:S(2)}, u32[]{:S(2)}) collective-permute-start(bf16[4,128,768]{2,1,0:T(8,128)(2,1)} %pad_maximum_fusion.3.refs_0_.refs_4_), channel_id=1, source_target_pairs={{0,2},{1,3},{2,4},{3,5},{4,6},{5,7},{8,10},{9,11},{10,12},{11,13},... | collective-permute-start | bytes 2359304 | tf_op jit(solution)/shard_map/ppermute | solution.py:267
  377.7 68.3 %collective-permute-start.42 = (bf16[4,128,768]{2,1,0:T(8,128)(2,1)}, bf16[4,128,768]{2,1,0:T(8,128)(2,1)}, u32[]{:S(2)}, u32[]{:S(2)}) collective-permute-start(bf16[4,128,768]{2,1,0:T(8,128)(2,1)} %pad_maximum_fusion.3.refs_0_.refs_4_), channel_id=1, source_target_pairs={{2,0},{3,1},{4,2},{5,3},{6,4},{7,5},{10,8},{11,9},{12,10},{13,11},... | collective-permute-start | bytes 2359304 | tf_op jit(solution)/shard_map/ppermute | solution.py:268
  394.7 52.6 %collective-permute-start.45 = (bf16[4,128,768]{2,1,0:T(8,128)(2,1)}, bf16[4,128,768]{2,1,0:T(8,128)(2,1)}, u32[]{:S(2)}, u32[]{:S(2)}) collective-permute-start(bf16[4,128,768]{2,1,0:T(8,128)(2,1)} %collective-permute-done.40.refs_1_.refs_5_), channel_id=1, source_target_pairs={{0,2},{1,3},{2,4},{3,5},{4,6},{5,7},{8,10},{9,11},{10,12},{11,13},... | collective-permute-start | bytes 2359304 | tf_op jit(solution)/shard_map/ppermute | solution.py:267
  477.7 47.1 %all-to-all-start.6 = ((bf16[4,4,64,1024]{3,2,1,0:T(8,128)(2,1)}), bf16[4,4,64,1024]{3,2,1,0:T(8,128)(2,1)}, u32[]{:S(2)}, u32[]{:S(2)}) async-start(bf16[4,4,64,1024]{3,2,1,0:T(8,128)(2,1)} %bitcast.35), calls=%async_computation.6 | async-start | bytes 4194304 | tf_op jit(solution)/shard_map/all_to_all | solution.py:313
  (114 other events, 2378.6 us)

commit v2 on v1

--- a/solution.py
+++ b/solution.py
@@ -242,8 +242,8 @@
     )(source, rows, *returned, *slots)
 
 
-def tie(values, *after):
-    return lax.optimization_barrier((values,) + after)[0]
+def tie(values, after):
+    return lax.optimization_barrier((values,) + tuple(after))[0]
 
 
 def body(lines, columns_wide, inputs, norm_gain, w_qkv, w_out, grad_out):
@@ -253,25 +253,12 @@
     line_place, column_place = place // columns_wide, place % columns_wide
     count = lines * columns_wide
 
-    right = [(i, i + columns_wide) for i in range(count - columns_wide)]
-    left = [(j, i) for i, j in right]
+    along = [(i, (i + columns_wide) % count) for i in range(count)]
 
     def turn(step):
         return [
             (i, i // columns_wide * columns_wide + (i + step) % columns_wide) for i in range(count)
         ]
-
-    def along_line(own):
-        to_right, to_left = [own], [own]
-        for _ in range(lines - 1):
-            to_right.append(lax.ppermute(to_right[-1], "frame", right))
-            to_left.append(lax.ppermute(to_left[-1], "frame", left))
-        return [own] + [
-            jnp.where(line_place >= k, to_right[k], to_left[lines - k]) for k in range(1, lines)
-        ]
-
-    def across(own):
-        return [own] + [lax.ppermute(own, "frame", turn(step)) for step in range(1, columns_wide)]
 
     order = [
         (line_place - k) % lines * columns_wide + (column_place - m) % columns_wide
@@ -291,17 +278,42 @@
         )
         for g in range(GROUPS)
     ]
-    lined, slots = [], []
-    for index, own in enumerate(shards):
-        if index >= 2:
-            own = tie(own, *lined[index - 2])
-        if index < len(shards) - 1:
-            line = along_line(own)
-            lined.append(line)
-            slots.append([piece for shard in line for piece in across(shard)])
-        else:
-            crossed = [along_line(piece) for piece in across(own)]
-            slots.append([crossed[m][k] for k in range(lines) for m in range(columns_wide)])
+    final = len(shards) - 1
+    line_steps = [(w, k, 0) for w in range(final) for k in range(1, lines)]
+    line_steps += [(final, k, m) for k in range(1, lines) for m in range(columns_wide)]
+    cross_steps = [(w, k, m) for w in range(final) for k in range(lines) for m in range(1, columns_wide)]
+    cross_steps += [(final, 0, m) for m in range(1, columns_wide)]
+
+    def rank(step):
+        early = 3 if step in cross_steps and step[0] == final else 0
+        return 2 * step[0] + 2 * step[1] - early, step[0], step[2]
+
+    line_steps, cross_steps = sorted(line_steps, key=rank), sorted(cross_steps, key=rank)
+    held = {(w, 0, 0): shard for w, shard in enumerate(shards)}
+    recent, pending = [], []
+    while line_steps or cross_steps:
+        landed = []
+        after = recent[-2] if len(recent) > 1 else []
+        ready = [s for s in line_steps if (s[0], s[1] - 1, s[2]) in held]
+        if ready:
+            step = ready[0]
+            line_steps.remove(step)
+            operand = held[(step[0], step[1] - 1, step[2])]
+            landed.append((step, lax.ppermute(tie(operand, after), "frame", along)))
+        ready = [s for s in cross_steps if (s[0], s[1], 0) in held]
+        if ready:
+            step = ready[0]
+            cross_steps.remove(step)
+            operand = held[(step[0], step[1], 0)]
+            landed.append((step, lax.ppermute(tie(operand, after), "frame", turn(step[2]))))
+        recent.append([value for _, value in landed])
+        held.update(pending)
+        pending = landed
+    held.update(pending)
+    slots = [
+        [held[(w, k, m)] for k in range(lines) for m in range(columns_wide)]
+        for w in range(len(shards))
+    ]
 
     wide_in = inputs.astype(F32)
     inverse_rms = lax.rsqrt(jnp.mean(wide_in * wide_in, axis=-1, keepdims=True) + EPSILON)

time: 643 us -> 558 us (0.87)
  starting transfers between devices: 177 us -> 85.6 us
  waiting for transfers between devices: 298 us -> 324 us
  other arithmetic: 29 us -> 4.62 us
    ppermute x53 -> x35, starting transfers between devices: 138 us -> 47.5 us  [the longest x17 24.3 us: body(): lax.ppermute(tie(operand, after), 'frame', turn(step[2]))]
    select_n x18 -> x0, other arithmetic: 20.9 us -> none  [along_line(): jnp.where(line_place >= k, to_right[k], to_left[lines - k])]
    all_to_all x9, waiting for transfers between devices: 29.9 us -> 46.4 us  [exchange(): return lax.all_to_all(values, 'cb', split_axis=0, concat_axis=0, tiled=True)]
    ppermute x53 -> x35, waiting for transfers between devices: 268 us -> 278 us  [the longest x18 185 us: body(): landed.append((step, lax.ppermute(tie(operand, after), 'frame', along)))]
    unnamed x156 -> x154, local copies, waits for them, and re-layouts: 53.2 us -> 60.3 us
  transfers between devices with their start and end apart: 62 -> 44, of which waited for: 28 -> 26; matrix products, arithmetic and copies ran while one was open for 6% -> 2% of each run, Pallas kernels for 10% -> 12%
where the time goes in v2:
time: 558 us; the launch traced here: 556 us
  waiting for transfers between devices  324 us (58%)
  starting transfers between devices  85.6 us (15%)
  Pallas kernels  77.8 us (14%)
  local copies, waits for them, and re-layouts  62.4 us (11%)
    ppermute x18, waiting for transfers between devices, body(): landed.append((step, lax.ppermute(tie(operand, after), 'frame', along)))  185 us
    ppermute x17, waiting for transfers between devices, body(): lax.ppermute(tie(operand, after), 'frame', turn(step[2]))  92.9 us
    unnamed x154, local copies, waits for them, and re-layouts  60.3 us
    all_to_all x9, waiting for transfers between devices, exchange(): return lax.all_to_all(values, 'cb', split_axis=0, concat_axis=0, tiled=True)  46.4 us
    all_to_all x9, starting transfers between devices, exchange(): return lax.all_to_all(values, 'cb', split_axis=0, concat_axis=0, tiled=True)  38.1 us
    pallas_call x4, Pallas kernels, attend(): pl.pallas_call(functools.partial(attend_kernel, heads), grid=(frames // F...  26.2 us
    ppermute x17, starting transfers between devices, body(): lax.ppermute(tie(operand, after), 'frame', turn(step[2]))  24.3 us
    pallas_call x5, Pallas kernels, project(): pl.pallas_call(functools.partial(project_kernel, back), grid=(codebooks,)...  23.3 us
  transfers between devices with their start and end apart: 44, of which 26 were waited for; matrix products, arithmetic and copies ran while one was open for 2% of the time, Pallas kernels for 12%

profile of v2, /device:TPU:0, one launch (start us, length us, event | category | flops | bytes accessed | tf_op | source)
XLA Modules:
  0.0 556.2 jit_solution(8482059844349650598)
XLA Ops:
  10.4 19.5 %collective-permute-done.4.refs_2_.refs_6_ = bf16[4,128,1024]{2,1,0:T(8,128)(2,1)S(1)} collective-permute-done((bf16[4,128,1024]{2,1,0:T(8,128)(2,1)}, bf16[4,128,1024]{2,1,0:T(8,128)(2,1)S(1)}, u32[]{:S(2)}, u32[]{:S(2)}) %collective-permute-start.4) | collective-permute-done | bytes 1048608 | tf_op jit(solution)/shard_map/ppermute | solution.py:302
  33.1 13.8 %collective-permute-done.refs_1_ = bf16[4,128,768]{2,1,0:T(8,128)(2,1)S(1)} collective-permute-done((bf16[4,128,768]{2,1,0:T(8,128)(2,1)S(1)}, bf16[4,128,768]{2,1,0:T(8,128)(2,1)S(1)}, u32[]{:S(2)}, u32[]{:S(2)}) %collective-permute-start) | collective-permute-done | bytes 786464 | tf_op jit(solution)/shard_map/ppermute | solution.py:308
  51.8 17.5 %collective-permute-done.6.refs_4_.refs_8_ = bf16[4,128,1024]{2,1,0:T(8,128)(2,1)S(1)} collective-permute-done((bf16[4,128,1024]{2,1,0:T(8,128)(2,1)S(1)}, bf16[4,128,1024]{2,1,0:T(8,128)(2,1)S(1)}, u32[]{:S(2)}, u32[]{:S(2)}) %collective-permute-start.6) | collective-permute-done | bytes 1048608 | tf_op jit(solution)/shard_map/ppermute | solution.py:302
  73.5 12.7 %collective-permute-done.3.refs_4_ = bf16[4,128,768]{2,1,0:T(8,128)(2,1)} collective-permute-done((bf16[4,128,768]{2,1,0:T(8,128)(2,1)S(1)}, bf16[4,128,768]{2,1,0:T(8,128)(2,1)}, u32[]{:S(2)}, u32[]{:S(2)}) %collective-permute-start.3) | collective-permute-done | bytes 786464 | tf_op jit(solution)/shard_map/ppermute | solution.py:302
  90.2 18.5 %collective-permute-done.8.refs_6_.refs_10_ = bf16[4,128,1024]{2,1,0:T(8,128)(2,1)} collective-permute-done((bf16[4,128,1024]{2,1,0:T(8,128)(2,1)S(1)}, bf16[4,128,1024]{2,1,0:T(8,128)(2,1)}, u32[]{:S(2)}, u32[]{:S(2)}) %collective-permute-start.8) | collective-permute-done | bytes 1048608 | tf_op jit(solution)/shard_map/ppermute | solution.py:302
  112.7 12.8 %collective-permute-done.13.refs_2_.refs_3_ = bf16[4,128,768]{2,1,0:T(8,128)(2,1)} collective-permute-done((bf16[4,128,768]{2,1,0:T(8,128)(2,1)S(1)}, bf16[4,128,768]{2,1,0:T(8,128)(2,1)}, u32[]{:S(2)}, u32[]{:S(2)}) %collective-permute-start.13) | collective-permute-done | bytes 786464 | tf_op jit(solution)/shard_map/ppermute | solution.py:302
  129.6 12.7 %collective-permute-done.10.refs_6_ = bf16[4,128,768]{2,1,0:T(8,128)(2,1)S(1)} collective-permute-done((bf16[4,128,768]{2,1,0:T(8,128)(2,1)}, bf16[4,128,768]{2,1,0:T(8,128)(2,1)S(1)}, u32[]{:S(2)}, u32[]{:S(2)}) %collective-permute-start.10) | collective-permute-done | bytes 786464 | tf_op jit(solution)/shard_map/ppermute | solution.py:302
  147.9 11.4 %collective-permute-done.15.refs_4_.refs_5_ = bf16[4,128,768]{2,1,0:T(8,128)(2,1)} collective-permute-done((bf16[4,128,768]{2,1,0:T(8,128)(2,1)}, bf16[4,128,768]{2,1,0:T(8,128)(2,1)}, u32[]{:S(2)}, u32[]{:S(2)}) %collective-permute-start.15) | collective-permute-done | bytes 786464 | tf_op jit(solution)/shard_map/ppermute | solution.py:302
  188.3 10.4 %collective-permute-done.18.refs_3_.refs_4_ = bf16[4,128,768]{2,1,0:T(8,128)(2,1)} collective-permute-done((bf16[4,128,768]{2,1,0:T(8,128)(2,1)}, bf16[4,128,768]{2,1,0:T(8,128)(2,1)}, u32[]{:S(2)}, u32[]{:S(2)}) %collective-permute-start.18) | collective-permute-done | bytes 786464 | tf_op jit(solution)/shard_map/ppermute | solution.py:308
  202.9 12.5 %collective-permute-done.22.refs_1_.refs_2_ = bf16[4,128,768]{2,1,0:T(8,128)(2,1)S(1)} collective-permute-done((bf16[4,128,768]{2,1,0:T(8,128)(2,1)}, bf16[4,128,768]{2,1,0:T(8,128)(2,1)S(1)}, u32[]{:S(2)}, u32[]{:S(2)}) %collective-permute-start.22) | collective-permute-done | bytes 786464 | tf_op jit(solution)/shard_map/ppermute | solution.py:308
  220.3 12.0 %collective-permute-done.19.refs_7_ = bf16[4,128,768]{2,1,0:T(8,128)(2,1)S(1)} collective-permute-done((bf16[4,128,768]{2,1,0:T(8,128)(2,1)}, bf16[4,128,768]{2,1,0:T(8,128)(2,1)S(1)}, u32[]{:S(2)}, u32[]{:S(2)}) %collective-permute-start.19) | collective-permute-done | bytes 786464 | tf_op jit(solution)/shard_map/ppermute | solution.py:308
  249.3 16.8 %collective-permute-done.25.refs_7_.refs_8_ = bf16[4,128,768]{2,1,0:T(8,128)(2,1)S(1)} collective-permute-done((bf16[4,128,768]{2,1,0:T(8,128)(2,1)}, bf16[4,128,768]{2,1,0:T(8,128)(2,1)S(1)}, u32[]{:S(2)}, u32[]{:S(2)}) %collective-permute-start.25) | collective-permute-done | bytes 786464 | tf_op jit(solution)/shard_map/ppermute | solution.py:308
  281.0 20.2 %collective-permute-done.26.refs_2_.refs_6_ = bf16[4,128,768]{2,1,0:T(8,128)(2,1)} collective-permute-done((bf16[4,128,768]{2,1,0:T(8,128)(2,1)S(1)}, bf16[4,128,768]{2,1,0:T(8,128)(2,1)}, u32[]{:S(2)}, u32[]{:S(2)}) %collective-permute-start.26) | collective-permute-done | bytes 786464 | tf_op jit(solution)/shard_map/ppermute | solution.py:302
  316.5 7.3 %collective-permute-done.28.refs_6_.refs_7_ = bf16[4,128,768]{2,1,0:T(8,128)(2,1)} collective-permute-done((bf16[4,128,768]{2,1,0:T(8,128)(2,1)}, bf16[4,128,768]{2,1,0:T(8,128)(2,1)}, u32[]{:S(2)}, u32[]{:S(2)}) %collective-permute-start.28) | collective-permute-done | bytes 786464 | tf_op jit(solution)/shard_map/ppermute | solution.py:302
  325.3 14.0 %collective-permute-done.30.refs_4_.refs_8_ = bf16[4,128,768]{2,1,0:T(8,128)(2,1)} collective-permute-done((bf16[4,128,768]{2,1,0:T(8,128)(2,1)}, bf16[4,128,768]{2,1,0:T(8,128)(2,1)}, u32[]{:S(2)}, u32[]{:S(2)}) %collective-permute-start.30) | collective-permute-done | bytes 786464 | tf_op jit(solution)/shard_map/ppermute | solution.py:302
  340.8 16.9 %collective-permute-done.31.refs_7_.refs_8_ = bf16[4,128,768]{2,1,0:T(8,128)(2,1)S(1)} collective-permute-done((bf16[4,128,768]{2,1,0:T(8,128)(2,1)}, bf16[4,128,768]{2,1,0:T(8,128)(2,1)S(1)}, u32[]{:S(2)}, u32[]{:S(2)}) %collective-permute-start.31) | collective-permute-done | bytes 786464 | tf_op jit(solution)/shard_map/ppermute | solution.py:308
  372.2 22.1 %collective-permute-done.33.refs_6_.refs_10_ = bf16[4,128,768]{2,1,0:T(8,128)(2,1)S(1)} collective-permute-done((bf16[4,128,768]{2,1,0:T(8,128)(2,1)}, bf16[4,128,768]{2,1,0:T(8,128)(2,1)S(1)}, u32[]{:S(2)}, u32[]{:S(2)}) %collective-permute-start.33) | collective-permute-done | bytes 786464 | tf_op jit(solution)/shard_map/ppermute | solution.py:302
  394.3 16.4 %collective-permute-done.34.refs_7_.refs_11_ = bf16[4,128,768]{2,1,0:T(8,128)(2,1)S(1)} collective-permute-done((bf16[4,128,768]{2,1,0:T(8,128)(2,1)}, bf16[4,128,768]{2,1,0:T(8,128)(2,1)S(1)}, u32[]{:S(2)}, u32[]{:S(2)}) %collective-permute-start.34) | collective-permute-done | bytes 786464 | tf_op jit(solution)/shard_map/ppermute | solution.py:302
  422.0 6.6 %attend.5 = bf16[16,64,1024]{2,1,0:T(8,128)(2,1)S(1)} custom-call(bf16[16,64,768]{2,1,0:T(8,128)(2,1)} %bitcast.14.qkv_ref, bf16[16,64,1024]{2,1,0:T(8,128)(2,1)} %bitcast.12.grad_ref), custom_call_target="tpu_custom_call" | custom-call | flops 1610612736 | bytes 4194304 | tf_op jit(solution)/shard_map/attend/pallas_call | solution.py:125
  429.9 12.1 %all-to-all-done.7 = bf16[4,4,64,768]{3,2,1,0:T(8,128)(2,1)S(1)} async-done(((bf16[4,4,64,768]{3,2,1,0:T(8,128)(2,1)}), bf16[4,4,64,768]{3,2,1,0:T(8,128)(2,1)S(1)}, u32[]{:S(2)}, u32[]{:S(2)}) %all-to-all-start.7) | async-done | bytes 1572896 | tf_op jit(solution)/shard_map/all_to_all | solution.py:325
  446.7 6.6 %attend.6 = bf16[16,64,1024]{2,1,0:T(8,128)(2,1)S(1)} custom-call(bf16[16,64,768]{2,1,0:T(8,128)(2,1)} %bitcast.16.qkv_ref, bf16[16,64,1024]{2,1,0:T(8,128)(2,1)} %bitcast.12.grad_ref), custom_call_target="tpu_custom_call" | custom-call | flops 1610612736 | bytes 4194304 | tf_op jit(solution)/shard_map/attend/pallas_call | solution.py:125
  454.7 17.8 %all-to-all-done.4.refs_1_.back_ref = bf16[4,4,64,1024]{3,2,1,0:T(8,128)(2,1)S(1)} async-done(((bf16[4,4,64,1024]{3,2,1,0:T(8,128)(2,1)}), bf16[4,4,64,1024]{3,2,1,0:T(8,128)(2,1)S(1)}, u32[]{:S(2)}, u32[]{:S(2)}) %all-to-all-start.4) | async-done | bytes 2097184 | tf_op jit(solution)/shard_map/all_to_all | solution.py:325
  486.1 16.5 %all-to-all-done.6.refs_2_.back_ref = bf16[4,4,64,1024]{3,2,1,0:T(8,128)(2,1)} async-done(((bf16[4,4,64,1024]{3,2,1,0:T(8,128)(2,1)}), bf16[4,4,64,1024]{3,2,1,0:T(8,128)(2,1)}, u32[]{:S(2)}, u32[]{:S(2)}) %all-to-all-start.6) | async-done | bytes 2097184 | tf_op jit(solution)/shard_map/all_to_all | solution.py:325
  538.0 7.1 %backward.7 = bf16[4,256,1024]{2,1,0:T(8,128)(2,1)S(1)} custom-call(s32[8]{0:T(128)S(1)} %stack.35.source_ref, bf16[4,4,64,1024]{3,2,1,0:T(8,128)(2,1)} %all-to-all-done.8.refs_3_.back_ref, f32[4,256,1024]{2,1,0:T(8,128)} %copy-done.5, bf16[4,256,1024]{2,1,0:T(8,128)(2,1)S(1)} %bitcast.30, bf16[4,256,1024]{2,1,0:T(8,128)(2,1)} %bitcast.29, ...), custom_call_target="tpu_custom_call" | custom-call | flops 1610612736 | bytes 16777216 | tf_op jit(solution)/shard_map/backward/pallas_call | solution.py:190
  (241 shorter events, 221.0 us)
Async XLA Ops:
  7.4 39.5 %collective-permute-start = (bf16[4,128,768]{2,1,0:T(8,128)(2,1)S(1)}, bf16[4,128,768]{2,1,0:T(8,128)(2,1)S(1)}, u32[]{:S(2)}, u32[]{:S(2)}) collective-permute-start(bf16[4,128,768]{2,1,0:T(8,128)(2,1)S(1)} %pad_maximum_fusion.refs_0_), channel_id=1, source_target_pairs={{0,1},{1,0},{2,3},{3,2},{4,5},{5,4},{6,7},{7,6},{8,9},{9,8},{10,11... | collective-permute-start | bytes 2359304 | tf_op jit(solution)/shard_map/ppermute | solution.py:308
  7.9 39.8 %collective-permute-start.1 = (bf16[4,128,768]{2,1,0:T(8,128)(2,1)S(1)}, bf16[4,128,768]{2,1,0:T(8,128)(2,1)S(1)}, u32[]{:S(2)}, u32[]{:S(2)}) collective-permute-start(bf16[4,128,768]{2,1,0:T(8,128)(2,1)S(1)} %pad_maximum_fusion.refs_0_), channel_id=1, source_target_pairs={{0,2},{1,3},{2,4},{3,5},{4,6},{5,7},{6,0},{7,1},{8,10},{9,11},{10,... | collective-permute-start | bytes 2359304 | tf_op jit(solution)/shard_map/ppermute | solution.py:302
  30.0 39.3 %collective-permute-start.6 = (bf16[4,128,1024]{2,1,0:T(8,128)(2,1)S(1)}, bf16[4,128,1024]{2,1,0:T(8,128)(2,1)S(1)}, u32[]{:S(2)}, u32[]{:S(2)}) collective-permute-start(bf16[4,128,1024]{2,1,0:T(8,128)(2,1)S(1)} %collective-permute-done.4.refs_2_.refs_6_), channel_id=1, source_target_pairs={{0,2},{1,3},{2,4},{3,5},{4,6},{5,7},{6,0},{7,1},{8,10},{9,11},{10,... | collective-permute-start | bytes 3145736 | tf_op jit(solution)/shard_map/ppermute | solution.py:302
  31.6 37.7 %collective-permute-start.7 = (bf16[4,128,1024]{2,1,0:T(8,128)(2,1)S(1)}, bf16[4,128,1024]{2,1,0:T(8,128)(2,1)S(1)}, u32[]{:S(2)}, u32[]{:S(2)}) collective-permute-start(bf16[4,128,1024]{2,1,0:T(8,128)(2,1)S(1)} %collective-permute-done.4.refs_2_.refs_6_), channel_id=1, source_target_pairs={{0,1},{1,0},{2,3},{3,2},{4,5},{5,4},{6,7},{7,6},{8,9},{9,8},{10,11... | collective-permute-start | bytes 3145736 | tf_op jit(solution)/shard_map/ppermute | solution.py:308
  47.8 38.4 %collective-permute-start.3 = (bf16[4,128,768]{2,1,0:T(8,128)(2,1)S(1)}, bf16[4,128,768]{2,1,0:T(8,128)(2,1)}, u32[]{:S(2)}, u32[]{:S(2)}) collective-permute-start(bf16[4,128,768]{2,1,0:T(8,128)(2,1)S(1)} %collective-permute-done.1.refs_2_), channel_id=1, source_target_pairs={{0,2},{1,3},{2,4},{3,5},{4,6},{5,7},{6,0},{7,1},{8,10},{9,11},{10,... | collective-permute-start | bytes 2359304 | tf_op jit(solution)/shard_map/ppermute | solution.py:302
  49.3 36.9 %collective-permute-start.2 = (bf16[4,128,768]{2,1,0:T(8,128)(2,1)S(1)}, bf16[4,128,768]{2,1,0:T(8,128)(2,1)S(1)}, u32[]{:S(2)}, u32[]{:S(2)}) collective-permute-start(bf16[4,128,768]{2,1,0:T(8,128)(2,1)S(1)} %collective-permute-done.1.refs_2_), channel_id=1, source_target_pairs={{0,1},{1,0},{2,3},{3,2},{4,5},{5,4},{6,7},{7,6},{8,9},{9,8},{10,11... | collective-permute-start | bytes 2359304 | tf_op jit(solution)/shard_map/ppermute | solution.py:308
  70.4 38.3 %collective-permute-start.8 = (bf16[4,128,1024]{2,1,0:T(8,128)(2,1)S(1)}, bf16[4,128,1024]{2,1,0:T(8,128)(2,1)}, u32[]{:S(2)}, u32[]{:S(2)}) collective-permute-start(bf16[4,128,1024]{2,1,0:T(8,128)(2,1)S(1)} %collective-permute-done.6.refs_4_.refs_8_), channel_id=1, source_target_pairs={{0,2},{1,3},{2,4},{3,5},{4,6},{5,7},{6,0},{7,1},{8,10},{9,11},{10,... | collective-permute-start | bytes 3145736 | tf_op jit(solution)/shard_map/ppermute | solution.py:302
  71.9 36.8 %collective-permute-start.9 = (bf16[4,128,1024]{2,1,0:T(8,128)(2,1)S(1)}, bf16[4,128,1024]{2,1,0:T(8,128)(2,1)S(1)}, u32[]{:S(2)}, u32[]{:S(2)}) collective-permute-start(bf16[4,128,1024]{2,1,0:T(8,128)(2,1)S(1)} %collective-permute-done.6.refs_4_.refs_8_), channel_id=1, source_target_pairs={{0,1},{1,0},{2,3},{3,2},{4,5},{5,4},{6,7},{7,6},{8,9},{9,8},{10,11... | collective-permute-start | bytes 3145736 | tf_op jit(solution)/shard_map/ppermute | solution.py:308
  87.1 38.4 %collective-permute-start.13 = (bf16[4,128,768]{2,1,0:T(8,128)(2,1)S(1)}, bf16[4,128,768]{2,1,0:T(8,128)(2,1)}, u32[]{:S(2)}, u32[]{:S(2)}) collective-permute-start(bf16[4,128,768]{2,1,0:T(8,128)(2,1)S(1)} %pad_maximum_fusion.2.refs_0_.refs_1_), channel_id=1, source_target_pairs={{0,2},{1,3},{2,4},{3,5},{4,6},{5,7},{6,0},{7,1},{8,10},{9,11},{10,... | collective-permute-start | bytes 2359304 | tf_op jit(solution)/shard_map/ppermute | solution.py:302
  88.6 36.9 %collective-permute-start.14 = (bf16[4,128,768]{2,1,0:T(8,128)(2,1)S(1)}, bf16[4,128,768]{2,1,0:T(8,128)(2,1)S(1)}, u32[]{:S(2)}, u32[]{:S(2)}) collective-permute-start(bf16[4,128,768]{2,1,0:T(8,128)(2,1)S(1)} %pad_maximum_fusion.2.refs_0_.refs_1_), channel_id=1, source_target_pairs={{0,1},{1,0},{2,3},{3,2},{4,5},{5,4},{6,7},{7,6},{8,9},{9,8},{10,11... | collective-permute-start | bytes 2359304 | tf_op jit(solution)/shard_map/ppermute | solution.py:308
  109.7 32.6 %collective-permute-start.10 = (bf16[4,128,768]{2,1,0:T(8,128)(2,1)}, bf16[4,128,768]{2,1,0:T(8,128)(2,1)S(1)}, u32[]{:S(2)}, u32[]{:S(2)}) collective-permute-start(bf16[4,128,768]{2,1,0:T(8,128)(2,1)} %collective-permute-done.3.refs_4_), channel_id=1, source_target_pairs={{0,2},{1,3},{2,4},{3,5},{4,6},{5,7},{6,0},{7,1},{8,10},{9,11},{10,... | collective-permute-start | bytes 2359304 | tf_op jit(solution)/shard_map/ppermute | solution.py:302
  125.5 39.4 %collective-permute-start.16 = (bf16[4,128,1024]{2,1,0:T(8,128)(2,1)}, bf16[4,128,1024]{2,1,0:T(8,128)(2,1)}, u32[]{:S(2)}, u32[]{:S(2)}) collective-permute-start(bf16[4,128,1024]{2,1,0:T(8,128)(2,1)} %collective-permute-done.8.refs_6_.refs_10_), channel_id=1, source_target_pairs={{0,1},{1,0},{2,3},{3,2},{4,5},{5,4},{6,7},{7,6},{8,9},{9,8},{10,11... | collective-permute-start | bytes 3145736 | tf_op jit(solution)/shard_map/ppermute | solution.py:308
  142.5 43.6 %collective-permute-start.12 = (bf16[4,128,768]{2,1,0:T(8,128)(2,1)}, bf16[4,128,768]{2,1,0:T(8,128)(2,1)}, u32[]{:S(2)}, u32[]{:S(2)}) collective-permute-start(bf16[4,128,768]{2,1,0:T(8,128)(2,1)} %collective-permute-done.3.refs_4_), channel_id=1, source_target_pairs={{0,1},{1,0},{2,3},{3,2},{4,5},{5,4},{6,7},{7,6},{8,9},{9,8},{10,11... | collective-permute-start | bytes 2359304 | tf_op jit(solution)/shard_map/ppermute | solution.py:308
  144.1 42.0 %collective-permute-start.20 = (bf16[4,128,768]{2,1,0:T(8,128)(2,1)}, bf16[4,128,768]{2,1,0:T(8,128)(2,1)}, u32[]{:S(2)}, u32[]{:S(2)}) collective-permute-start(bf16[4,128,768]{2,1,0:T(8,128)(2,1)} %pad_maximum_fusion.3.refs_0_.refs_1_), channel_id=1, source_target_pairs={{0,2},{1,3},{2,4},{3,5},{4,6},{5,7},{6,0},{7,1},{8,10},{9,11},{10,... | collective-permute-start | bytes 2359304 | tf_op jit(solution)/shard_map/ppermute | solution.py:302
  164.9 33.7 %collective-permute-start.18 = (bf16[4,128,768]{2,1,0:T(8,128)(2,1)}, bf16[4,128,768]{2,1,0:T(8,128)(2,1)}, u32[]{:S(2)}, u32[]{:S(2)}) collective-permute-start(bf16[4,128,768]{2,1,0:T(8,128)(2,1)} %collective-permute-done.13.refs_2_.refs_3_), channel_id=1, source_target_pairs={{0,1},{1,0},{2,3},{3,2},{4,5},{5,4},{6,7},{7,6},{8,9},{9,8},{10,11... | collective-permute-start | bytes 2359304 | tf_op jit(solution)/shard_map/ppermute | solution.py:308
  166.5 32.2 %collective-permute-start.17 = (bf16[4,128,768]{2,1,0:T(8,128)(2,1)}, bf16[4,128,768]{2,1,0:T(8,128)(2,1)}, u32[]{:S(2)}, u32[]{:S(2)}) collective-permute-start(bf16[4,128,768]{2,1,0:T(8,128)(2,1)} %collective-permute-done.15.refs_4_.refs_5_), channel_id=1, source_target_pairs={{0,2},{1,3},{2,4},{3,5},{4,6},{5,7},{6,0},{7,1},{8,10},{9,11},{10,... | collective-permute-start | bytes 2359304 | tf_op jit(solution)/shard_map/ppermute | solution.py:302
  181.6 57.1 %all-to-all-start.1 = ((bf16[4,4,64,1024]{3,2,1,0:T(8,128)(2,1)}), bf16[4,4,64,1024]{3,2,1,0:T(8,128)(2,1)}, u32[]{:S(2)}, u32[]{:S(2)}) async-start(bf16[4,4,64,1024]{3,2,1,0:T(8,128)(2,1)} %copy-done.6), calls=%async_computation.1 | async-start | bytes 4194304 | tf_op jit(solution)/shard_map/all_to_all | solution.py:325
  198.6 33.6 %collective-permute-start.19 = (bf16[4,128,768]{2,1,0:T(8,128)(2,1)}, bf16[4,128,768]{2,1,0:T(8,128)(2,1)S(1)}, u32[]{:S(2)}, u32[]{:S(2)}) collective-permute-start(bf16[4,128,768]{2,1,0:T(8,128)(2,1)} %copy-done.62), channel_id=1, source_target_pairs={{0,1},{1,0},{2,3},{3,2},{4,5},{5,4},{6,7},{7,6},{8,9},{9,8},{10,11... | collective-permute-start | bytes 2359304 | tf_op jit(solution)/shard_map/ppermute | solution.py:308
  238.7 36.4 %all-to-all-start = ((bf16[4,4,64,768]{3,2,1,0:T(8,128)(2,1)}), bf16[4,4,64,768]{3,2,1,0:T(8,128)(2,1)}, u32[]{:S(2)}, u32[]{:S(2)}) async-start(bf16[4,4,64,768]{3,2,1,0:T(8,128)(2,1)} %copy-done.15), calls=%async_computation | async-start | bytes 3145728 | tf_op jit(solution)/shard_map/all_to_all | solution.py:325
  275.1 37.0 %all-to-all-start.3 = ((bf16[4,4,64,768]{3,2,1,0:T(8,128)(2,1)}), bf16[4,4,64,768]{3,2,1,0:T(8,128)(2,1)}, u32[]{:S(2)}, u32[]{:S(2)}) async-start(bf16[4,4,64,768]{3,2,1,0:T(8,128)(2,1)} %copy-done.13), calls=%async_computation.3 | async-start | bytes 3145728 | tf_op jit(solution)/shard_map/all_to_all | solution.py:325
  302.8 36.5 %collective-permute-start.30 = (bf16[4,128,768]{2,1,0:T(8,128)(2,1)}, bf16[4,128,768]{2,1,0:T(8,128)(2,1)}, u32[]{:S(2)}, u32[]{:S(2)}) collective-permute-start(bf16[4,128,768]{2,1,0:T(8,128)(2,1)} %collective-permute-done.26.refs_2_.refs_6_), channel_id=1, source_target_pairs={{0,2},{1,3},{2,4},{3,5},{4,6},{5,7},{6,0},{7,1},{8,10},{9,11},{10,... | collective-permute-start | bytes 2359304 | tf_op jit(solution)/shard_map/ppermute | solution.py:302
  312.0 55.5 %all-to-all-start.2 = ((bf16[4,4,64,1024]{3,2,1,0:T(8,128)(2,1)}), bf16[4,4,64,1024]{3,2,1,0:T(8,128)(2,1)}, u32[]{:S(2)}, u32[]{:S(2)}) async-start(bf16[4,4,64,1024]{3,2,1,0:T(8,128)(2,1)} %bitcast.35), calls=%async_computation.2 | async-start | bytes 4194304 | tf_op jit(solution)/shard_map/all_to_all | solution.py:325
  367.5 50.8 %all-to-all-start.5 = ((bf16[4,4,64,768]{3,2,1,0:T(8,128)(2,1)}), bf16[4,4,64,768]{3,2,1,0:T(8,128)(2,1)}, u32[]{:S(2)}, u32[]{:S(2)}) async-start(bf16[4,4,64,768]{3,2,1,0:T(8,128)(2,1)} %copy-done.14), calls=%async_computation.5 | async-start | bytes 3145728 | tf_op jit(solution)/shard_map/all_to_all | solution.py:325
  372.0 38.7 %collective-permute-start.34 = (bf16[4,128,768]{2,1,0:T(8,128)(2,1)}, bf16[4,128,768]{2,1,0:T(8,128)(2,1)S(1)}, u32[]{:S(2)}, u32[]{:S(2)}) collective-permute-start(bf16[4,128,768]{2,1,0:T(8,128)(2,1)} %collective-permute-done.32.refs_5_.refs_9_), channel_id=1, source_target_pairs={{0,2},{1,3},{2,4},{3,5},{4,6},{5,7},{6,0},{7,1},{8,10},{9,11},{10,... | collective-permute-start | bytes 2359304 | tf_op jit(solution)/shard_map/ppermute | solution.py:302
  (95 other events, 1207.1 us)

commit v3 on v1

v3 whole, which is shorter than its diff:
```python
import functools

import jax
import jax.numpy as jnp
from jax import lax
from jax.experimental import pallas as pl
from jax.experimental.pallas import tpu as pltpu
from jax.sharding import PartitionSpec as P

HEADS = 16
GROUP_HEADS = (4, 4, 4, 4)
KERNEL_STEPS = 1
EXCHANGE_STEPS = 2
CROSS_FIRST = 3
CROSS_EARLY = 1.5
ORDER = (0, 1, 2, 3, 4)
VMEM_LIMIT = 60 * 1024 * 1024
EPSILON = 1e-05
F32 = jnp.float32
BF16 = jnp.bfloat16
FRAME_BLOCK = 16
HALF = 8


def params():
    return pltpu.CompilerParams(
        dimension_semantics=("arbitrary",), vmem_limit_bytes=VMEM_LIMIT
    )


def cost(flops, byte_count):
    return pl.CostEstimate(flops=flops, bytes_accessed=byte_count, transcendentals=0)


def fill(layout, source_ref, refs, whole_ref):
    refs = list(refs)
    for way, first, count in layout:
        depth, width = refs[0].shape[1:]
        for slot in range(count):
            start = pl.multiple_of(source_ref[way, slot] * depth, depth)
            whole_ref[pl.ds(start, depth), first : first + width] = refs.pop(0)[0]


def layout_of(pieces):
    layout, slots, first = [], [], 0
    for way, shards in pieces:
        layout.append((way, first, len(shards)))
        slots += shards
        first += shards[0].shape[2]
    depth = sum(shard.shape[1] for shard in pieces[0][1])
    specs = [pl.BlockSpec((1,) + shard.shape[1:], lambda c: (c, 0, 0)) for shard in slots]
    return tuple(layout), slots, specs, (depth, first)


def project_kernel(layout, back, source_ref, rows_ref, *refs):
    out_ref, whole_ref = refs[-2:]
    fill(layout, source_ref, refs[:-2], whole_ref)
    contract = ((1,), (1,)) if back else ((1,), (0,))
    result = lax.dot_general(
        rows_ref[0], whole_ref[...], (contract, ((), ())), preferred_element_type=F32
    )
    out_ref[...] = result.astype(BF16).reshape(out_ref.shape)


def project(source, rows, pieces, parts, back):
    codebooks, frames, columns = rows.shape
    layout, slots, specs, (depth, width) = layout_of(pieces)
    out_columns = depth if back else width
    share = frames // parts
    return pl.pallas_call(
        functools.partial(project_kernel, layout, back),
        grid=(codebooks,),
        in_specs=[
            pl.BlockSpec(memory_space=pltpu.SMEM),
            pl.BlockSpec((1, frames, columns), lambda c: (c, 0, 0)),
        ]
        + specs,
        out_specs=pl.BlockSpec((parts, 1, share, out_columns), lambda c: (0, c, 0, 0)),
        out_shape=jax.ShapeDtypeStruct((parts, codebooks, share, out_columns), BF16),
        scratch_shapes=[pltpu.VMEM((depth, width), BF16)],
        compiler_params=params(),
        cost_estimate=cost(
            2 * codebooks * frames * depth * width, 2 * codebooks * depth * (width + frames)
        ),
        name="project_back" if back else "project",
    )(source, rows, *slots)


def attend_kernel(heads, qkv_ref, grad_ref, *out_refs):
    codebooks, _, width = grad_ref.shape
    head_width = width // heads
    rows = codebooks * HALF
    factor = head_width ** (-0.5)
    row = lax.broadcasted_iota(jnp.int32, (rows, rows), 0)
    column = lax.broadcasted_iota(jnp.int32, (rows, rows), 1)
    allowed = jnp.logical_and(row % HALF == column % HALF, row >= column)[None]
    lane_head = lax.broadcasted_iota(jnp.int32, (rows, width), 1) // head_width

    def wide(ref, first):
        values = ref[:, :, first : first + width].astype(F32)
        return values.reshape(codebooks, FRAME_BLOCK // HALF, HALF, width)

    def stacked(values):
        pieces = [jnp.where(lane_head == h, values, 0.0).astype(BF16) for h in range(heads)]
        return jnp.concatenate(pieces, axis=0)

    def beside(values):
        return jnp.concatenate([values[h * rows : (h + 1) * rows] for h in range(heads)], axis=1)

    def dot(left, right, left_dim, right_dim):
        return lax.dot_general(
            left, right, (((left_dim,), (right_dim,)), ((), ())), preferred_element_type=F32
        )

    parts = [wide(qkv_ref, 0), wide(qkv_ref, width), wide(qkv_ref, 2 * width), wide(grad_ref, 0)]
    results = [[], [], [], []]
    for half in range(FRAME_BLOCK // HALF):
        q, k, v, g = [part[:, half].reshape(rows, width) for part in parts]
        q_heads, k_heads, v_heads, g_heads = stacked(q), stacked(k), stacked(v), stacked(g)
        scores = dot(q_heads, k.astype(BF16), 1, 1).reshape(heads, rows, rows) * factor
        scores = jnp.where(allowed, scores, -jnp.inf)
        weights = jnp.exp(scores - jnp.max(scores, axis=-1, keepdims=True))
        probs = weights / jnp.sum(weights, axis=-1, keepdims=True)
        grad_probs = dot(g_heads, v.astype(BF16), 1, 1).reshape(heads, rows, rows)
        inner = jnp.sum(probs * grad_probs, axis=-1, keepdims=True)
        grad_scores = (probs * (grad_probs - inner) * factor).astype(BF16)
        probs_low = probs.astype(BF16).reshape(heads * rows, rows)
        grad_scores = grad_scores.reshape(heads * rows, rows)
        results[0].append(dot(beside(probs_low), v_heads, 1, 0))
        results[1].append(dot(beside(grad_scores), k_heads, 1, 0))
        results[2].append(dot(grad_scores, q_heads, 0, 0))
        results[3].append(dot(probs_low, g_heads, 0, 0))
    for index, halves in enumerate(results):
        halves = [value.reshape(codebooks, 1, HALF, width) for value in halves]
        whole = jnp.concatenate(halves, axis=1).reshape(codebooks, FRAME_BLOCK, width)
        if len(out_refs) == 2 and index == 0:
            out_refs[0][...] = whole.astype(BF16)
        else:
            start = (index + 1 - len(out_refs)) * width
            out_refs[-1][:, :, start : start + width] = whole.astype(BF16)


def attend(place, heads, split, qkv, grad_context):
    codebooks, frames, columns = qkv.shape
    width = columns // 3
    rows = codebooks * HALF
    counts = (1, 3) if split else (4,)
    return pl.pallas_call(
        functools.partial(attend_kernel, heads),
        grid=(frames // FRAME_BLOCK,),
        in_specs=[
            pl.BlockSpec((codebooks, FRAME_BLOCK, columns), lambda f: (0, f, 0)),
            pl.BlockSpec((codebooks, FRAME_BLOCK, width), lambda f: (0, f, place)),
        ],
        out_specs=[
            pl.BlockSpec((codebooks, FRAME_BLOCK, n * width), lambda f: (0, f, 0)) for n in counts
        ],
        out_shape=[
            jax.ShapeDtypeStruct((codebooks, frames, n * width), BF16) for n in counts
        ],
        compiler_params=params(),
        cost_estimate=cost(
            12 * heads * rows * rows * width * (frames // HALF),
            2 * codebooks * frames * width * 8,
        ),
        name="attend",
    )(qkv, grad_context)


def backward_kernel(layout, first, last, source_ref, back_ref, *refs):
    refs = list(refs)
    whole_ref = refs.pop()
    out_ref = refs.pop()
    total_ref = None if first else refs.pop(0)
    if last:
        rows_ref, grad_ref, gain_ref = refs.pop(0), refs.pop(0), refs.pop(0)
    fill(layout, source_ref, refs, whole_ref)
    frames = out_ref.shape[1]
    width = whole_ref.shape[1]
    grad = back_ref[...].reshape(frames, back_ref.shape[3])[:, -width:]
    total = lax.dot_general(
        grad, whole_ref[...], (((1,), (1,)), ((), ())), preferred_element_type=F32
    )
    if not first:
        total = total + total_ref[0]
    if last:
        rows = rows_ref[0].astype(F32)
        inverse_rms = lax.rsqrt(jnp.mean(rows * rows, axis=-1, keepdims=True) + EPSILON)
        scaled = total * gain_ref[...]
        inner = jnp.mean(scaled * rows, axis=-1, keepdims=True)
        total = grad_ref[0].astype(F32) + inverse_rms * (
            scaled - rows * (inverse_rms * inverse_rms * inner)
        )
    out_ref[0] = total.astype(out_ref.dtype)


def backward(source, returned, pieces, total, epilogue):
    parts, codebooks, share, columns = returned.shape
    frames = parts * share
    layout, slots, slot_specs, (depth, width) = layout_of(pieces)
    row_spec = pl.BlockSpec((1, frames, depth), lambda c: (c, 0, 0))
    operands = [source, returned]
    specs = [
        pl.BlockSpec(memory_space=pltpu.SMEM),
        pl.BlockSpec((parts, 1, share, columns), lambda c: (0, c, 0, 0)),
    ]
    if total is not None:
        operands.append(total)
        specs.append(row_spec)
    if epilogue is not None:
        rows, grad_out, gain = epilogue
        operands += [rows, grad_out, gain.reshape(1, depth)]
        specs += [row_spec, row_spec, pl.BlockSpec((1, depth), lambda c: (0, 0))]
    return pl.pallas_call(
        functools.partial(backward_kernel, layout, total is None, epilogue is not None),
        grid=(codebooks,),
        in_specs=specs + slot_specs,
        out_specs=row_spec,
        out_shape=jax.ShapeDtypeStruct(
            (codebooks, frames, depth), F32 if epilogue is None else BF16
        ),
        scratch_shapes=[pltpu.VMEM((depth, width), BF16)],
        compiler_params=params(),
        cost_estimate=cost(
            2 * codebooks * frames * depth * width, 2 * codebooks * depth * (width + 5 * frames)
        ),
        name="backward",
    )(*operands, *slots)


def output_kernel(layout, groups, source_ref, rows_ref, *refs):
    refs = list(refs)
    whole_ref = refs.pop()
    out_ref = refs.pop()
    fill(layout, source_ref, refs[groups:], whole_ref)
    frames = out_ref.shape[1]
    pieces = [ref[...].reshape(frames, ref.shape[3]) for ref in refs[:groups]]
    result = jnp.dot(
        jnp.concatenate(pieces, axis=1), whole_ref[...], preferred_element_type=F32
    )
    out_ref[0] = (rows_ref[0].astype(F32) + result).astype(BF16)


def output(source, rows, returned, widths, pieces):
    codebooks, frames, columns = rows.shape
    parts, _, share, _ = returned[0].shape
    layout, slots, specs, size = layout_of(pieces)
    row_spec = pl.BlockSpec((1, frames, columns), lambda c: (c, 0, 0))
    return pl.pallas_call(
        functools.partial(output_kernel, layout, len(returned)),
        grid=(codebooks,),
        in_specs=[pl.BlockSpec(memory_space=pltpu.SMEM), row_spec]
        + [pl.BlockSpec((parts, 1, share, wide), lambda c: (0, c, 0, 0)) for wide in widths]
        + specs,
        out_specs=row_spec,
        out_shape=jax.ShapeDtypeStruct(rows.shape, BF16),
        scratch_shapes=[pltpu.VMEM(size, BF16)],
        compiler_params=params(),
        cost_estimate=cost(
            2 * codebooks * frames * columns * columns, 2 * codebooks * columns * (columns + 3 * frames)
        ),
        name="output",
    )(source, rows, *returned, *slots)


def tie(values, after):
    return lax.optimization_barrier((values,) + tuple(after))[0] if after else values


def body(lines, columns_wide, inputs, norm_gain, w_qkv, w_out, grad_out):
    frames, codebooks, columns = inputs.shape
    parts = lax.axis_size("cb")
    count = lines * columns_wide

    place = lax.axis_index("frame")
    line, column = lax.div(place, columns_wide), lax.rem(place, columns_wide)
    along = [(i, (i + columns_wide) % count) for i in range(count)]

    def turn(step):
        return [
            (i, i // columns_wide * columns_wide + (i + step) % columns_wide) for i in range(count)
        ]

    back = jnp.arange(count, dtype=jnp.int32)
    back_line, back_column = back // columns_wide, back % columns_wide
    source = lax.rem(line - back_line + lines, lines) * columns_wide + lax.rem(
        column - back_column + columns_wide, columns_wide
    )
    source = source.astype(jnp.int32)[None]

    head_width = columns // HEADS
    widths = [heads * head_width for heads in GROUP_HEADS]
    starts = [sum(widths[:g]) for g in range(len(widths))]
    final = len(widths) - 1

    def packed(g):
        pieces = [
            w_qkv[:, :, kind * columns + starts[g] : kind * columns + starts[g] + widths[g]]
            for kind in range(3)
        ]
        return jnp.concatenate(pieces, axis=-1)

    shards = [w_out] + [packed(g) for g in range(len(widths))]
    line_steps, cross_steps = [], []
    for w in ORDER:
        first = w == CROSS_FIRST
        for k in range(1, lines):
            line_steps += [(w, k, m) for m in range(columns_wide if first else 1)]
        for m in range(1, columns_wide):
            cross_steps += [(w, k, m) for k in range(1 if first else lines)]
    cross_steps.sort(key=lambda step: ORDER.index(step[0]) - CROSS_EARLY * (step[0] == CROSS_FIRST))
    held = {(w, 0, 0): shard for w, shard in enumerate(shards)}

    wide_in = inputs.astype(F32)
    inverse_rms = lax.rsqrt(jnp.mean(wide_in * wide_in, axis=-1, keepdims=True) + EPSILON)
    normed = (wide_in * inverse_rms * norm_gain).astype(BF16).transpose(1, 0, 2)
    rows = inputs.transpose(1, 0, 2)
    grad_rows = grad_out.transpose(1, 0, 2)
    due = {1: [normed, rows, grad_rows] + shards}
    latest = []

    def join(window, *values):
        due.setdefault(window, []).extend(values)

    def carry():
        after = latest[-1] + due.get(len(latest), []) if latest else []
        landed = []
        for steps, along_line in ((line_steps, True), (cross_steps, False)):
            for step in steps:
                w, k, m = step
                origin = (w, k - 1, m) if along_line else (w, k, 0)
                if origin in held:
                    steps.remove(step)
                    pairs = along if along_line else turn(m)
                    landed.append((step, lax.ppermute(tie(held[origin], after), "frame", pairs)))
                    break
        held.update(landed)
        latest.append([value for _, value in landed])

    def arrived(w):
        return all((w, k, m) in held for k in range(lines) for m in range(columns_wide))

    def weight(w):
        return [(0, [held[(w, k, m)] for k in range(lines) for m in range(columns_wide)])]

    def group(g):
        return weight(1 + g)

    def exchange(values):
        return lax.all_to_all(values, "cb", split_axis=0, concat_axis=0, tiled=True)

    def joined(values):
        return values.reshape((values.shape[0] * values.shape[1],) + values.shape[2:])

    state = {"total": None}
    contexts = []

    def forward(g, step):
        made = project(source, tie(normed, latest[-1]), group(g), parts, False)
        state[g] = joined(exchange(made))
        join(step + KERNEL_STEPS, made)

    def mix(g, step):
        split = g == final
        place, heads = starts[g] // widths[g], GROUP_HEADS[g]
        mixed = attend(place, heads, split, tie(state[g], latest[-1]), state["grad"])
        back = [exchange(m.reshape((parts, codebooks) + m.shape[1:])) for m in mixed]
        join(step + KERNEL_STEPS, *mixed)
        state[g] = back[-1]
        contexts.append(back[0])

    def reverse(g, step):
        epilogue = (rows, grad_rows, norm_gain) if g == final else None
        back = tie(state[g], latest[-1])
        state["total"] = backward(source, back, group(g), state["total"], epilogue)
        join(step + KERNEL_STEPS, state["total"])

    def start(step):
        grad = tie(grad_rows, latest[-1])
        made = project(source, grad, weight(0), parts, True)
        state["grad"] = joined(exchange(made))
        join(step + KERNEL_STEPS, made)
        join(step + EXCHANGE_STEPS, state["grad"])

    waiting, tasks = list(range(len(shards))), []
    while line_steps or cross_steps or waiting or tasks:
        now = len(latest)
        for w in [w for w in waiting if arrived(w)]:
            waiting.remove(w)
            tasks.append((now, 0, start, ()) if w == 0 else (now, w, forward, (w - 1,)))
        ready = sorted(task for task in tasks if task[0] <= now)
        for task in ready[: 1 if line_steps or cross_steps else len(ready)]:
            tasks.remove(task)
            _, _, run, operands = task
            if run is mix and "grad" not in state:
                tasks.append((now + 1,) + task[1:])
                continue
            run(*operands, now)
            if run is forward:
                tasks.append((now + EXCHANGE_STEPS, 10 + operands[0], mix, operands))
            elif run is mix and operands[0] < final:
                tasks.append((now + EXCHANGE_STEPS + 1, 20 + operands[0], reverse, operands))
        carry()
    outputs = output(source, rows, contexts, widths, weight(0))
    reverse(final, len(latest))
    return outputs.transpose(1, 0, 2), state["total"].transpose(1, 0, 2)


def solution(mesh):
    count = mesh.shape["frame"]
    columns_wide = 2 if count % 2 == 0 else 1
    return jax.shard_map(
        functools.partial(body, count // columns_wide, columns_wide),
        mesh=mesh,
        in_specs=(
            P("frame", "cb", None),
            P(),
            P("cb", "frame", None),
            P("cb", "frame", None),
            P("frame", "cb", None),
        ),
        out_specs=(P("frame", "cb", None), P("frame", "cb", None)),
        check_vma=False,
    )
```

time: 643 us -> 501 us (0.78)
  starting transfers between devices: 177 us -> 60.5 us
  blocking collectives: 0 us -> 37.5 us
  local copies, waits for them, and re-layouts: 56.6 us -> 20.7 us
  Pallas kernels: 76 us -> 102 us
  waiting for transfers between devices: 298 us -> 272 us
  other arithmetic: 29 us -> 6.49 us
    ppermute x53 -> x35, starting transfers between devices: 138 us -> 27.4 us  [carry(): lax.ppermute(tie(held[origin], after), 'frame', pairs)]
    unnamed x156 -> x46, local copies, waits for them, and re-layouts: 53.2 us -> 15.2 us
    all_to_all x0 -> x2, blocking collectives: none -> 37.5 us  [exchange(): return lax.all_to_all(values, 'cb', split_axis=0, concat_axis=0, tiled=True)]
    ppermute x53 -> x35, waiting for transfers between devices: 268 us -> 242 us  [carry(): lax.ppermute(tie(held[origin], after), 'frame', pairs)]
    pallas_call x10, Pallas kernels: 49.7 us -> 72.4 us  [the longest x5 33 us: project(): pl.pallas_call(functools.partial(project_kernel, layout, back), grid=(cod...]
    select_n x18 -> x0, other arithmetic: 20.9 us -> none  [along_line(): jnp.where(line_place >= k, to_right[k], to_left[lines - k])]
    all_to_all x9 -> x8, starting transfers between devices: 39.3 us -> 33.1 us  [exchange(): return lax.all_to_all(values, 'cb', split_axis=0, concat_axis=0, tiled=True)]
    all_to_all x9 -> x8, waiting for transfers between devices: 29.9 us -> 30 us  [exchange(): return lax.all_to_all(values, 'cb', split_axis=0, concat_axis=0, tiled=True)]
  transfers between devices with their start and end apart: 62 -> 43, of which waited for: 28 -> 24; matrix products, arithmetic and copies ran while one was open for 6% -> 3% of each run, Pallas kernels for 10% -> 19%
where the time goes in v3:
time: 501 us; the launch traced here: 500 us
  waiting for transfers between devices  272 us (54%)
  Pallas kernels  102 us (20%)
  starting transfers between devices  60.5 us (12%)
  blocking collectives  37.5 us (7%)
  local copies, waits for them, and re-layouts  20.7 us (4%)
  other arithmetic  6.49 us (1%)
    ppermute x35, waiting for transfers between devices, carry(): lax.ppermute(tie(held[origin], after), 'frame', pairs)  242 us
    all_to_all x2, blocking collectives, exchange(): return lax.all_to_all(values, 'cb', split_axis=0, concat_axis=0, tiled=True)  37.5 us
    all_to_all x8, starting transfers between devices, exchange(): return lax.all_to_all(values, 'cb', split_axis=0, concat_axis=0, tiled=True)  33.1 us
    pallas_call x5, Pallas kernels, project(): pl.pallas_call(functools.partial(project_kernel, layout, back), grid=(cod...  33 us
    pallas_call x4, Pallas kernels, backward(): pl.pallas_call(functools.partial(backward_kernel, layout, total is None,...  31.7 us
    all_to_all x8, waiting for transfers between devices, exchange(): return lax.all_to_all(values, 'cb', split_axis=0, concat_axis=0, tiled=True)  30 us
    pallas_call x4, Pallas kernels, attend(): pl.pallas_call(functools.partial(attend_kernel, heads), grid=(frames // F...  29.2 us
    ppermute x35, starting transfers between devices, carry(): lax.ppermute(tie(held[origin], after), 'frame', pairs)  27.4 us
  transfers between devices with their start and end apart: 43, of which 24 were waited for; matrix products, arithmetic and copies ran while one was open for 3% of the time, Pallas kernels for 19%

profile of v3, /device:TPU:0, one launch (start us, length us, event | category | flops | bytes accessed | tf_op | source)
XLA Modules:
  0.0 499.6 jit_solution(10181733001826421968)
XLA Ops:
  19.1 10.0 %collective-permute-done.refs_2_.refs_6_ = bf16[4,128,1024]{2,1,0:T(8,128)(2,1)S(1)} collective-permute-done((bf16[4,128,1024]{2,1,0:T(8,128)(2,1)}, bf16[4,128,1024]{2,1,0:T(8,128)(2,1)S(1)}, u32[]{:S(2)}, u32[]{:S(2)}) %collective-permute-start) | collective-permute-done | bytes 1048608 | tf_op jit(solution)/shard_map/ppermute | solution.py:335
  31.6 23.7 %collective-permute-done.2.refs_4_.refs_8_ = bf16[4,128,1024]{2,1,0:T(8,128)(2,1)S(1)} collective-permute-done((bf16[4,128,1024]{2,1,0:T(8,128)(2,1)S(1)}, bf16[4,128,1024]{2,1,0:T(8,128)(2,1)S(1)}, u32[]{:S(2)}, u32[]{:S(2)}) %collective-permute-start.2) | collective-permute-done | bytes 1048608 | tf_op jit(solution)/shard_map/ppermute | solution.py:335
  57.6 23.1 %collective-permute-done.4.refs_6_.refs_10_ = bf16[4,128,1024]{2,1,0:T(8,128)(2,1)} collective-permute-done((bf16[4,128,1024]{2,1,0:T(8,128)(2,1)S(1)}, bf16[4,128,1024]{2,1,0:T(8,128)(2,1)}, u32[]{:S(2)}, u32[]{:S(2)}) %collective-permute-start.4) | collective-permute-done | bytes 1048608 | tf_op jit(solution)/shard_map/ppermute | solution.py:335
  82.4 18.3 %collective-permute-done.6.refs_2_ = bf16[4,128,768]{2,1,0:T(8,128)(2,1)} collective-permute-done((bf16[4,128,768]{2,1,0:T(8,128)(2,1)}, bf16[4,128,768]{2,1,0:T(8,128)(2,1)}, u32[]{:S(2)}, u32[]{:S(2)}) %collective-permute-start.6) | collective-permute-done | bytes 786464 | tf_op jit(solution)/shard_map/ppermute | solution.py:335
  105.1 7.3 %project_back.1 = bf16[4,4,64,1024]{3,2,1,0:T(8,128)(2,1)} custom-call(s32[1,8]{1,0:T(1,128)} %fusion.10.source_ref, bf16[4,256,1024]{2,1,0:T(8,128)(2,1)} %get-tuple-element.49.rows_ref.refs_2_, bf16[4,128,1024]{2,1,0:T(8,128)(2,1)} %refs_4_.1, bf16[4,128,1024]{2,1,0:T(8,128)(2,1)} %copy-done.8, bf16[4,128,1024]{2,1,0:T(8,128)(2,1)} %copy-done.7, ...), custom_call_target="tpu_custom_call" | custom-call | flops 2147483648 | bytes 10485760 | tf_op jit(solution)/shard_map/project_back/pallas_call | solution.py:70
  122.2 17.0 %collective-permute-done.10.refs_6_ = bf16[4,128,768]{2,1,0:T(8,128)(2,1)} collective-permute-done((bf16[4,128,768]{2,1,0:T(8,128)(2,1)}, bf16[4,128,768]{2,1,0:T(8,128)(2,1)}, u32[]{:S(2)}, u32[]{:S(2)}) %collective-permute-start.10) | collective-permute-done | bytes 786464 | tf_op jit(solution)/shard_map/ppermute | solution.py:335
  143.7 20.2 %collective-permute-done.12.refs_2_.refs_3_ = bf16[4,128,768]{2,1,0:T(8,128)(2,1)S(1)} collective-permute-done((bf16[4,128,768]{2,1,0:T(8,128)(2,1)S(1)}, bf16[4,128,768]{2,1,0:T(8,128)(2,1)S(1)}, u32[]{:S(2)}, u32[]{:S(2)}) %collective-permute-start.12) | collective-permute-done | bytes 786464 | tf_op jit(solution)/shard_map/ppermute | solution.py:335
  165.0 19.3 %collective-permute-done.14.refs_4_.refs_5_ = bf16[4,128,768]{2,1,0:T(8,128)(2,1)} collective-permute-done((bf16[4,128,768]{2,1,0:T(8,128)(2,1)S(1)}, bf16[4,128,768]{2,1,0:T(8,128)(2,1)}, u32[]{:S(2)}, u32[]{:S(2)}) %collective-permute-start.14) | collective-permute-done | bytes 786464 | tf_op jit(solution)/shard_map/ppermute | solution.py:335
  192.6 11.4 %collective-permute-done.16.refs_6_.refs_7_ = bf16[4,128,768]{2,1,0:T(8,128)(2,1)} collective-permute-done((bf16[4,128,768]{2,1,0:T(8,128)(2,1)}, bf16[4,128,768]{2,1,0:T(8,128)(2,1)}, u32[]{:S(2)}, u32[]{:S(2)}) %collective-permute-start.16) | collective-permute-done | bytes 786464 | tf_op jit(solution)/shard_map/ppermute | solution.py:335
  209.5 13.1 %collective-permute-done.18.refs_2_.refs_3_ = bf16[4,128,768]{2,1,0:T(8,128)(2,1)} collective-permute-done((bf16[4,128,768]{2,1,0:T(8,128)(2,1)S(1)}, bf16[4,128,768]{2,1,0:T(8,128)(2,1)}, u32[]{:S(2)}, u32[]{:S(2)}) %collective-permute-start.18) | collective-permute-done | bytes 786464 | tf_op jit(solution)/shard_map/ppermute | solution.py:335
  241.5 16.9 %collective-permute-done.22.refs_4_.refs_5_ = bf16[4,128,768]{2,1,0:T(8,128)(2,1)} collective-permute-done((bf16[4,128,768]{2,1,0:T(8,128)(2,1)}, bf16[4,128,768]{2,1,0:T(8,128)(2,1)}, u32[]{:S(2)}, u32[]{:S(2)}) %collective-permute-start.22) | collective-permute-done | bytes 786464 | tf_op jit(solution)/shard_map/ppermute | solution.py:335
  263.3 12.4 %collective-permute-done.24.refs_5_.refs_6_ = bf16[4,128,768]{2,1,0:T(8,128)(2,1)} collective-permute-done((bf16[4,128,768]{2,1,0:T(8,128)(2,1)}, bf16[4,128,768]{2,1,0:T(8,128)(2,1)}, u32[]{:S(2)}, u32[]{:S(2)}) %collective-permute-start.24) | collective-permute-done | bytes 786464 | tf_op jit(solution)/shard_map/ppermute | solution.py:335
  285.9 7.6 %collective-permute-done.26.refs_6_.refs_7_ = bf16[4,128,768]{2,1,0:T(8,128)(2,1)} collective-permute-done((bf16[4,128,768]{2,1,0:T(8,128)(2,1)}, bf16[4,128,768]{2,1,0:T(8,128)(2,1)}, u32[]{:S(2)}, u32[]{:S(2)}) %collective-permute-start.26) | collective-permute-done | bytes 786464 | tf_op jit(solution)/shard_map/ppermute | solution.py:335
  328.8 7.3 %attend.5 = bf16[16,64,1024]{2,1,0:T(8,128)(2,1)} custom-call(bf16[16,64,768]{2,1,0:T(8,128)(2,1)} %bitcast.6.qkv_ref, bf16[16,64,1024]{2,1,0:T(8,128)(2,1)} %bitcast.3.grad_ref), custom_call_target="tpu_custom_call" | custom-call | flops 1610612736 | bytes 4194304 | tf_op jit(solution)/shard_map/attend/pallas_call | solution.py:148
  336.1 9.1 %collective-permute-done.30.refs_4_.refs_8_ = bf16[4,128,768]{2,1,0:T(8,128)(2,1)S(1)} collective-permute-done((bf16[4,128,768]{2,1,0:T(8,128)(2,1)S(1)}, bf16[4,128,768]{2,1,0:T(8,128)(2,1)S(1)}, u32[]{:S(2)}, u32[]{:S(2)}) %collective-permute-start.30) | collective-permute-done | bytes 786464 | tf_op jit(solution)/shard_map/ppermute | solution.py:335
  363.3 14.9 %collective-permute-done.34.refs_7_.refs_11_ = bf16[4,128,768]{2,1,0:T(8,128)(2,1)S(1)} collective-permute-done((bf16[4,128,768]{2,1,0:T(8,128)(2,1)}, bf16[4,128,768]{2,1,0:T(8,128)(2,1)S(1)}, u32[]{:S(2)}, u32[]{:S(2)}) %collective-permute-start.34) | collective-permute-done | bytes 786464 | tf_op jit(solution)/shard_map/ppermute | solution.py:335
  385.5 24.5 %all_to_all.50 = bf16[4,4,64,768]{3,2,1,0:T(8,128)(2,1)} all-to-all(bf16[4,4,64,768]{3,2,1,0:T(8,128)(2,1)} %project.7), channel_id=1, replica_groups=mesh['cb'=4,'frame'=8] {'cb'}, dimensions={0} | all-to-all | bytes 3145728 | tf_op jit(solution)/shard_map/all_to_all | solution.py:350
  414.4 7.4 %attend.7 = (bf16[16,64,256]{2,1,0:T(8,128)(2,1)}, bf16[16,64,768]{2,1,0:T(8,128)(2,1)}) custom-call(bf16[16,64,768]{2,1,0:T(8,128)(2,1)} %bitcast.25, bf16[16,64,1024]{2,1,0:T(8,128)(2,1)} %bitcast.3.grad_ref), custom_call_target="tpu_custom_call" | custom-call | flops 1610612736 | bytes 4194304 | tf_op jit(solution)/shard_map/attend/pallas_call | solution.py:148
  421.8 18.4 %all-to-all-done.6.refs_2_.back_ref = bf16[4,4,64,1024]{3,2,1,0:T(8,128)(2,1)} async-done(((bf16[4,4,64,1024]{3,2,1,0:T(8,128)(2,1)}), bf16[4,4,64,1024]{3,2,1,0:T(8,128)(2,1)}, u32[]{:S(2)}, u32[]{:S(2)}) %all-to-all-start.6) | async-done | bytes 2097184 | tf_op jit(solution)/shard_map/all_to_all | solution.py:350
  440.2 13.0 %all_to_all.51.refs_3_ = bf16[4,4,64,256]{3,2,1,0:T(8,128)(2,1)} all-to-all(bf16[4,4,64,256]{3,2,1,0:T(8,128)(2,1)} %bitcast.26), channel_id=1, replica_groups=mesh['cb'=4,'frame'=8] {'cb'}, dimensions={0} | all-to-all | bytes 1048576 | tf_op jit(solution)/shard_map/all_to_all | solution.py:350
  456.8 8.0 %backward.5.refs_0_ = f32[4,256,1024]{2,1,0:T(8,128)} custom-call(s32[1,8]{1,0:T(1,128)} %fusion.10.source_ref, bf16[4,4,64,1024]{3,2,1,0:T(8,128)(2,1)} %copy-done.2, f32[4,256,1024]{2,1,0:T(8,128)} %backward.4.refs_0_, bf16[4,128,768]{2,1,0:T(8,128)(2,1)} %copy-done.5, bf16[4,128,768]{2,1,0:T(8,128)(2,1)} %collective-permute-done.19.refs_1_.refs_2_, ...), custom_call_target="tpu_custom_call" | custom-call | flops 1610612736 | bytes 16777216 | tf_op jit(solution)/shard_map/backward/pallas_call | solution.py:214
  464.8 7.9 %backward.6.refs_0_ = f32[4,256,1024]{2,1,0:T(8,128)} custom-call(s32[1,8]{1,0:T(1,128)} %fusion.10.source_ref, bf16[4,4,64,1024]{3,2,1,0:T(8,128)(2,1)} %all-to-all-done.6.refs_2_.back_ref, f32[4,256,1024]{2,1,0:T(8,128)} %backward.5.refs_0_, bf16[4,128,768]{2,1,0:T(8,128)(2,1)} %copy-done.4, bf16[4,128,768]{2,1,0:T(8,128)(2,1)} %collective-permute-done.17.refs_1_.refs_2_, ...), custom_call_target="tpu_custom_call" | custom-call | flops 1610612736 | bytes 16777216 | tf_op jit(solution)/shard_map/backward/pallas_call | solution.py:214
  472.7 7.7 %output.1 = bf16[4,256,1024]{2,1,0:T(8,128)(2,1)} custom-call(s32[1,8]{1,0:T(1,128)} %fusion.10.source_ref, bf16[4,256,1024]{2,1,0:T(8,128)(2,1)} %get-tuple-element.103.rows_ref.refs_1_, bf16[4,4,64,1024]{3,2,1,0:T(8,128)(2,1)} %copy-done.1, bf16[4,4,64,1024]{3,2,1,0:T(8,128)(2,1)} %copy-done.2, bf16[4,4,64,1024]{3,2,1,0:T(8,128)(2,1)} %all-to-all-done.6.refs_2_.back_ref, ...), custom_call_target="tpu_custom_call" | custom-call | flops 2147483648 | bytes 14680064 | tf_op jit(solution)/shard_map/output/pallas_call | solution.py:249
  486.2 8.8 %backward.7 = bf16[4,256,1024]{2,1,0:T(8,128)(2,1)} custom-call(s32[1,8]{1,0:T(1,128)} %fusion.10.source_ref, bf16[4,4,64,768]{3,2,1,0:T(8,128)(2,1)} %copy-done.6, f32[4,256,1024]{2,1,0:T(8,128)} %backward.6.refs_0_, bf16[4,256,1024]{2,1,0:T(8,128)(2,1)} %get-tuple-element.103.rows_ref.refs_1_, bf16[4,256,1024]{2,1,0:T(8,128)(2,1)} %get-tuple-element.49.rows_ref.refs_2_, ...), custom_call_target="tpu_custom_call" | custom-call | flops 1610612736 | bytes 16777216 | tf_op jit(solution)/shard_map/backward/pallas_call | solution.py:214
  (132 shorter events, 171.5 us)
Async XLA Ops:
  0.6 28.5 %collective-permute-start = (bf16[4,128,1024]{2,1,0:T(8,128)(2,1)}, bf16[4,128,1024]{2,1,0:T(8,128)(2,1)S(1)}, u32[]{:S(2)}, u32[]{:S(2)}) collective-permute-start(bf16[4,128,1024]{2,1,0:T(8,128)(2,1)} %refs_4_.1), channel_id=1, source_target_pairs={{0,2},{1,3},{2,4},{3,5},{4,6},{5,7},{6,0},{7,1},{8,10},{9,11},{10,... | collective-permute-start | bytes 3145736 | tf_op jit(solution)/shard_map/ppermute | solution.py:335
  3.7 25.4 %collective-permute-start.1 = (bf16[4,128,1024]{2,1,0:T(8,128)(2,1)}, bf16[4,128,1024]{2,1,0:T(8,128)(2,1)S(1)}, u32[]{:S(2)}, u32[]{:S(2)}) collective-permute-start(bf16[4,128,1024]{2,1,0:T(8,128)(2,1)} %refs_4_.1), channel_id=1, source_target_pairs={{0,1},{1,0},{2,3},{3,2},{4,5},{5,4},{6,7},{7,6},{8,9},{9,8},{10,11... | collective-permute-start | bytes 3145736 | tf_op jit(solution)/shard_map/ppermute | solution.py:335
  29.1 26.2 %collective-permute-start.2 = (bf16[4,128,1024]{2,1,0:T(8,128)(2,1)S(1)}, bf16[4,128,1024]{2,1,0:T(8,128)(2,1)S(1)}, u32[]{:S(2)}, u32[]{:S(2)}) collective-permute-start(bf16[4,128,1024]{2,1,0:T(8,128)(2,1)S(1)} %collective-permute-done.refs_2_.refs_6_), channel_id=1, source_target_pairs={{0,2},{1,3},{2,4},{3,5},{4,6},{5,7},{6,0},{7,1},{8,10},{9,11},{10,... | collective-permute-start | bytes 3145736 | tf_op jit(solution)/shard_map/ppermute | solution.py:335
  30.1 25.2 %collective-permute-start.3 = (bf16[4,128,1024]{2,1,0:T(8,128)(2,1)S(1)}, bf16[4,128,1024]{2,1,0:T(8,128)(2,1)S(1)}, u32[]{:S(2)}, u32[]{:S(2)}) collective-permute-start(bf16[4,128,1024]{2,1,0:T(8,128)(2,1)S(1)} %collective-permute-done.refs_2_.refs_6_), channel_id=1, source_target_pairs={{0,1},{1,0},{2,3},{3,2},{4,5},{5,4},{6,7},{7,6},{8,9},{9,8},{10,11... | collective-permute-start | bytes 3145736 | tf_op jit(solution)/shard_map/ppermute | solution.py:335
  55.3 25.4 %collective-permute-start.4 = (bf16[4,128,1024]{2,1,0:T(8,128)(2,1)S(1)}, bf16[4,128,1024]{2,1,0:T(8,128)(2,1)}, u32[]{:S(2)}, u32[]{:S(2)}) collective-permute-start(bf16[4,128,1024]{2,1,0:T(8,128)(2,1)S(1)} %collective-permute-done.2.refs_4_.refs_8_), channel_id=1, source_target_pairs={{0,2},{1,3},{2,4},{3,5},{4,6},{5,7},{6,0},{7,1},{8,10},{9,11},{10,... | collective-permute-start | bytes 3145736 | tf_op jit(solution)/shard_map/ppermute | solution.py:335
  56.3 24.4 %collective-permute-start.5 = (bf16[4,128,1024]{2,1,0:T(8,128)(2,1)S(1)}, bf16[4,128,1024]{2,1,0:T(8,128)(2,1)S(1)}, u32[]{:S(2)}, u32[]{:S(2)}) collective-permute-start(bf16[4,128,1024]{2,1,0:T(8,128)(2,1)S(1)} %collective-permute-done.2.refs_4_.refs_8_), channel_id=1, source_target_pairs={{0,1},{1,0},{2,3},{3,2},{4,5},{5,4},{6,7},{7,6},{8,9},{9,8},{10,11... | collective-permute-start | bytes 3145736 | tf_op jit(solution)/shard_map/ppermute | solution.py:335
  80.7 23.4 %collective-permute-start.7 = (bf16[4,128,1024]{2,1,0:T(8,128)(2,1)}, bf16[4,128,1024]{2,1,0:T(8,128)(2,1)}, u32[]{:S(2)}, u32[]{:S(2)}) collective-permute-start(bf16[4,128,1024]{2,1,0:T(8,128)(2,1)} %collective-permute-done.4.refs_6_.refs_10_), channel_id=1, source_target_pairs={{0,1},{1,0},{2,3},{3,2},{4,5},{5,4},{6,7},{7,6},{8,9},{9,8},{10,11... | collective-permute-start | bytes 3145736 | tf_op jit(solution)/shard_map/ppermute | solution.py:335
  81.8 18.9 %collective-permute-start.6 = (bf16[4,128,768]{2,1,0:T(8,128)(2,1)}, bf16[4,128,768]{2,1,0:T(8,128)(2,1)}, u32[]{:S(2)}, u32[]{:S(2)}) collective-permute-start(bf16[4,128,768]{2,1,0:T(8,128)(2,1)} %get-tuple-element.48.refs_0_), channel_id=1, source_target_pairs={{0,2},{1,3},{2,4},{3,5},{4,6},{5,7},{6,0},{7,1},{8,10},{9,11},{10,... | collective-permute-start | bytes 2359304 | tf_op jit(solution)/shard_map/ppermute | solution.py:335
  112.4 30.2 %all-to-all-start = ((bf16[4,4,64,1024]{3,2,1,0:T(8,128)(2,1)}), bf16[4,4,64,1024]{3,2,1,0:T(8,128)(2,1)}, u32[]{:S(2)}, u32[]{:S(2)}) async-start(bf16[4,4,64,1024]{3,2,1,0:T(8,128)(2,1)} %project_back.1), calls=%async_computation | async-start | bytes 4194304 | tf_op jit(solution)/shard_map/all_to_all | solution.py:350
  142.7 21.2 %collective-permute-start.12 = (bf16[4,128,768]{2,1,0:T(8,128)(2,1)S(1)}, bf16[4,128,768]{2,1,0:T(8,128)(2,1)S(1)}, u32[]{:S(2)}, u32[]{:S(2)}) collective-permute-start(bf16[4,128,768]{2,1,0:T(8,128)(2,1)S(1)} %get-tuple-element.60.refs_0_.refs_1_), channel_id=1, source_target_pairs={{0,2},{1,3},{2,4},{3,5},{4,6},{5,7},{6,0},{7,1},{8,10},{9,11},{10,... | collective-permute-start | bytes 2359304 | tf_op jit(solution)/shard_map/ppermute | solution.py:335
  142.7 21.2 %collective-permute-start.13 = (bf16[4,128,768]{2,1,0:T(8,128)(2,1)}, bf16[4,128,768]{2,1,0:T(8,128)(2,1)S(1)}, u32[]{:S(2)}, u32[]{:S(2)}) collective-permute-start(bf16[4,128,768]{2,1,0:T(8,128)(2,1)} %collective-permute-done.8.refs_4_), channel_id=1, source_target_pairs={{0,1},{1,0},{2,3},{3,2},{4,5},{5,4},{6,7},{7,6},{8,9},{9,8},{10,11... | collective-permute-start | bytes 2359304 | tf_op jit(solution)/shard_map/ppermute | solution.py:335
  163.8 20.4 %collective-permute-start.14 = (bf16[4,128,768]{2,1,0:T(8,128)(2,1)S(1)}, bf16[4,128,768]{2,1,0:T(8,128)(2,1)}, u32[]{:S(2)}, u32[]{:S(2)}) collective-permute-start(bf16[4,128,768]{2,1,0:T(8,128)(2,1)S(1)} %collective-permute-done.12.refs_2_.refs_3_), channel_id=1, source_target_pairs={{0,2},{1,3},{2,4},{3,5},{4,6},{5,7},{6,0},{7,1},{8,10},{9,11},{10,... | collective-permute-start | bytes 2359304 | tf_op jit(solution)/shard_map/ppermute | solution.py:335
  163.9 20.4 %collective-permute-start.15 = (bf16[4,128,768]{2,1,0:T(8,128)(2,1)}, bf16[4,128,768]{2,1,0:T(8,128)(2,1)S(1)}, u32[]{:S(2)}, u32[]{:S(2)}) collective-permute-start(bf16[4,128,768]{2,1,0:T(8,128)(2,1)} %collective-permute-done.10.refs_6_), channel_id=1, source_target_pairs={{0,1},{1,0},{2,3},{3,2},{4,5},{5,4},{6,7},{7,6},{8,9},{9,8},{10,11... | collective-permute-start | bytes 2359304 | tf_op jit(solution)/shard_map/ppermute | solution.py:335
  184.3 19.7 %collective-permute-start.16 = (bf16[4,128,768]{2,1,0:T(8,128)(2,1)}, bf16[4,128,768]{2,1,0:T(8,128)(2,1)}, u32[]{:S(2)}, u32[]{:S(2)}) collective-permute-start(bf16[4,128,768]{2,1,0:T(8,128)(2,1)} %collective-permute-done.14.refs_4_.refs_5_), channel_id=1, source_target_pairs={{0,2},{1,3},{2,4},{3,5},{4,6},{5,7},{6,0},{7,1},{8,10},{9,11},{10,... | collective-permute-start | bytes 2359304 | tf_op jit(solution)/shard_map/ppermute | solution.py:335
  185.2 18.9 %collective-permute-start.17 = (bf16[4,128,768]{2,1,0:T(8,128)(2,1)S(1)}, bf16[4,128,768]{2,1,0:T(8,128)(2,1)}, u32[]{:S(2)}, u32[]{:S(2)}) collective-permute-start(bf16[4,128,768]{2,1,0:T(8,128)(2,1)S(1)} %get-tuple-element.59.refs_0_.refs_1_), channel_id=1, source_target_pairs={{0,1},{1,0},{2,3},{3,2},{4,5},{5,4},{6,7},{7,6},{8,9},{9,8},{10,11... | collective-permute-start | bytes 2359304 | tf_op jit(solution)/shard_map/ppermute | solution.py:335
  204.0 18.6 %collective-permute-start.18 = (bf16[4,128,768]{2,1,0:T(8,128)(2,1)S(1)}, bf16[4,128,768]{2,1,0:T(8,128)(2,1)}, u32[]{:S(2)}, u32[]{:S(2)}) collective-permute-start(bf16[4,128,768]{2,1,0:T(8,128)(2,1)S(1)} %get-tuple-element.59.refs_0_.refs_1_), channel_id=1, source_target_pairs={{0,2},{1,3},{2,4},{3,5},{4,6},{5,7},{6,0},{7,1},{8,10},{9,11},{10,... | collective-permute-start | bytes 2359304 | tf_op jit(solution)/shard_map/ppermute | solution.py:335
  204.1 18.5 %collective-permute-start.19 = (bf16[4,128,768]{2,1,0:T(8,128)(2,1)S(1)}, bf16[4,128,768]{2,1,0:T(8,128)(2,1)}, u32[]{:S(2)}, u32[]{:S(2)}) collective-permute-start(bf16[4,128,768]{2,1,0:T(8,128)(2,1)S(1)} %get-tuple-element.60.refs_0_.refs_1_), channel_id=1, source_target_pairs={{0,1},{1,0},{2,3},{3,2},{4,5},{5,4},{6,7},{7,6},{8,9},{9,8},{10,11... | collective-permute-start | bytes 2359304 | tf_op jit(solution)/shard_map/ppermute | solution.py:335
  205.1 24.5 %all-to-all-start.1 = ((bf16[4,4,64,768]{3,2,1,0:T(8,128)(2,1)}), bf16[4,4,64,768]{3,2,1,0:T(8,128)(2,1)}, u32[]{:S(2)}, u32[]{:S(2)}) async-start(bf16[4,4,64,768]{3,2,1,0:T(8,128)(2,1)} %project.4), calls=%async_computation.1 | async-start | bytes 3145728 | tf_op jit(solution)/shard_map/all_to_all | solution.py:350
  259.7 34.9 %all-to-all-start.2 = ((bf16[4,4,64,1024]{3,2,1,0:T(8,128)(2,1)}), bf16[4,4,64,1024]{3,2,1,0:T(8,128)(2,1)S(1)}, u32[]{:S(2)}, u32[]{:S(2)}) async-start(bf16[4,4,64,1024]{3,2,1,0:T(8,128)(2,1)} %bitcast.21), calls=%async_computation.2 | async-start | bytes 4194304 | tf_op jit(solution)/shard_map/all_to_all | solution.py:350
  294.6 24.5 %all-to-all-start.3 = ((bf16[4,4,64,768]{3,2,1,0:T(8,128)(2,1)}), bf16[4,4,64,768]{3,2,1,0:T(8,128)(2,1)}, u32[]{:S(2)}, u32[]{:S(2)}) async-start(bf16[4,4,64,768]{3,2,1,0:T(8,128)(2,1)} %project.5), calls=%async_computation.3 | async-start | bytes 3145728 | tf_op jit(solution)/shard_map/all_to_all | solution.py:350
  319.1 27.3 %all-to-all-start.5 = ((bf16[4,4,64,768]{3,2,1,0:T(8,128)(2,1)}), bf16[4,4,64,768]{3,2,1,0:T(8,128)(2,1)}, u32[]{:S(2)}, u32[]{:S(2)}) async-start(bf16[4,4,64,768]{3,2,1,0:T(8,128)(2,1)} %project.6), calls=%async_computation.5 | async-start | bytes 3145728 | tf_op jit(solution)/shard_map/all_to_all | solution.py:350
  346.4 39.1 %all-to-all-start.4 = ((bf16[4,4,64,1024]{3,2,1,0:T(8,128)(2,1)}), bf16[4,4,64,1024]{3,2,1,0:T(8,128)(2,1)S(1)}, u32[]{:S(2)}, u32[]{:S(2)}) async-start(bf16[4,4,64,1024]{3,2,1,0:T(8,128)(2,1)} %bitcast.22), calls=%async_computation.4 | async-start | bytes 4194304 | tf_op jit(solution)/shard_map/all_to_all | solution.py:350
  410.0 30.2 %all-to-all-start.6 = ((bf16[4,4,64,1024]{3,2,1,0:T(8,128)(2,1)}), bf16[4,4,64,1024]{3,2,1,0:T(8,128)(2,1)}, u32[]{:S(2)}, u32[]{:S(2)}) async-start(bf16[4,4,64,1024]{3,2,1,0:T(8,128)(2,1)} %bitcast.23), calls=%async_computation.6 | async-start | bytes 4194304 | tf_op jit(solution)/shard_map/all_to_all | solution.py:350
  453.2 31.7 %all-to-all-start.9 = ((bf16[4,4,64,768]{3,2,1,0:T(8,128)(2,1)}), bf16[4,4,64,768]{3,2,1,0:T(8,128)(2,1)S(1)}, u32[]{:S(2)}, u32[]{:S(2)}) async-start(bf16[4,4,64,768]{3,2,1,0:T(8,128)(2,1)} %bitcast.24), calls=%async_computation.9 | async-start | bytes 3145728 | tf_op jit(solution)/shard_map/all_to_all | solution.py:350
  (41 other events, 1290.7 us)

commit v4 on v3

--- a/solution.py
+++ b/solution.py
@@ -10,8 +10,8 @@
 HEADS = 16
 GROUP_HEADS = (4, 4, 4, 4)
 KERNEL_STEPS = 1
-EXCHANGE_STEPS = 2
-CROSS_FIRST = 3
+EXCHANGE_STEPS = 3
+CROSS_FIRST = 4
 CROSS_EARLY = 1.5
 ORDER = (0, 1, 2, 3, 4)
 VMEM_LIMIT = 60 * 1024 * 1024
@@ -346,8 +346,12 @@
     def group(g):
         return weight(1 + g)
 
+    sent = []
+
     def exchange(values):
-        return lax.all_to_all(values, "cb", split_axis=0, concat_axis=0, tiled=True)
+        values = tie(values, sent[-1:])
+        sent.append(lax.all_to_all(values, "cb", split_axis=0, concat_axis=0, tiled=True))
+        return sent[-1]
 
     def joined(values):
         return values.reshape((values.shape[0] * values.shape[1],) + values.shape[2:])
@@ -357,23 +361,32 @@
 
     def forward(g, step):
         made = project(source, tie(normed, latest[-1]), group(g), parts, False)
-        state[g] = joined(exchange(made))
         join(step + KERNEL_STEPS, made)
+        if g < final:
+            state[g] = joined(exchange(made))
+            return
+        state[g] = joined(exchange(tie(made, [state[g - 1]])))
+        for h in range(final - 1):
+            reverse(h, [made])
 
     def mix(g, step):
         split = g == final
         place, heads = starts[g] // widths[g], GROUP_HEADS[g]
-        mixed = attend(place, heads, split, tie(state[g], latest[-1]), state["grad"])
-        back = [exchange(m.reshape((parts, codebooks) + m.shape[1:])) for m in mixed]
+        after = [state["total"]] if split else latest[-1]
+        mixed = attend(place, heads, split, tie(state[g], after), state["grad"])
         join(step + KERNEL_STEPS, *mixed)
-        state[g] = back[-1]
-        contexts.append(back[0])
-
-    def reverse(g, step):
+        mixed = [m.reshape((parts, codebooks) + m.shape[1:]) for m in mixed]
+        contexts.append(exchange(mixed[0]))
+        if split:
+            reverse(g - 1, [mixed[0]])
+            state[g] = exchange(tie(mixed[1], [state["total"]]))
+        else:
+            state[g] = contexts[-1]
+
+    def reverse(g, after):
         epilogue = (rows, grad_rows, norm_gain) if g == final else None
-        back = tie(state[g], latest[-1])
+        back = tie(state[g], after)
         state["total"] = backward(source, back, group(g), state["total"], epilogue)
-        join(step + KERNEL_STEPS, state["total"])
 
     def start(step):
         grad = tie(grad_rows, latest[-1])
@@ -388,7 +401,7 @@
         for w in [w for w in waiting if arrived(w)]:
             waiting.remove(w)
             tasks.append((now, 0, start, ()) if w == 0 else (now, w, forward, (w - 1,)))
-        ready = sorted(task for task in tasks if task[0] <= now)
+        ready = sorted((task for task in tasks if task[0] <= now), key=lambda task: task[:2])
         for task in ready[: 1 if line_steps or cross_steps else len(ready)]:
             tasks.remove(task)
             _, _, run, operands = task
@@ -398,11 +411,9 @@
             run(*operands, now)
             if run is forward:
                 tasks.append((now + EXCHANGE_STEPS, 10 + operands[0], mix, operands))
-            elif run is mix and operands[0] < final:
-                tasks.append((now + EXCHANGE_STEPS + 1, 20 + operands[0], reverse, operands))
         carry()
     outputs = output(source, rows, contexts, widths, weight(0))
-    reverse(final, len(latest))
+    reverse(final, [])
     return outputs.transpose(1, 0, 2), state["total"].transpose(1, 0, 2)
 
 

time: 501 us -> 486 us (0.970)
  blocking collectives: 37.5 us -> 0 us
  waiting for transfers between devices: 272 us -> 291 us
    all_to_all x2 -> x0, blocking collectives: 37.5 us -> none  [exchange(): return lax.all_to_all(values, 'cb', split_axis=0, concat_axis=0, tiled=True)]
    ppermute x35, waiting for transfers between devices: 242 us -> 254 us  [carry(): lax.ppermute(tie(held[origin], after), 'frame', pairs)]
    all_to_all x8 -> x10, waiting for transfers between devices: 30 us -> 37.1 us  [exchange(): lax.all_to_all(values, 'cb', split_axis=0, concat_axis=0, tiled=True)]
    ppermute x35, starting transfers between devices: 27.4 us -> 21.2 us  [carry(): lax.ppermute(tie(held[origin], after), 'frame', pairs)]
    all_to_all x8 -> x10, starting transfers between devices: 33.1 us -> 39.3 us  [exchange(): lax.all_to_all(values, 'cb', split_axis=0, concat_axis=0, tiled=True)]
    unnamed x46 -> x60, local copies, waits for them, and re-layouts: 15.2 us -> 18.6 us
  transfers between devices with their start and end apart: 43 -> 45, of which waited for: 24 -> 31; matrix products, arithmetic and copies ran while one was open for 3% -> 3% of each run, Pallas kernels for 19% -> 19%
where the time goes in v4:
time: 486 us; the launch traced here: 484 us
  waiting for transfers between devices  291 us (60%)
  Pallas kernels  102 us (21%)
  starting transfers between devices  60.4 us (12%)
  local copies, waits for them, and re-layouts  24.1 us (5%)
  other arithmetic  5.58 us (1%)
    ppermute x35, waiting for transfers between devices, carry(): lax.ppermute(tie(held[origin], after), 'frame', pairs)  254 us
    all_to_all x10, starting transfers between devices, exchange(): lax.all_to_all(values, 'cb', split_axis=0, concat_axis=0, tiled=True)  39.3 us
    all_to_all x10, waiting for transfers between devices, exchange(): lax.all_to_all(values, 'cb', split_axis=0, concat_axis=0, tiled=True)  37.1 us
    pallas_call x5, Pallas kernels, project(): pl.pallas_call(functools.partial(project_kernel, layout, back), grid=(cod...  33.3 us
    pallas_call x4, Pallas kernels, backward(): pl.pallas_call(functools.partial(backward_kernel, layout, total is None,...  31.7 us
    pallas_call x4, Pallas kernels, attend(): pl.pallas_call(functools.partial(attend_kernel, heads), grid=(frames // F...  29.3 us
    ppermute x35, starting transfers between devices, carry(): lax.ppermute(tie(held[origin], after), 'frame', pairs)  21.2 us
    unnamed x60, local copies, waits for them, and re-layouts  18.6 us
  transfers between devices with their start and end apart: 45, of which 31 were waited for; matrix products, arithmetic and copies ran while one was open for 3% of the time, Pallas kernels for 19%

profile of v4, /device:TPU:0, one launch (start us, length us, event | category | flops | bytes accessed | tf_op | source)
XLA Modules:
  0.0 484.2 jit_solution(6248277783392963222)
XLA Ops:
  18.5 8.6 %collective-permute-done.1.refs_1_.refs_5_ = bf16[4,128,1024]{2,1,0:T(8,128)(2,1)S(1)} collective-permute-done((bf16[4,128,1024]{2,1,0:T(8,128)(2,1)}, bf16[4,128,1024]{2,1,0:T(8,128)(2,1)S(1)}, u32[]{:S(2)}, u32[]{:S(2)}) %collective-permute-start.1) | collective-permute-done | bytes 1048608 | tf_op jit(solution)/shard_map/ppermute | solution.py:335
  30.9 23.3 %collective-permute-done.3.refs_3_.refs_7_ = bf16[4,128,1024]{2,1,0:T(8,128)(2,1)S(1)} collective-permute-done((bf16[4,128,1024]{2,1,0:T(8,128)(2,1)S(1)}, bf16[4,128,1024]{2,1,0:T(8,128)(2,1)S(1)}, u32[]{:S(2)}, u32[]{:S(2)}) %collective-permute-start.3) | collective-permute-done | bytes 1048608 | tf_op jit(solution)/shard_map/ppermute | solution.py:335
  57.7 21.5 %collective-permute-done.5.refs_5_.refs_9_ = bf16[4,128,1024]{2,1,0:T(8,128)(2,1)S(1)} collective-permute-done((bf16[4,128,1024]{2,1,0:T(8,128)(2,1)S(1)}, bf16[4,128,1024]{2,1,0:T(8,128)(2,1)S(1)}, u32[]{:S(2)}, u32[]{:S(2)}) %collective-permute-start.5) | collective-permute-done | bytes 1048608 | tf_op jit(solution)/shard_map/ppermute | solution.py:335
  82.8 17.6 %collective-permute-done.6.refs_2_ = bf16[4,128,768]{2,1,0:T(8,128)(2,1)} collective-permute-done((bf16[4,128,768]{2,1,0:T(8,128)(2,1)S(1)}, bf16[4,128,768]{2,1,0:T(8,128)(2,1)}, u32[]{:S(2)}, u32[]{:S(2)}) %collective-permute-start.6) | collective-permute-done | bytes 786464 | tf_op jit(solution)/shard_map/ppermute | solution.py:335
  128.0 10.9 %collective-permute-done.10.refs_6_ = bf16[4,128,768]{2,1,0:T(8,128)(2,1)S(1)} collective-permute-done((bf16[4,128,768]{2,1,0:T(8,128)(2,1)}, bf16[4,128,768]{2,1,0:T(8,128)(2,1)S(1)}, u32[]{:S(2)}, u32[]{:S(2)}) %collective-permute-start.10) | collective-permute-done | bytes 786464 | tf_op jit(solution)/shard_map/ppermute | solution.py:335
  141.2 12.5 %all-to-all-done = bf16[4,4,64,1024]{3,2,1,0:T(8,128)(2,1)} async-done(((bf16[4,4,64,1024]{3,2,1,0:T(8,128)(2,1)}), bf16[4,4,64,1024]{3,2,1,0:T(8,128)(2,1)}, u32[]{:S(2)}, u32[]{:S(2)}) %all-to-all-start) | async-done | bytes 2097184 | tf_op jit(solution)/shard_map/all_to_all | solution.py:353
  155.4 19.7 %collective-permute-done.14.refs_4_.refs_5_ = bf16[4,128,768]{2,1,0:T(8,128)(2,1)} collective-permute-done((bf16[4,128,768]{2,1,0:T(8,128)(2,1)S(1)}, bf16[4,128,768]{2,1,0:T(8,128)(2,1)}, u32[]{:S(2)}, u32[]{:S(2)}) %collective-permute-start.14) | collective-permute-done | bytes 786464 | tf_op jit(solution)/shard_map/ppermute | solution.py:335
  183.5 12.7 %collective-permute-done.16.refs_6_.refs_7_ = bf16[4,128,768]{2,1,0:T(8,128)(2,1)} collective-permute-done((bf16[4,128,768]{2,1,0:T(8,128)(2,1)}, bf16[4,128,768]{2,1,0:T(8,128)(2,1)}, u32[]{:S(2)}, u32[]{:S(2)}) %collective-permute-start.16) | collective-permute-done | bytes 786464 | tf_op jit(solution)/shard_map/ppermute | solution.py:335
  201.8 13.5 %collective-permute-done.18.refs_2_.refs_3_ = bf16[4,128,768]{2,1,0:T(8,128)(2,1)S(1)} collective-permute-done((bf16[4,128,768]{2,1,0:T(8,128)(2,1)S(1)}, bf16[4,128,768]{2,1,0:T(8,128)(2,1)S(1)}, u32[]{:S(2)}, u32[]{:S(2)}) %collective-permute-start.18) | collective-permute-done | bytes 786464 | tf_op jit(solution)/shard_map/ppermute | solution.py:335
  216.1 17.5 %collective-permute-done.20.refs_4_.refs_5_ = bf16[4,128,768]{2,1,0:T(8,128)(2,1)} collective-permute-done((bf16[4,128,768]{2,1,0:T(8,128)(2,1)S(1)}, bf16[4,128,768]{2,1,0:T(8,128)(2,1)}, u32[]{:S(2)}, u32[]{:S(2)}) %collective-permute-start.20) | collective-permute-done | bytes 786464 | tf_op jit(solution)/shard_map/ppermute | solution.py:335
  234.1 7.3 %attend.4 = bf16[16,64,1024]{2,1,0:T(8,128)(2,1)} custom-call(bf16[16,64,768]{2,1,0:T(8,128)(2,1)} %bitcast.4.qkv_ref, bf16[16,64,1024]{2,1,0:T(8,128)(2,1)} %bitcast.3.grad_ref), custom_call_target="tpu_custom_call" | custom-call | flops 1610612736 | bytes 4194304 | tf_op jit(solution)/shard_map/attend/pallas_call | solution.py:148
  257.9 8.4 %collective-permute-done.25.refs_1_.refs_5_ = bf16[4,128,768]{2,1,0:T(8,128)(2,1)} collective-permute-done((bf16[4,128,768]{2,1,0:T(8,128)(2,1)S(1)}, bf16[4,128,768]{2,1,0:T(8,128)(2,1)}, u32[]{:S(2)}, u32[]{:S(2)}) %collective-permute-start.25) | collective-permute-done | bytes 786464 | tf_op jit(solution)/shard_map/ppermute | solution.py:335
  275.1 11.6 %collective-permute-done.26.refs_3_.refs_7_ = bf16[4,128,768]{2,1,0:T(8,128)(2,1)S(1)} collective-permute-done((bf16[4,128,768]{2,1,0:T(8,128)(2,1)}, bf16[4,128,768]{2,1,0:T(8,128)(2,1)S(1)}, u32[]{:S(2)}, u32[]{:S(2)}) %collective-permute-start.26) | collective-permute-done | bytes 786464 | tf_op jit(solution)/shard_map/ppermute | solution.py:335
  288.3 14.5 %collective-permute-done.28.refs_4_.refs_8_ = bf16[4,128,768]{2,1,0:T(8,128)(2,1)S(1)} collective-permute-done((bf16[4,128,768]{2,1,0:T(8,128)(2,1)}, bf16[4,128,768]{2,1,0:T(8,128)(2,1)S(1)}, u32[]{:S(2)}, u32[]{:S(2)}) %collective-permute-start.28) | collective-permute-done | bytes 786464 | tf_op jit(solution)/shard_map/ppermute | solution.py:335
  306.1 7.3 %attend.5 = bf16[16,64,1024]{2,1,0:T(8,128)(2,1)} custom-call(bf16[16,64,768]{2,1,0:T(8,128)(2,1)} %bitcast.6.qkv_ref, bf16[16,64,1024]{2,1,0:T(8,128)(2,1)} %bitcast.3.grad_ref), custom_call_target="tpu_custom_call" | custom-call | flops 1610612736 | bytes 4194304 | tf_op jit(solution)/shard_map/attend/pallas_call | solution.py:148
  319.9 19.3 %collective-permute-done.32.refs_6_.refs_10_ = bf16[4,128,768]{2,1,0:T(8,128)(2,1)S(1)} collective-permute-done((bf16[4,128,768]{2,1,0:T(8,128)(2,1)}, bf16[4,128,768]{2,1,0:T(8,128)(2,1)S(1)}, u32[]{:S(2)}, u32[]{:S(2)}) %collective-permute-start.32) | collective-permute-done | bytes 786464 | tf_op jit(solution)/shard_map/ppermute | solution.py:335
  350.4 21.9 %collective-permute-done.34.refs_7_.refs_11_ = bf16[4,128,768]{2,1,0:T(8,128)(2,1)S(1)} collective-permute-done((bf16[4,128,768]{2,1,0:T(8,128)(2,1)}, bf16[4,128,768]{2,1,0:T(8,128)(2,1)S(1)}, u32[]{:S(2)}, u32[]{:S(2)}) %collective-permute-start.34) | collective-permute-done | bytes 786464 | tf_op jit(solution)/shard_map/ppermute | solution.py:335
  390.5 12.8 %all-to-all-done.6 = bf16[4,4,64,768]{3,2,1,0:T(8,128)(2,1)S(1)} async-done(((bf16[4,4,64,768]{3,2,1,0:T(8,128)(2,1)}), bf16[4,4,64,768]{3,2,1,0:T(8,128)(2,1)S(1)}, u32[]{:S(2)}, u32[]{:S(2)}) %all-to-all-start.6) | async-done | bytes 1572896 | tf_op jit(solution)/shard_map/all_to_all | solution.py:353
  415.0 8.0 %backward.5.refs_0_ = f32[4,256,1024]{2,1,0:T(8,128)} custom-call(s32[1,8]{1,0:T(1,128)} %fusion.10.source_ref, bf16[4,4,64,1024]{3,2,1,0:T(8,128)(2,1)} %copy-done.2, f32[4,256,1024]{2,1,0:T(8,128)} %backward.4.refs_0_, bf16[4,128,768]{2,1,0:T(8,128)(2,1)} %copy-done.6, bf16[4,128,768]{2,1,0:T(8,128)(2,1)} %collective-permute-done.17.refs_1_.refs_2_, ...), custom_call_target="tpu_custom_call" | custom-call | flops 1610612736 | bytes 16777216 | tf_op jit(solution)/shard_map/backward/pallas_call | solution.py:214
  423.0 7.4 %attend.7 = (bf16[16,64,256]{2,1,0:T(8,128)(2,1)}, bf16[16,64,768]{2,1,0:T(8,128)(2,1)}) custom-call(bf16[16,64,768]{2,1,0:T(8,128)(2,1)} %bitcast.25, bf16[16,64,1024]{2,1,0:T(8,128)(2,1)} %bitcast.3.grad_ref), custom_call_target="tpu_custom_call" | custom-call | flops 1610612736 | bytes 4194304 | tf_op jit(solution)/shard_map/attend/pallas_call | solution.py:148
  437.2 7.9 %backward.6.refs_0_ = f32[4,256,1024]{2,1,0:T(8,128)} custom-call(s32[1,8]{1,0:T(1,128)} %fusion.10.source_ref, bf16[4,4,64,1024]{3,2,1,0:T(8,128)(2,1)} %copy-done.3, f32[4,256,1024]{2,1,0:T(8,128)} %backward.5.refs_0_, bf16[4,128,768]{2,1,0:T(8,128)(2,1)} %copy-done.5, bf16[4,128,768]{2,1,0:T(8,128)(2,1)} %collective-permute-done.27.refs_1_.refs_2_, ...), custom_call_target="tpu_custom_call" | custom-call | flops 1610612736 | bytes 16777216 | tf_op jit(solution)/shard_map/backward/pallas_call | solution.py:214
  449.8 7.7 %output.1 = bf16[4,256,1024]{2,1,0:T(8,128)(2,1)} custom-call(s32[1,8]{1,0:T(1,128)} %fusion.10.source_ref, bf16[4,256,1024]{2,1,0:T(8,128)(2,1)} %get-tuple-element.129.rows_ref.refs_1_, bf16[4,4,64,1024]{3,2,1,0:T(8,128)(2,1)} %copy-done.1, bf16[4,4,64,1024]{3,2,1,0:T(8,128)(2,1)} %copy-done.2, bf16[4,4,64,1024]{3,2,1,0:T(8,128)(2,1)} %copy-done.3, ...), custom_call_target="tpu_custom_call" | custom-call | flops 2147483648 | bytes 14680064 | tf_op jit(solution)/shard_map/output/pallas_call | solution.py:249
  462.1 7.6 %all-to-all-done.9.back_ref = bf16[4,4,64,768]{3,2,1,0:T(8,128)(2,1)S(1)} async-done(((bf16[4,4,64,768]{3,2,1,0:T(8,128)(2,1)}), bf16[4,4,64,768]{3,2,1,0:T(8,128)(2,1)S(1)}, u32[]{:S(2)}, u32[]{:S(2)}) %all-to-all-start.9) | async-done | bytes 1572896 | tf_op jit(solution)/shard_map/all_to_all | solution.py:353
  470.9 8.8 %backward.7 = bf16[4,256,1024]{2,1,0:T(8,128)(2,1)} custom-call(s32[1,8]{1,0:T(1,128)} %fusion.10.source_ref, bf16[4,4,64,768]{3,2,1,0:T(8,128)(2,1)} %copy-done.8, f32[4,256,1024]{2,1,0:T(8,128)} %backward.6.refs_0_, bf16[4,256,1024]{2,1,0:T(8,128)(2,1)} %get-tuple-element.129.rows_ref.refs_1_, bf16[4,256,1024]{2,1,0:T(8,128)(2,1)} %get-tuple-element.62.rows_ref.refs_2_, ...), custom_call_target="tpu_custom_call" | custom-call | flops 1610612736 | bytes 16777216 | tf_op jit(solution)/shard_map/backward/pallas_call | solution.py:214
  (148 shorter events, 175.0 us)
Async XLA Ops:
  0.6 26.4 %collective-permute-start.1 = (bf16[4,128,1024]{2,1,0:T(8,128)(2,1)}, bf16[4,128,1024]{2,1,0:T(8,128)(2,1)S(1)}, u32[]{:S(2)}, u32[]{:S(2)}) collective-permute-start(bf16[4,128,1024]{2,1,0:T(8,128)(2,1)} %refs_4_.1), channel_id=1, source_target_pairs={{0,1},{1,0},{2,3},{3,2},{4,5},{5,4},{6,7},{7,6},{8,9},{9,8},{10,11... | collective-permute-start | bytes 3145736 | tf_op jit(solution)/shard_map/ppermute | solution.py:335
  3.7 26.7 %collective-permute-start = (bf16[4,128,1024]{2,1,0:T(8,128)(2,1)}, bf16[4,128,1024]{2,1,0:T(8,128)(2,1)S(1)}, u32[]{:S(2)}, u32[]{:S(2)}) collective-permute-start(bf16[4,128,1024]{2,1,0:T(8,128)(2,1)} %refs_4_.1), channel_id=1, source_target_pairs={{0,2},{1,3},{2,4},{3,5},{4,6},{5,7},{6,0},{7,1},{8,10},{9,11},{10,... | collective-permute-start | bytes 3145736 | tf_op jit(solution)/shard_map/ppermute | solution.py:335
  30.4 23.8 %collective-permute-start.3 = (bf16[4,128,1024]{2,1,0:T(8,128)(2,1)S(1)}, bf16[4,128,1024]{2,1,0:T(8,128)(2,1)S(1)}, u32[]{:S(2)}, u32[]{:S(2)}) collective-permute-start(bf16[4,128,1024]{2,1,0:T(8,128)(2,1)S(1)} %collective-permute-done.refs_2_.refs_6_), channel_id=1, source_target_pairs={{0,1},{1,0},{2,3},{3,2},{4,5},{5,4},{6,7},{7,6},{8,9},{9,8},{10,11... | collective-permute-start | bytes 3145736 | tf_op jit(solution)/shard_map/ppermute | solution.py:335
  30.9 25.5 %collective-permute-start.2 = (bf16[4,128,1024]{2,1,0:T(8,128)(2,1)S(1)}, bf16[4,128,1024]{2,1,0:T(8,128)(2,1)S(1)}, u32[]{:S(2)}, u32[]{:S(2)}) collective-permute-start(bf16[4,128,1024]{2,1,0:T(8,128)(2,1)S(1)} %collective-permute-done.refs_2_.refs_6_), channel_id=1, source_target_pairs={{0,2},{1,3},{2,4},{3,5},{4,6},{5,7},{6,0},{7,1},{8,10},{9,11},{10,... | collective-permute-start | bytes 3145736 | tf_op jit(solution)/shard_map/ppermute | solution.py:335
  56.4 22.8 %collective-permute-start.5 = (bf16[4,128,1024]{2,1,0:T(8,128)(2,1)S(1)}, bf16[4,128,1024]{2,1,0:T(8,128)(2,1)S(1)}, u32[]{:S(2)}, u32[]{:S(2)}) collective-permute-start(bf16[4,128,1024]{2,1,0:T(8,128)(2,1)S(1)} %collective-permute-done.2.refs_4_.refs_8_), channel_id=1, source_target_pairs={{0,1},{1,0},{2,3},{3,2},{4,5},{5,4},{6,7},{7,6},{8,9},{9,8},{10,11... | collective-permute-start | bytes 3145736 | tf_op jit(solution)/shard_map/ppermute | solution.py:335
  57.7 24.1 %collective-permute-start.4 = (bf16[4,128,1024]{2,1,0:T(8,128)(2,1)S(1)}, bf16[4,128,1024]{2,1,0:T(8,128)(2,1)S(1)}, u32[]{:S(2)}, u32[]{:S(2)}) collective-permute-start(bf16[4,128,1024]{2,1,0:T(8,128)(2,1)S(1)} %collective-permute-done.2.refs_4_.refs_8_), channel_id=1, source_target_pairs={{0,2},{1,3},{2,4},{3,5},{4,6},{5,7},{6,0},{7,1},{8,10},{9,11},{10,... | collective-permute-start | bytes 3145736 | tf_op jit(solution)/shard_map/ppermute | solution.py:335
  81.9 23.1 %collective-permute-start.7 = (bf16[4,128,1024]{2,1,0:T(8,128)(2,1)S(1)}, bf16[4,128,1024]{2,1,0:T(8,128)(2,1)S(1)}, u32[]{:S(2)}, u32[]{:S(2)}) collective-permute-start(bf16[4,128,1024]{2,1,0:T(8,128)(2,1)S(1)} %collective-permute-done.4.refs_6_.refs_10_), channel_id=1, source_target_pairs={{0,1},{1,0},{2,3},{3,2},{4,5},{5,4},{6,7},{7,6},{8,9},{9,8},{10,11... | collective-permute-start | bytes 3145736 | tf_op jit(solution)/shard_map/ppermute | solution.py:335
  123.5 30.2 %all-to-all-start = ((bf16[4,4,64,1024]{3,2,1,0:T(8,128)(2,1)}), bf16[4,4,64,1024]{3,2,1,0:T(8,128)(2,1)}, u32[]{:S(2)}, u32[]{:S(2)}) async-start(bf16[4,4,64,1024]{3,2,1,0:T(8,128)(2,1)} %project_back.1), calls=%async_computation | async-start | bytes 4194304 | tf_op jit(solution)/shard_map/all_to_all | solution.py:353
  154.1 21.0 %collective-permute-start.14 = (bf16[4,128,768]{2,1,0:T(8,128)(2,1)S(1)}, bf16[4,128,768]{2,1,0:T(8,128)(2,1)}, u32[]{:S(2)}, u32[]{:S(2)}) collective-permute-start(bf16[4,128,768]{2,1,0:T(8,128)(2,1)S(1)} %collective-permute-done.12.refs_2_.refs_3_), channel_id=1, source_target_pairs={{0,2},{1,3},{2,4},{3,5},{4,6},{5,7},{6,0},{7,1},{8,10},{9,11},{10,... | collective-permute-start | bytes 2359304 | tf_op jit(solution)/shard_map/ppermute | solution.py:335
  154.1 21.0 %collective-permute-start.15 = (bf16[4,128,768]{2,1,0:T(8,128)(2,1)}, bf16[4,128,768]{2,1,0:T(8,128)(2,1)S(1)}, u32[]{:S(2)}, u32[]{:S(2)}) collective-permute-start(bf16[4,128,768]{2,1,0:T(8,128)(2,1)} %copy-done.23), channel_id=1, source_target_pairs={{0,1},{1,0},{2,3},{3,2},{4,5},{5,4},{6,7},{7,6},{8,9},{9,8},{10,11... | collective-permute-start | bytes 2359304 | tf_op jit(solution)/shard_map/ppermute | solution.py:335
  176.0 20.3 %collective-permute-start.16 = (bf16[4,128,768]{2,1,0:T(8,128)(2,1)}, bf16[4,128,768]{2,1,0:T(8,128)(2,1)}, u32[]{:S(2)}, u32[]{:S(2)}) collective-permute-start(bf16[4,128,768]{2,1,0:T(8,128)(2,1)} %collective-permute-done.14.refs_4_.refs_5_), channel_id=1, source_target_pairs={{0,2},{1,3},{2,4},{3,5},{4,6},{5,7},{6,0},{7,1},{8,10},{9,11},{10,... | collective-permute-start | bytes 2359304 | tf_op jit(solution)/shard_map/ppermute | solution.py:335
  176.0 20.3 %collective-permute-start.17 = (bf16[4,128,768]{2,1,0:T(8,128)(2,1)S(1)}, bf16[4,128,768]{2,1,0:T(8,128)(2,1)}, u32[]{:S(2)}, u32[]{:S(2)}) collective-permute-start(bf16[4,128,768]{2,1,0:T(8,128)(2,1)S(1)} %get-tuple-element.72.refs_0_.refs_1_), channel_id=1, source_target_pairs={{0,1},{1,0},{2,3},{3,2},{4,5},{5,4},{6,7},{7,6},{8,9},{9,8},{10,11... | collective-permute-start | bytes 2359304 | tf_op jit(solution)/shard_map/ppermute | solution.py:335
  196.3 19.1 %collective-permute-start.18 = (bf16[4,128,768]{2,1,0:T(8,128)(2,1)S(1)}, bf16[4,128,768]{2,1,0:T(8,128)(2,1)S(1)}, u32[]{:S(2)}, u32[]{:S(2)}) collective-permute-start(bf16[4,128,768]{2,1,0:T(8,128)(2,1)S(1)} %get-tuple-element.85.refs_0_.refs_1_), channel_id=1, source_target_pairs={{0,2},{1,3},{2,4},{3,5},{4,6},{5,7},{6,0},{7,1},{8,10},{9,11},{10,... | collective-permute-start | bytes 2359304 | tf_op jit(solution)/shard_map/ppermute | solution.py:335
  197.5 36.7 %all-to-all-start.1 = ((bf16[4,4,64,768]{3,2,1,0:T(8,128)(2,1)}), bf16[4,4,64,768]{3,2,1,0:T(8,128)(2,1)}, u32[]{:S(2)}, u32[]{:S(2)}) async-start(bf16[4,4,64,768]{3,2,1,0:T(8,128)(2,1)} %project.4), calls=%async_computation.1 | async-start | bytes 3145728 | tf_op jit(solution)/shard_map/all_to_all | solution.py:353
  241.5 29.3 %all-to-all-start.2 = ((bf16[4,4,64,1024]{3,2,1,0:T(8,128)(2,1)}), bf16[4,4,64,1024]{3,2,1,0:T(8,128)(2,1)S(1)}, u32[]{:S(2)}, u32[]{:S(2)}) async-start(bf16[4,4,64,1024]{3,2,1,0:T(8,128)(2,1)} %bitcast.21), calls=%async_computation.2 | async-start | bytes 4194304 | tf_op jit(solution)/shard_map/all_to_all | solution.py:353
  270.7 35.3 %all-to-all-start.3 = ((bf16[4,4,64,768]{3,2,1,0:T(8,128)(2,1)}), bf16[4,4,64,768]{3,2,1,0:T(8,128)(2,1)}, u32[]{:S(2)}, u32[]{:S(2)}) async-start(bf16[4,4,64,768]{3,2,1,0:T(8,128)(2,1)} %project.5), calls=%async_computation.3 | async-start | bytes 3145728 | tf_op jit(solution)/shard_map/all_to_all | solution.py:353
  313.4 32.5 %all-to-all-start.4 = ((bf16[4,4,64,1024]{3,2,1,0:T(8,128)(2,1)}), bf16[4,4,64,1024]{3,2,1,0:T(8,128)(2,1)S(1)}, u32[]{:S(2)}, u32[]{:S(2)}) async-start(bf16[4,4,64,1024]{3,2,1,0:T(8,128)(2,1)} %bitcast.23), calls=%async_computation.4 | async-start | bytes 4194304 | tf_op jit(solution)/shard_map/all_to_all | solution.py:353
  319.0 20.2 %collective-permute-start.32 = (bf16[4,128,768]{2,1,0:T(8,128)(2,1)}, bf16[4,128,768]{2,1,0:T(8,128)(2,1)S(1)}, u32[]{:S(2)}, u32[]{:S(2)}) collective-permute-start(bf16[4,128,768]{2,1,0:T(8,128)(2,1)} %copy-done.19), channel_id=1, source_target_pairs={{0,2},{1,3},{2,4},{3,5},{4,6},{5,7},{6,0},{7,1},{8,10},{9,11},{10,... | collective-permute-start | bytes 2359304 | tf_op jit(solution)/shard_map/ppermute | solution.py:335
  319.3 19.9 %collective-permute-start.33 = (bf16[4,128,768]{2,1,0:T(8,128)(2,1)}, bf16[4,128,768]{2,1,0:T(8,128)(2,1)}, u32[]{:S(2)}, u32[]{:S(2)}) collective-permute-start(bf16[4,128,768]{2,1,0:T(8,128)(2,1)} %collective-permute-done.22.refs_6_.refs_7_), channel_id=1, source_target_pairs={{0,1},{1,0},{2,3},{3,2},{4,5},{5,4},{6,7},{7,6},{8,9},{9,8},{10,11... | collective-permute-start | bytes 2359304 | tf_op jit(solution)/shard_map/ppermute | solution.py:335
  346.0 33.7 %all-to-all-start.5 = ((bf16[4,4,64,768]{3,2,1,0:T(8,128)(2,1)}), bf16[4,4,64,768]{3,2,1,0:T(8,128)(2,1)}, u32[]{:S(2)}, u32[]{:S(2)}) async-start(bf16[4,4,64,768]{3,2,1,0:T(8,128)(2,1)} %project.6), calls=%async_computation.5 | async-start | bytes 3145728 | tf_op jit(solution)/shard_map/all_to_all | solution.py:353
  350.3 21.9 %collective-permute-start.34 = (bf16[4,128,768]{2,1,0:T(8,128)(2,1)}, bf16[4,128,768]{2,1,0:T(8,128)(2,1)S(1)}, u32[]{:S(2)}, u32[]{:S(2)}) collective-permute-start(bf16[4,128,768]{2,1,0:T(8,128)(2,1)} %collective-permute-done.30.refs_5_.refs_9_), channel_id=1, source_target_pairs={{0,2},{1,3},{2,4},{3,5},{4,6},{5,7},{6,0},{7,1},{8,10},{9,11},{10,... | collective-permute-start | bytes 2359304 | tf_op jit(solution)/shard_map/ppermute | solution.py:335
  379.7 23.6 %all-to-all-start.6 = ((bf16[4,4,64,768]{3,2,1,0:T(8,128)(2,1)}), bf16[4,4,64,768]{3,2,1,0:T(8,128)(2,1)S(1)}, u32[]{:S(2)}, u32[]{:S(2)}) async-start(bf16[4,4,64,768]{3,2,1,0:T(8,128)(2,1)} %project.7), calls=%async_computation.6 | async-start | bytes 3145728 | tf_op jit(solution)/shard_map/all_to_all | solution.py:353
  404.4 29.3 %all-to-all-start.7 = ((bf16[4,4,64,1024]{3,2,1,0:T(8,128)(2,1)}), bf16[4,4,64,1024]{3,2,1,0:T(8,128)(2,1)S(1)}, u32[]{:S(2)}, u32[]{:S(2)}) async-start(bf16[4,4,64,1024]{3,2,1,0:T(8,128)(2,1)} %bitcast.22), calls=%async_computation.7 | async-start | bytes 4194304 | tf_op jit(solution)/shard_map/all_to_all | solution.py:353
  446.0 23.6 %all-to-all-start.9 = ((bf16[4,4,64,768]{3,2,1,0:T(8,128)(2,1)}), bf16[4,4,64,768]{3,2,1,0:T(8,128)(2,1)S(1)}, u32[]{:S(2)}, u32[]{:S(2)}) async-start(bf16[4,4,64,768]{3,2,1,0:T(8,128)(2,1)} %bitcast.24), calls=%async_computation.9 | async-start | bytes 3145728 | tf_op jit(solution)/shard_map/all_to_all | solution.py:353
  (50 other events, 1541.3 us)

commit v5 on v4

--- a/solution.py
+++ b/solution.py
@@ -120,7 +120,7 @@
         scores = dot(q_heads, k.astype(BF16), 1, 1).reshape(heads, rows, rows) * factor
         scores = jnp.where(allowed, scores, -jnp.inf)
         weights = jnp.exp(scores - jnp.max(scores, axis=-1, keepdims=True))
-        probs = weights / jnp.sum(weights, axis=-1, keepdims=True)
+        probs = weights * (1.0 / jnp.sum(weights, axis=-1, keepdims=True))
         grad_probs = dot(g_heads, v.astype(BF16), 1, 1).reshape(heads, rows, rows)
         inner = jnp.sum(probs * grad_probs, axis=-1, keepdims=True)
         grad_scores = (probs * (grad_probs - inner) * factor).astype(BF16)

time: 486 us -> 486 us (level)
  no operation moved by 1% of the time
where the time goes in v5:
time: 486 us; the launch traced here: 484 us
  waiting for transfers between devices  291 us (60%)
  Pallas kernels  102 us (21%)
  starting transfers between devices  60.4 us (12%)
  local copies, waits for them, and re-layouts  24.1 us (5%)
  other arithmetic  5.58 us (1%)
    ppermute x35, waiting for transfers between devices, carry(): lax.ppermute(tie(held[origin], after), 'frame', pairs)  254 us
    all_to_all x10, starting transfers between devices, exchange(): lax.all_to_all(values, 'cb', split_axis=0, concat_axis=0, tiled=True)  39.3 us
    all_to_all x10, waiting for transfers between devices, exchange(): lax.all_to_all(values, 'cb', split_axis=0, concat_axis=0, tiled=True)  37.1 us
    pallas_call x5, Pallas kernels, project(): pl.pallas_call(functools.partial(project_kernel, layout, back), grid=(cod...  33.3 us
    pallas_call x4, Pallas kernels, backward(): pl.pallas_call(functools.partial(backward_kernel, layout, total is None,...  31.7 us
    pallas_call x4, Pallas kernels, attend(): pl.pallas_call(functools.partial(attend_kernel, heads), grid=(frames // F...  29.3 us
    ppermute x35, starting transfers between devices, carry(): lax.ppermute(tie(held[origin], after), 'frame', pairs)  21.2 us
    unnamed x60, local copies, waits for them, and re-layouts  18.6 us
  transfers between devices with their start and end apart: 45, of which 31 were waited for; matrix products, arithmetic and copies ran while one was open for 3% of the time, Pallas kernels for 19%

profile of v5, /device:TPU:0, one launch (start us, length us, event | category | flops | bytes accessed | tf_op | source)
XLA Modules:
  0.0 484.2 jit_solution(6248277783392963222)
XLA Ops:
  18.5 8.6 %collective-permute-done.1.refs_1_.refs_5_ = bf16[4,128,1024]{2,1,0:T(8,128)(2,1)S(1)} collective-permute-done((bf16[4,128,1024]{2,1,0:T(8,128)(2,1)}, bf16[4,128,1024]{2,1,0:T(8,128)(2,1)S(1)}, u32[]{:S(2)}, u32[]{:S(2)}) %collective-permute-start.1) | collective-permute-done | bytes 1048608 | tf_op jit(solution)/shard_map/ppermute | solution.py:335
  30.9 23.3 %collective-permute-done.3.refs_3_.refs_7_ = bf16[4,128,1024]{2,1,0:T(8,128)(2,1)S(1)} collective-permute-done((bf16[4,128,1024]{2,1,0:T(8,128)(2,1)S(1)}, bf16[4,128,1024]{2,1,0:T(8,128)(2,1)S(1)}, u32[]{:S(2)}, u32[]{:S(2)}) %collective-permute-start.3) | collective-permute-done | bytes 1048608 | tf_op jit(solution)/shard_map/ppermute | solution.py:335
  57.7 21.5 %collective-permute-done.5.refs_5_.refs_9_ = bf16[4,128,1024]{2,1,0:T(8,128)(2,1)S(1)} collective-permute-done((bf16[4,128,1024]{2,1,0:T(8,128)(2,1)S(1)}, bf16[4,128,1024]{2,1,0:T(8,128)(2,1)S(1)}, u32[]{:S(2)}, u32[]{:S(2)}) %collective-permute-start.5) | collective-permute-done | bytes 1048608 | tf_op jit(solution)/shard_map/ppermute | solution.py:335
  82.8 17.6 %collective-permute-done.6.refs_2_ = bf16[4,128,768]{2,1,0:T(8,128)(2,1)} collective-permute-done((bf16[4,128,768]{2,1,0:T(8,128)(2,1)S(1)}, bf16[4,128,768]{2,1,0:T(8,128)(2,1)}, u32[]{:S(2)}, u32[]{:S(2)}) %collective-permute-start.6) | collective-permute-done | bytes 786464 | tf_op jit(solution)/shard_map/ppermute | solution.py:335
  128.0 10.9 %collective-permute-done.10.refs_6_ = bf16[4,128,768]{2,1,0:T(8,128)(2,1)S(1)} collective-permute-done((bf16[4,128,768]{2,1,0:T(8,128)(2,1)}, bf16[4,128,768]{2,1,0:T(8,128)(2,1)S(1)}, u32[]{:S(2)}, u32[]{:S(2)}) %collective-permute-start.10) | collective-permute-done | bytes 786464 | tf_op jit(solution)/shard_map/ppermute | solution.py:335
  141.2 12.5 %all-to-all-done = bf16[4,4,64,1024]{3,2,1,0:T(8,128)(2,1)} async-done(((bf16[4,4,64,1024]{3,2,1,0:T(8,128)(2,1)}), bf16[4,4,64,1024]{3,2,1,0:T(8,128)(2,1)}, u32[]{:S(2)}, u32[]{:S(2)}) %all-to-all-start) | async-done | bytes 2097184 | tf_op jit(solution)/shard_map/all_to_all | solution.py:353
  155.4 19.7 %collective-permute-done.14.refs_4_.refs_5_ = bf16[4,128,768]{2,1,0:T(8,128)(2,1)} collective-permute-done((bf16[4,128,768]{2,1,0:T(8,128)(2,1)S(1)}, bf16[4,128,768]{2,1,0:T(8,128)(2,1)}, u32[]{:S(2)}, u32[]{:S(2)}) %collective-permute-start.14) | collective-permute-done | bytes 786464 | tf_op jit(solution)/shard_map/ppermute | solution.py:335
  183.5 12.7 %collective-permute-done.16.refs_6_.refs_7_ = bf16[4,128,768]{2,1,0:T(8,128)(2,1)} collective-permute-done((bf16[4,128,768]{2,1,0:T(8,128)(2,1)}, bf16[4,128,768]{2,1,0:T(8,128)(2,1)}, u32[]{:S(2)}, u32[]{:S(2)}) %collective-permute-start.16) | collective-permute-done | bytes 786464 | tf_op jit(solution)/shard_map/ppermute | solution.py:335
  201.8 13.5 %collective-permute-done.18.refs_2_.refs_3_ = bf16[4,128,768]{2,1,0:T(8,128)(2,1)S(1)} collective-permute-done((bf16[4,128,768]{2,1,0:T(8,128)(2,1)S(1)}, bf16[4,128,768]{2,1,0:T(8,128)(2,1)S(1)}, u32[]{:S(2)}, u32[]{:S(2)}) %collective-permute-start.18) | collective-permute-done | bytes 786464 | tf_op jit(solution)/shard_map/ppermute | solution.py:335
  216.1 17.5 %collective-permute-done.20.refs_4_.refs_5_ = bf16[4,128,768]{2,1,0:T(8,128)(2,1)} collective-permute-done((bf16[4,128,768]{2,1,0:T(8,128)(2,1)S(1)}, bf16[4,128,768]{2,1,0:T(8,128)(2,1)}, u32[]{:S(2)}, u32[]{:S(2)}) %collective-permute-start.20) | collective-permute-done | bytes 786464 | tf_op jit(solution)/shard_map/ppermute | solution.py:335
  234.1 7.3 %attend.4 = bf16[16,64,1024]{2,1,0:T(8,128)(2,1)} custom-call(bf16[16,64,768]{2,1,0:T(8,128)(2,1)} %bitcast.4.qkv_ref, bf16[16,64,1024]{2,1,0:T(8,128)(2,1)} %bitcast.3.grad_ref), custom_call_target="tpu_custom_call" | custom-call | flops 1610612736 | bytes 4194304 | tf_op jit(solution)/shard_map/attend/pallas_call | solution.py:148
  257.9 8.4 %collective-permute-done.25.refs_1_.refs_5_ = bf16[4,128,768]{2,1,0:T(8,128)(2,1)} collective-permute-done((bf16[4,128,768]{2,1,0:T(8,128)(2,1)S(1)}, bf16[4,128,768]{2,1,0:T(8,128)(2,1)}, u32[]{:S(2)}, u32[]{:S(2)}) %collective-permute-start.25) | collective-permute-done | bytes 786464 | tf_op jit(solution)/shard_map/ppermute | solution.py:335
  275.1 11.6 %collective-permute-done.26.refs_3_.refs_7_ = bf16[4,128,768]{2,1,0:T(8,128)(2,1)S(1)} collective-permute-done((bf16[4,128,768]{2,1,0:T(8,128)(2,1)}, bf16[4,128,768]{2,1,0:T(8,128)(2,1)S(1)}, u32[]{:S(2)}, u32[]{:S(2)}) %collective-permute-start.26) | collective-permute-done | bytes 786464 | tf_op jit(solution)/shard_map/ppermute | solution.py:335
  288.3 14.5 %collective-permute-done.28.refs_4_.refs_8_ = bf16[4,128,768]{2,1,0:T(8,128)(2,1)S(1)} collective-permute-done((bf16[4,128,768]{2,1,0:T(8,128)(2,1)}, bf16[4,128,768]{2,1,0:T(8,128)(2,1)S(1)}, u32[]{:S(2)}, u32[]{:S(2)}) %collective-permute-start.28) | collective-permute-done | bytes 786464 | tf_op jit(solution)/shard_map/ppermute | solution.py:335
  306.1 7.3 %attend.5 = bf16[16,64,1024]{2,1,0:T(8,128)(2,1)} custom-call(bf16[16,64,768]{2,1,0:T(8,128)(2,1)} %bitcast.6.qkv_ref, bf16[16,64,1024]{2,1,0:T(8,128)(2,1)} %bitcast.3.grad_ref), custom_call_target="tpu_custom_call" | custom-call | flops 1610612736 | bytes 4194304 | tf_op jit(solution)/shard_map/attend/pallas_call | solution.py:148
  319.9 19.3 %collective-permute-done.32.refs_6_.refs_10_ = bf16[4,128,768]{2,1,0:T(8,128)(2,1)S(1)} collective-permute-done((bf16[4,128,768]{2,1,0:T(8,128)(2,1)}, bf16[4,128,768]{2,1,0:T(8,128)(2,1)S(1)}, u32[]{:S(2)}, u32[]{:S(2)}) %collective-permute-start.32) | collective-permute-done | bytes 786464 | tf_op jit(solution)/shard_map/ppermute | solution.py:335
  350.4 21.9 %collective-permute-done.34.refs_7_.refs_11_ = bf16[4,128,768]{2,1,0:T(8,128)(2,1)S(1)} collective-permute-done((bf16[4,128,768]{2,1,0:T(8,128)(2,1)}, bf16[4,128,768]{2,1,0:T(8,128)(2,1)S(1)}, u32[]{:S(2)}, u32[]{:S(2)}) %collective-permute-start.34) | collective-permute-done | bytes 786464 | tf_op jit(solution)/shard_map/ppermute | solution.py:335
  390.5 12.8 %all-to-all-done.6 = bf16[4,4,64,768]{3,2,1,0:T(8,128)(2,1)S(1)} async-done(((bf16[4,4,64,768]{3,2,1,0:T(8,128)(2,1)}), bf16[4,4,64,768]{3,2,1,0:T(8,128)(2,1)S(1)}, u32[]{:S(2)}, u32[]{:S(2)}) %all-to-all-start.6) | async-done | bytes 1572896 | tf_op jit(solution)/shard_map/all_to_all | solution.py:353
  415.0 8.0 %backward.5.refs_0_ = f32[4,256,1024]{2,1,0:T(8,128)} custom-call(s32[1,8]{1,0:T(1,128)} %fusion.10.source_ref, bf16[4,4,64,1024]{3,2,1,0:T(8,128)(2,1)} %copy-done.2, f32[4,256,1024]{2,1,0:T(8,128)} %backward.4.refs_0_, bf16[4,128,768]{2,1,0:T(8,128)(2,1)} %copy-done.6, bf16[4,128,768]{2,1,0:T(8,128)(2,1)} %collective-permute-done.17.refs_1_.refs_2_, ...), custom_call_target="tpu_custom_call" | custom-call | flops 1610612736 | bytes 16777216 | tf_op jit(solution)/shard_map/backward/pallas_call | solution.py:214
  423.0 7.4 %attend.7 = (bf16[16,64,256]{2,1,0:T(8,128)(2,1)}, bf16[16,64,768]{2,1,0:T(8,128)(2,1)}) custom-call(bf16[16,64,768]{2,1,0:T(8,128)(2,1)} %bitcast.25, bf16[16,64,1024]{2,1,0:T(8,128)(2,1)} %bitcast.3.grad_ref), custom_call_target="tpu_custom_call" | custom-call | flops 1610612736 | bytes 4194304 | tf_op jit(solution)/shard_map/attend/pallas_call | solution.py:148
  437.2 7.9 %backward.6.refs_0_ = f32[4,256,1024]{2,1,0:T(8,128)} custom-call(s32[1,8]{1,0:T(1,128)} %fusion.10.source_ref, bf16[4,4,64,1024]{3,2,1,0:T(8,128)(2,1)} %copy-done.3, f32[4,256,1024]{2,1,0:T(8,128)} %backward.5.refs_0_, bf16[4,128,768]{2,1,0:T(8,128)(2,1)} %copy-done.5, bf16[4,128,768]{2,1,0:T(8,128)(2,1)} %collective-permute-done.27.refs_1_.refs_2_, ...), custom_call_target="tpu_custom_call" | custom-call | flops 1610612736 | bytes 16777216 | tf_op jit(solution)/shard_map/backward/pallas_call | solution.py:214
  449.8 7.7 %output.1 = bf16[4,256,1024]{2,1,0:T(8,128)(2,1)} custom-call(s32[1,8]{1,0:T(1,128)} %fusion.10.source_ref, bf16[4,256,1024]{2,1,0:T(8,128)(2,1)} %get-tuple-element.129.rows_ref.refs_1_, bf16[4,4,64,1024]{3,2,1,0:T(8,128)(2,1)} %copy-done.1, bf16[4,4,64,1024]{3,2,1,0:T(8,128)(2,1)} %copy-done.2, bf16[4,4,64,1024]{3,2,1,0:T(8,128)(2,1)} %copy-done.3, ...), custom_call_target="tpu_custom_call" | custom-call | flops 2147483648 | bytes 14680064 | tf_op jit(solution)/shard_map/output/pallas_call | solution.py:249
  462.1 7.6 %all-to-all-done.9.back_ref = bf16[4,4,64,768]{3,2,1,0:T(8,128)(2,1)S(1)} async-done(((bf16[4,4,64,768]{3,2,1,0:T(8,128)(2,1)}), bf16[4,4,64,768]{3,2,1,0:T(8,128)(2,1)S(1)}, u32[]{:S(2)}, u32[]{:S(2)}) %all-to-all-start.9) | async-done | bytes 1572896 | tf_op jit(solution)/shard_map/all_to_all | solution.py:353
  470.9 8.8 %backward.7 = bf16[4,256,1024]{2,1,0:T(8,128)(2,1)} custom-call(s32[1,8]{1,0:T(1,128)} %fusion.10.source_ref, bf16[4,4,64,768]{3,2,1,0:T(8,128)(2,1)} %copy-done.8, f32[4,256,1024]{2,1,0:T(8,128)} %backward.6.refs_0_, bf16[4,256,1024]{2,1,0:T(8,128)(2,1)} %get-tuple-element.129.rows_ref.refs_1_, bf16[4,256,1024]{2,1,0:T(8,128)(2,1)} %get-tuple-element.62.rows_ref.refs_2_, ...), custom_call_target="tpu_custom_call" | custom-call | flops 1610612736 | bytes 16777216 | tf_op jit(solution)/shard_map/backward/pallas_call | solution.py:214
  (148 shorter events, 175.0 us)
Async XLA Ops:
  0.6 26.4 %collective-permute-start.1 = (bf16[4,128,1024]{2,1,0:T(8,128)(2,1)}, bf16[4,128,1024]{2,1,0:T(8,128)(2,1)S(1)}, u32[]{:S(2)}, u32[]{:S(2)}) collective-permute-start(bf16[4,128,1024]{2,1,0:T(8,128)(2,1)} %refs_4_.1), channel_id=1, source_target_pairs={{0,1},{1,0},{2,3},{3,2},{4,5},{5,4},{6,7},{7,6},{8,9},{9,8},{10,11... | collective-permute-start | bytes 3145736 | tf_op jit(solution)/shard_map/ppermute | solution.py:335
  3.7 26.7 %collective-permute-start = (bf16[4,128,1024]{2,1,0:T(8,128)(2,1)}, bf16[4,128,1024]{2,1,0:T(8,128)(2,1)S(1)}, u32[]{:S(2)}, u32[]{:S(2)}) collective-permute-start(bf16[4,128,1024]{2,1,0:T(8,128)(2,1)} %refs_4_.1), channel_id=1, source_target_pairs={{0,2},{1,3},{2,4},{3,5},{4,6},{5,7},{6,0},{7,1},{8,10},{9,11},{10,... | collective-permute-start | bytes 3145736 | tf_op jit(solution)/shard_map/ppermute | solution.py:335
  30.4 23.8 %collective-permute-start.3 = (bf16[4,128,1024]{2,1,0:T(8,128)(2,1)S(1)}, bf16[4,128,1024]{2,1,0:T(8,128)(2,1)S(1)}, u32[]{:S(2)}, u32[]{:S(2)}) collective-permute-start(bf16[4,128,1024]{2,1,0:T(8,128)(2,1)S(1)} %collective-permute-done.refs_2_.refs_6_), channel_id=1, source_target_pairs={{0,1},{1,0},{2,3},{3,2},{4,5},{5,4},{6,7},{7,6},{8,9},{9,8},{10,11... | collective-permute-start | bytes 3145736 | tf_op jit(solution)/shard_map/ppermute | solution.py:335
  30.9 25.5 %collective-permute-start.2 = (bf16[4,128,1024]{2,1,0:T(8,128)(2,1)S(1)}, bf16[4,128,1024]{2,1,0:T(8,128)(2,1)S(1)}, u32[]{:S(2)}, u32[]{:S(2)}) collective-permute-start(bf16[4,128,1024]{2,1,0:T(8,128)(2,1)S(1)} %collective-permute-done.refs_2_.refs_6_), channel_id=1, source_target_pairs={{0,2},{1,3},{2,4},{3,5},{4,6},{5,7},{6,0},{7,1},{8,10},{9,11},{10,... | collective-permute-start | bytes 3145736 | tf_op jit(solution)/shard_map/ppermute | solution.py:335
  56.4 22.8 %collective-permute-start.5 = (bf16[4,128,1024]{2,1,0:T(8,128)(2,1)S(1)}, bf16[4,128,1024]{2,1,0:T(8,128)(2,1)S(1)}, u32[]{:S(2)}, u32[]{:S(2)}) collective-permute-start(bf16[4,128,1024]{2,1,0:T(8,128)(2,1)S(1)} %collective-permute-done.2.refs_4_.refs_8_), channel_id=1, source_target_pairs={{0,1},{1,0},{2,3},{3,2},{4,5},{5,4},{6,7},{7,6},{8,9},{9,8},{10,11... | collective-permute-start | bytes 3145736 | tf_op jit(solution)/shard_map/ppermute | solution.py:335
  57.7 24.1 %collective-permute-start.4 = (bf16[4,128,1024]{2,1,0:T(8,128)(2,1)S(1)}, bf16[4,128,1024]{2,1,0:T(8,128)(2,1)S(1)}, u32[]{:S(2)}, u32[]{:S(2)}) collective-permute-start(bf16[4,128,1024]{2,1,0:T(8,128)(2,1)S(1)} %collective-permute-done.2.refs_4_.refs_8_), channel_id=1, source_target_pairs={{0,2},{1,3},{2,4},{3,5},{4,6},{5,7},{6,0},{7,1},{8,10},{9,11},{10,... | collective-permute-start | bytes 3145736 | tf_op jit(solution)/shard_map/ppermute | solution.py:335
  81.9 23.1 %collective-permute-start.7 = (bf16[4,128,1024]{2,1,0:T(8,128)(2,1)S(1)}, bf16[4,128,1024]{2,1,0:T(8,128)(2,1)S(1)}, u32[]{:S(2)}, u32[]{:S(2)}) collective-permute-start(bf16[4,128,1024]{2,1,0:T(8,128)(2,1)S(1)} %collective-permute-done.4.refs_6_.refs_10_), channel_id=1, source_target_pairs={{0,1},{1,0},{2,3},{3,2},{4,5},{5,4},{6,7},{7,6},{8,9},{9,8},{10,11... | collective-permute-start | bytes 3145736 | tf_op jit(solution)/shard_map/ppermute | solution.py:335
  123.5 30.2 %all-to-all-start = ((bf16[4,4,64,1024]{3,2,1,0:T(8,128)(2,1)}), bf16[4,4,64,1024]{3,2,1,0:T(8,128)(2,1)}, u32[]{:S(2)}, u32[]{:S(2)}) async-start(bf16[4,4,64,1024]{3,2,1,0:T(8,128)(2,1)} %project_back.1), calls=%async_computation | async-start | bytes 4194304 | tf_op jit(solution)/shard_map/all_to_all | solution.py:353
  154.1 21.0 %collective-permute-start.14 = (bf16[4,128,768]{2,1,0:T(8,128)(2,1)S(1)}, bf16[4,128,768]{2,1,0:T(8,128)(2,1)}, u32[]{:S(2)}, u32[]{:S(2)}) collective-permute-start(bf16[4,128,768]{2,1,0:T(8,128)(2,1)S(1)} %collective-permute-done.12.refs_2_.refs_3_), channel_id=1, source_target_pairs={{0,2},{1,3},{2,4},{3,5},{4,6},{5,7},{6,0},{7,1},{8,10},{9,11},{10,... | collective-permute-start | bytes 2359304 | tf_op jit(solution)/shard_map/ppermute | solution.py:335
  154.1 21.0 %collective-permute-start.15 = (bf16[4,128,768]{2,1,0:T(8,128)(2,1)}, bf16[4,128,768]{2,1,0:T(8,128)(2,1)S(1)}, u32[]{:S(2)}, u32[]{:S(2)}) collective-permute-start(bf16[4,128,768]{2,1,0:T(8,128)(2,1)} %copy-done.23), channel_id=1, source_target_pairs={{0,1},{1,0},{2,3},{3,2},{4,5},{5,4},{6,7},{7,6},{8,9},{9,8},{10,11... | collective-permute-start | bytes 2359304 | tf_op jit(solution)/shard_map/ppermute | solution.py:335
  176.0 20.3 %collective-permute-start.16 = (bf16[4,128,768]{2,1,0:T(8,128)(2,1)}, bf16[4,128,768]{2,1,0:T(8,128)(2,1)}, u32[]{:S(2)}, u32[]{:S(2)}) collective-permute-start(bf16[4,128,768]{2,1,0:T(8,128)(2,1)} %collective-permute-done.14.refs_4_.refs_5_), channel_id=1, source_target_pairs={{0,2},{1,3},{2,4},{3,5},{4,6},{5,7},{6,0},{7,1},{8,10},{9,11},{10,... | collective-permute-start | bytes 2359304 | tf_op jit(solution)/shard_map/ppermute | solution.py:335
  176.0 20.3 %collective-permute-start.17 = (bf16[4,128,768]{2,1,0:T(8,128)(2,1)S(1)}, bf16[4,128,768]{2,1,0:T(8,128)(2,1)}, u32[]{:S(2)}, u32[]{:S(2)}) collective-permute-start(bf16[4,128,768]{2,1,0:T(8,128)(2,1)S(1)} %get-tuple-element.72.refs_0_.refs_1_), channel_id=1, source_target_pairs={{0,1},{1,0},{2,3},{3,2},{4,5},{5,4},{6,7},{7,6},{8,9},{9,8},{10,11... | collective-permute-start | bytes 2359304 | tf_op jit(solution)/shard_map/ppermute | solution.py:335
  196.3 19.1 %collective-permute-start.18 = (bf16[4,128,768]{2,1,0:T(8,128)(2,1)S(1)}, bf16[4,128,768]{2,1,0:T(8,128)(2,1)S(1)}, u32[]{:S(2)}, u32[]{:S(2)}) collective-permute-start(bf16[4,128,768]{2,1,0:T(8,128)(2,1)S(1)} %get-tuple-element.85.refs_0_.refs_1_), channel_id=1, source_target_pairs={{0,2},{1,3},{2,4},{3,5},{4,6},{5,7},{6,0},{7,1},{8,10},{9,11},{10,... | collective-permute-start | bytes 2359304 | tf_op jit(solution)/shard_map/ppermute | solution.py:335
  197.5 36.7 %all-to-all-start.1 = ((bf16[4,4,64,768]{3,2,1,0:T(8,128)(2,1)}), bf16[4,4,64,768]{3,2,1,0:T(8,128)(2,1)}, u32[]{:S(2)}, u32[]{:S(2)}) async-start(bf16[4,4,64,768]{3,2,1,0:T(8,128)(2,1)} %project.4), calls=%async_computation.1 | async-start | bytes 3145728 | tf_op jit(solution)/shard_map/all_to_all | solution.py:353
  241.5 29.3 %all-to-all-start.2 = ((bf16[4,4,64,1024]{3,2,1,0:T(8,128)(2,1)}), bf16[4,4,64,1024]{3,2,1,0:T(8,128)(2,1)S(1)}, u32[]{:S(2)}, u32[]{:S(2)}) async-start(bf16[4,4,64,1024]{3,2,1,0:T(8,128)(2,1)} %bitcast.21), calls=%async_computation.2 | async-start | bytes 4194304 | tf_op jit(solution)/shard_map/all_to_all | solution.py:353
  270.7 35.3 %all-to-all-start.3 = ((bf16[4,4,64,768]{3,2,1,0:T(8,128)(2,1)}), bf16[4,4,64,768]{3,2,1,0:T(8,128)(2,1)}, u32[]{:S(2)}, u32[]{:S(2)}) async-start(bf16[4,4,64,768]{3,2,1,0:T(8,128)(2,1)} %project.5), calls=%async_computation.3 | async-start | bytes 3145728 | tf_op jit(solution)/shard_map/all_to_all | solution.py:353
  313.4 32.5 %all-to-all-start.4 = ((bf16[4,4,64,1024]{3,2,1,0:T(8,128)(2,1)}), bf16[4,4,64,1024]{3,2,1,0:T(8,128)(2,1)S(1)}, u32[]{:S(2)}, u32[]{:S(2)}) async-start(bf16[4,4,64,1024]{3,2,1,0:T(8,128)(2,1)} %bitcast.23), calls=%async_computation.4 | async-start | bytes 4194304 | tf_op jit(solution)/shard_map/all_to_all | solution.py:353
  319.0 20.2 %collective-permute-start.32 = (bf16[4,128,768]{2,1,0:T(8,128)(2,1)}, bf16[4,128,768]{2,1,0:T(8,128)(2,1)S(1)}, u32[]{:S(2)}, u32[]{:S(2)}) collective-permute-start(bf16[4,128,768]{2,1,0:T(8,128)(2,1)} %copy-done.19), channel_id=1, source_target_pairs={{0,2},{1,3},{2,4},{3,5},{4,6},{5,7},{6,0},{7,1},{8,10},{9,11},{10,... | collective-permute-start | bytes 2359304 | tf_op jit(solution)/shard_map/ppermute | solution.py:335
  319.3 19.9 %collective-permute-start.33 = (bf16[4,128,768]{2,1,0:T(8,128)(2,1)}, bf16[4,128,768]{2,1,0:T(8,128)(2,1)}, u32[]{:S(2)}, u32[]{:S(2)}) collective-permute-start(bf16[4,128,768]{2,1,0:T(8,128)(2,1)} %collective-permute-done.22.refs_6_.refs_7_), channel_id=1, source_target_pairs={{0,1},{1,0},{2,3},{3,2},{4,5},{5,4},{6,7},{7,6},{8,9},{9,8},{10,11... | collective-permute-start | bytes 2359304 | tf_op jit(solution)/shard_map/ppermute | solution.py:335
  346.0 33.7 %all-to-all-start.5 = ((bf16[4,4,64,768]{3,2,1,0:T(8,128)(2,1)}), bf16[4,4,64,768]{3,2,1,0:T(8,128)(2,1)}, u32[]{:S(2)}, u32[]{:S(2)}) async-start(bf16[4,4,64,768]{3,2,1,0:T(8,128)(2,1)} %project.6), calls=%async_computation.5 | async-start | bytes 3145728 | tf_op jit(solution)/shard_map/all_to_all | solution.py:353
  350.3 21.9 %collective-permute-start.34 = (bf16[4,128,768]{2,1,0:T(8,128)(2,1)}, bf16[4,128,768]{2,1,0:T(8,128)(2,1)S(1)}, u32[]{:S(2)}, u32[]{:S(2)}) collective-permute-start(bf16[4,128,768]{2,1,0:T(8,128)(2,1)} %collective-permute-done.30.refs_5_.refs_9_), channel_id=1, source_target_pairs={{0,2},{1,3},{2,4},{3,5},{4,6},{5,7},{6,0},{7,1},{8,10},{9,11},{10,... | collective-permute-start | bytes 2359304 | tf_op jit(solution)/shard_map/ppermute | solution.py:335
  379.7 23.6 %all-to-all-start.6 = ((bf16[4,4,64,768]{3,2,1,0:T(8,128)(2,1)}), bf16[4,4,64,768]{3,2,1,0:T(8,128)(2,1)S(1)}, u32[]{:S(2)}, u32[]{:S(2)}) async-start(bf16[4,4,64,768]{3,2,1,0:T(8,128)(2,1)} %project.7), calls=%async_computation.6 | async-start | bytes 3145728 | tf_op jit(solution)/shard_map/all_to_all | solution.py:353
  404.4 29.3 %all-to-all-start.7 = ((bf16[4,4,64,1024]{3,2,1,0:T(8,128)(2,1)}), bf16[4,4,64,1024]{3,2,1,0:T(8,128)(2,1)S(1)}, u32[]{:S(2)}, u32[]{:S(2)}) async-start(bf16[4,4,64,1024]{3,2,1,0:T(8,128)(2,1)} %bitcast.22), calls=%async_computation.7 | async-start | bytes 4194304 | tf_op jit(solution)/shard_map/all_to_all | solution.py:353
  446.0 23.6 %all-to-all-start.9 = ((bf16[4,4,64,768]{3,2,1,0:T(8,128)(2,1)}), bf16[4,4,64,768]{3,2,1,0:T(8,128)(2,1)S(1)}, u32[]{:S(2)}, u32[]{:S(2)}) async-start(bf16[4,4,64,768]{3,2,1,0:T(8,128)(2,1)} %bitcast.24), calls=%async_computation.9 | async-start | bytes 3145728 | tf_op jit(solution)/shard_map/all_to_all | solution.py:353
  (50 other events, 1541.3 us)
